TPU v7x, 32 devices: a whole 2x2x4 slice. The times are simulated.
32 devices in a mesh: grp: 4 (over z), dev: 8 (over y, x, core).
Axes of the slice: x: 2, y: 2, z: 4, core: 2. Of those that a mesh axis runs over, the one named last changes fastest.
Arguments:
- feats: bfloat16 [96, 3200], P(('grp', 'dev')), may hold values from -6 to 6
- ln_gain: float32 [3200], replicated, may hold values from 0.1 to 1.9
- ln_shift: float32 [3200], replicated, may hold values from -3 to 3
- w_proj: bfloat16 [3200, 8192], P(None, 'dev'), may hold values from -0.109375 to 0.109375
- b_proj: float32 [8192], P('dev'), may hold values from -3 to 3
- cotangent: bfloat16 [96, 8192], P('grp', 'dev'), may hold values from -6 to 6
- img_seq: int32 [32], replicated, may hold values from 0 to 3, as said below
- img_count: int32 [32], replicated, may hold values from 1 to 5, as said below
- img_offset: int32 [32], replicated, may hold values from 0 to 23, as said below
Outputs:
- projected: bfloat16 [96, 8192], P('grp', 'dev')
- grad_feats: bfloat16 [96, 3200], P(('grp', 'dev'))
- grad_weight: float32 [3200, 8192], P(None, 'dev')
- grad_bias: float32 [8192], P('dev')
Inputs may be any that keep to these rules, and one draw needn't show every extreme that they name: Image i is sent to sequence img_seq[i], which fills rows img_seq[i] * 24 to img_seq[i] * 24 + 23 of projected. Of the 24 encoder rows of each group, exactly 6 go to each sequence. `img_count`: the counts add up to 96; no image spans the rows of two groups. `img_offset`: the images of one sequence cover its 24 rows exactly once.
All inputs are finite; a program needn't handle non-finite values.
Results may differ from a plain program's by a relative error of at most 0.0075.
Values may be sent and summed in bfloat16 or wider, within the bound.
No kernel may reach another device: no remote copies, remote signals or barrier semaphores. Data moves between devices by JAX's collectives and lax.ppermute only.
A program may use at most 128 MiB of HBM per device.

v0:
```python
import jax
import jax.numpy as jnp
from jax import lax
from jax.sharding import PartitionSpec as P

epsilon = 1e-05


def activate(values):
    return jax.nn.gelu(values, approximate=True)


def row_targets(img_seq, img_count, img_offset, all_rows, seq_rows):
    img_ends = jnp.cumsum(img_count)
    img_starts = img_ends - img_count
    row_ids = jnp.arange(all_rows, dtype=jnp.int32)
    member = (
        (row_ids[:, None] >= img_starts[None, :]) & (row_ids[:, None] < img_ends[None, :])
    ).astype(jnp.int32)
    base_rows = img_seq * seq_rows + img_offset - img_starts
    return jnp.sum(member * base_rows[None, :], axis=1) + row_ids


def normalize(rows, ln_gain, ln_shift):
    values = rows.astype(jnp.float32)
    row_mean = jnp.mean(values, axis=1, keepdims=True)
    centered = values - row_mean
    inv_scale = lax.rsqrt(jnp.mean(centered * centered, axis=1, keepdims=True) + epsilon)
    unit_rows = centered * inv_scale
    return (unit_rows, inv_scale, unit_rows * ln_gain + ln_shift)


def local(feats, ln_gain, ln_shift, w_proj, b_proj, cotangent, img_seq, img_count, img_offset):
    lane_count = lax.axis_size("dev")
    groups = lax.axis_size("grp")
    my_group = lax.axis_index("grp")
    own_rows = feats.shape[0]
    group_rows = own_rows * lane_count
    all_rows = group_rows * groups
    row_base = my_group * group_rows
    target = row_targets(img_seq, img_count, img_offset, all_rows, group_rows)
    source_rows = (
        jnp.zeros((all_rows,), jnp.int32).at[target].set(jnp.arange(all_rows, dtype=jnp.int32))
    )
    arrivals = lax.dynamic_slice_in_dim(source_rows, row_base, group_rows)
    whole = lax.all_gather(feats, "dev", axis=0, tiled=True)
    unit_rows, inv_scale, normed = normalize(whole, ln_gain, ln_shift)
    normed = normed.astype(jnp.bfloat16)
    pre_act = jnp.dot(normed, w_proj, preferred_element_type=jnp.float32) + b_proj
    acted, gelu_pull = jax.vjp(activate, pre_act)
    local_cols = acted.astype(jnp.bfloat16)
    all_cols = lax.all_gather(local_cols, "grp", axis=0, tiled=True)
    projected = all_cols[arrivals]
    all_grads = lax.all_gather(cotangent, "grp", axis=0, tiled=True)
    own_targets = lax.dynamic_slice_in_dim(target, row_base, group_rows)
    upstream = all_grads[own_targets]
    grad_pre = gelu_pull(upstream.astype(jnp.float32))[0].astype(jnp.bfloat16)
    weight_term = lax.dot_general(
        normed, grad_pre, (((0,), (0,)), ((), ())), preferred_element_type=jnp.float32
    )
    bias_term = jnp.sum(grad_pre.astype(jnp.float32), axis=0)
    vis_width = weight_term.shape[0]
    padded_rows = (vis_width + groups) // groups * groups
    joint_term = jnp.concatenate(
        [
            weight_term,
            bias_term[None, :],
            jnp.zeros((padded_rows - vis_width - 1, weight_term.shape[1]), jnp.float32),
        ],
        axis=0,
    )
    summed_share = lax.psum_scatter(joint_term, "grp", scatter_dimension=0, tiled=True)
    summed_whole = lax.all_gather(
        summed_share.astype(jnp.bfloat16), "grp", axis=0, tiled=True
    ).astype(summed_share.dtype)
    grad_weight = summed_whole[:vis_width]
    grad_bias = summed_whole[vis_width]
    grad_normed = lax.psum_scatter(
        lax.dot_general(
            grad_pre, w_proj, (((1,), (1,)), ((), ())), preferred_element_type=jnp.float32
        ),
        "dev",
        scatter_dimension=0,
        tiled=True,
    )
    lane_start = lax.axis_index("dev") * own_rows
    own_unit = lax.dynamic_slice_in_dim(unit_rows, lane_start, own_rows, 0)
    own_scale = lax.dynamic_slice_in_dim(inv_scale, lane_start, own_rows, 0)
    scaled_grad = grad_normed * ln_gain
    grad_feats = own_scale * (
        scaled_grad
        - jnp.mean(scaled_grad, axis=1, keepdims=True)
        - own_unit * jnp.mean(scaled_grad * own_unit, axis=1, keepdims=True)
    )
    return (projected, grad_feats.astype(jnp.bfloat16), grad_weight, grad_bias)


def solution(mesh):
    placed = (
        P(("grp", "dev"), None),
        P(),
        P(),
        P(None, "dev"),
        P("dev"),
        P("grp", "dev"),
        P(),
        P(),
        P(),
    )
    return jax.shard_map(
        local,
        mesh=mesh,
        in_specs=placed,
        out_specs=(P("grp", "dev"), P(("grp", "dev"), None), P(None, "dev"), P("dev")),
        check_vma=False,
    )
```

profile of v0, /device:TPU:0, one launch (start us, length us, event | category | flops | bytes accessed | tf_op | source)
XLA Modules:
  0.0 467.6 jit_solution(9751224176952283435)
XLA Ops:
  8.1 10.9 %all-gather = bf16[8,3,3200]{2,1,0:T(4,128)(2,1)S(1)} all-gather(bf16[1,3,3200]{2,1,0:T(4,128)(2,1)} %bitcast.21), channel_id=1, replica_groups=mesh['grp'=4,'dev'=8] {'dev'}, dimensions={0}, use_global_device_ids=true | all-gather | bytes 172800 | tf_op jit(solution)/shard_map/all_gather | solution.py:46
  19.3 0.7 copy.16
  20.2 0.7 add_subtract_fusion
  21.1 14.1 %all_gather.14 = bf16[96,1024]{1,0:T(8,128)(2,1)S(1)} all-gather(bf16[24,1024]{1,0:T(8,128)(2,1)} %param.14), channel_id=1, replica_groups=mesh['grp'=4,'dev'=8] {'grp'}, dimensions={0}, use_global_device_ids=true | all-gather | bytes 245760 | tf_op jit(solution)/shard_map/all_gather | solution.py:54
  35.6 0.6 gather_fusion.1
  36.2 3.9 convert_reduce_fusion.1
  40.2 6.9 %fusion.13 = f32[3200,1024]{1,0:T(8,128)} fusion(bf16[24,1024]{1,0:T(8,128)(2,1)S(1)} %get-tuple-element.7, f32[24,3200]{1,0:T(8,128)S(1)} %subtract_multiply_fusion, f32[3200]{0:T(1024)S(1)} %copy-done.2, f32[3200]{0:T(1024)S(1)} %copy-done.1), kind=kOutput, calls=%fused_computation.30 | convolution fusion | flops 157516800 | bytes 13489152 | tf_op jit(solution)/shard_map/dot_general | solution.py:58
  47.1 29.9 %concatenate.3 = f32[3204,1024]{1,0:T(8,128)} concatenate(f32[3200,1024]{1,0:T(8,128)} %fusion.13, f32[1,1024]{1,0:T(1,128)S(1)} %bitcast.22, f32[3,1024]{1,0:T(4,128)S(1)} %broadcast_in_dim.11), dimensions={0} | concatenate | bytes 26247168 | tf_op jit(solution)/shard_map/concatenate | solution.py:64
  77.0 221.7 %fusion = f32[808,1024]{1,0:T(8,128)S(1)} fusion(f32[3204,1024]{1,0:T(8,128)} %concatenate.3), kind=kCustom, calls=%all-reduce-scatter | all-reduce-scatter fusion | flops 3309569 | bytes 16433664
  298.8 2.1 collective-permute-start
  300.9 5.4 %fusion.19 = f32[24,3200]{1,0:T(8,128)} fusion(bf16[24,1024]{1,0:T(8,128)(2,1)S(1)} %get-tuple-element.7, bf16[3200,1024]{1,0:T(8,128)(2,1)} %param.12), kind=kOutput, calls=%fused_computation.50 | convolution fusion | flops 157286400 | bytes 6909952 | tf_op jit(solution)/shard_map/dot_general | solution.py:79
  306.5 0.6 dynamic-slice.10
  307.7 7.8 %concatenate.4 = bf16[829,1024]{1,0:T(8,128)(2,1)} concatenate(bf16[21,1024]{1,0:T(8,128)(2,1)S(1)} %collective-permute-done, f32[808,1024]{1,0:T(8,128)S(1)} %fusion), dimensions={0} | concatenate | bytes 5050368
  315.5 3.1 fusion.1
  320.0 0.9 scatter_custom_fusion
  320.8 18.5 %all_gather.13 = bf16[96,1024]{1,0:T(8,128)(2,1)S(1)} all-gather(bf16[24,1024]{1,0:T(8,128)(2,1)S(1)} %get-tuple-element.10), channel_id=1, replica_groups=mesh['grp'=4,'dev'=8] {'grp'}, dimensions={0}, use_global_device_ids=true | all-gather | bytes 245760 | tf_op jit(solution)/shard_map/all_gather | solution.py:52
  339.4 1.2 gather_fusion
  340.7 16.3 %all-reduce.5.cloned.1.call-done = f32[24,3200]{1,0:T(8,128)} async-done(((f32[24,3200]{1,0:T(8,128)}), f32[24,3200]{1,0:T(8,128)}) %all-reduce.5.cloned.1.call-update) | async-done | bytes 307216
  357.0 1.2 fusion.12
  358.2 1.7 multiply_convert_fusion.1
  360.0 77.2 %all-gather.4.cloned.1.call-done = bf16[4,801,1024]{2,1,0:T(8,128)(2,1)} async-done(((bf16[1,801,1024]{2,1,0:T(8,128)(2,1)}), bf16[4,801,1024]{2,1,0:T(8,128)(2,1)}) %all-gather.4.cloned.1.call-update) | async-done | bytes 6561808 | tf_op jit(solution)/shard_map/all_gather | solution.py:73
  437.2 9.0 %reshape.124 = f32[3204,1024]{1,0:T(8,128)} reshape(bf16[4,801,1024]{2,1,0:T(8,128)(2,1)} %all-gather.4.cloned.1.call-done) | data formatting | bytes 19685376 | tf_op jit(solution)/shard_map/convert_element_type | solution.py:75
  446.2 1.4 slice.13
  447.6 12.5 %slice.12 = f32[3200,1024]{1,0:T(8,128)} slice(f32[3204,1024]{1,0:T(8,128)} %reshape.124), slice={[0:3200], [0:1024]} | slice | bytes 26214400 | tf_op jit(solution)/shard_map/slice | solution.py:76
  (37 shorter events, 2.0 us)
Async XLA Ops:
  8.0 32.2 %copy-start.1 = (f32[3200]{0:T(1024)S(1)}, f32[3200]{0:T(1024)}, u32[]{:S(2)}) copy-start(f32[3200]{0:T(1024)} %param.10) | copy-start | bytes 38404
  8.0 32.2 %copy-start.2 = (f32[3200]{0:T(1024)S(1)}, f32[3200]{0:T(1024)}, u32[]{:S(2)}) copy-start(f32[3200]{0:T(1024)} %param.11) | copy-start | bytes 38404
  8.0 349.0 %all-reduce.5.cloned.1.call-start = ((), (), s32[]{:S(2)}) async-start(), calls=%async_computation.1 | async-start | bytes 614400
  35.6 11.5 %copy-start = (f32[24,3200]{1,0:T(8,128)}, f32[24,3200]{1,0:T(8,128)S(1)}, u32[]{:S(2)}) copy-start(f32[24,3200]{1,0:T(8,128)S(1)} %subtract_multiply_fusion) | copy-start | bytes 921604
  298.8 7.7 %copy-start.3 = (u32[32]{0:T(128)S(1)}, u32[32]{0:T(128)}, u32[]{:S(2)}) copy-start(u32[32]{0:T(128)} %constant.56) | copy-start | bytes 388
  298.8 8.9 %collective-permute-start = (bf16[21,1024]{1,0:T(8,128)(2,1)S(1)}, bf16[21,1024]{1,0:T(8,128)(2,1)S(1)}, u32[]{:S(2)}, u32[]{:S(2)}) collective-permute-start(bf16[21,1024]{1,0:T(8,128)(2,1)S(1)} %slice.14), channel_id=1, source_target_pairs={{0,8},{8,16},{16,24},{1,9},{9,17},{17,25},{2,10},{10,18},{18,26},{... | collective-permute-start | bytes 129032
  306.4 12.3 %copy-start.4 = (u32[32]{0:T(128)S(1)}, u32[32]{0:T(128)}, u32[]{:S(2)}) copy-start(u32[32]{0:T(128)} %constant.52) | copy-start | bytes 388
  306.4 130.8 %all-gather.4.cloned.1.call-start = ((), (), s32[]{:S(2)}) async-start(), calls=%async_computation | async-start | bytes 8273920 | tf_op jit(solution)/shard_map/all_gather | solution.py:73
Sparse Core Ops, SparseCore 0:
  306.5 50.4 all-reduce.4
Sparse Core Ops, SparseCore 1:
  318.7 118.4 all-gather.3
where the time goes:
time: 469 us; the launch traced here: 468 us
  blocking collectives  265 us (57%)
  waiting for transfers between devices  93.6 us (20%)
  local copies, waits for them, and re-layouts  68.7 us (15%)
  between operations  17 us (4%)
  matrix products  16.2 us (3%)
    unnamed x1, blocking collectives  222 us
    all_gather x1, waiting for transfers between devices, local(): lax.all_gather(summed_share.astype(jnp.bfloat16), 'grp', axis=0, tiled=True)  77.2 us
    concatenate x1, local copies, waits for them, and re-layouts, local(): jnp.concatenate([weight_term, bias_term[None, :], jnp.zeros((padded_rows...  29.9 us
    all_gather x1, blocking collectives, local(): all_cols = lax.all_gather(local_cols, 'grp', axis=0, tiled=True)  18.5 us
    unnamed x4, waiting for transfers between devices  16.4 us
    all_gather x1, blocking collectives, local(): all_grads = lax.all_gather(cotangent, 'grp', axis=0, tiled=True)  14.1 us
    slice x1, local copies, waits for them, and re-layouts, local(): grad_weight = summed_whole[:vis_width]  12.5 us
    unnamed x15, local copies, waits for them, and re-layouts  12.1 us
  transfers between devices with their start and end apart: 3, of which 2 were waited for; matrix products, arithmetic and copies ran while one was open for 5% of the time, Pallas kernels for 0%

commit v1 on v0

--- a/solution.py
+++ b/solution.py
@@ -11,8 +11,11 @@
 
 
 def row_targets(img_seq, img_count, img_offset, all_rows, seq_rows):
-    img_ends = jnp.cumsum(img_count)
-    img_starts = img_ends - img_count
+    image_ids = jnp.arange(img_count.shape[0], dtype=jnp.int32)
+    img_starts = jnp.sum(
+        jnp.where(image_ids[None, :] < image_ids[:, None], img_count[None, :], 0), axis=1
+    )
+    img_ends = img_starts + img_count
     row_ids = jnp.arange(all_rows, dtype=jnp.int32)
     member = (
         (row_ids[:, None] >= img_starts[None, :]) & (row_ids[:, None] < img_ends[None, :])

time: 469 us -> 469 us (level)
  no operation moved by 1% of the time
where the time goes in v1:
time: 469 us; the launch traced here: 467 us
  blocking collectives  265 us (57%)
  waiting for transfers between devices  93.6 us (20%)
  local copies, waits for them, and re-layouts  68 us (14%)
  between operations  16.9 us (4%)
  matrix products  16.2 us (3%)
  other arithmetic  5.21 us (1%)
    unnamed x1, blocking collectives  222 us
    all_gather x1, waiting for transfers between devices, local(): lax.all_gather(summed_share.astype(jnp.bfloat16), 'grp', axis=0, tiled=True)  77.2 us
    concatenate x1, local copies, waits for them, and re-layouts, local(): jnp.concatenate([weight_term, bias_term[None, :], jnp.zeros((padded_rows...  29.9 us
    all_gather x1, blocking collectives, local(): all_cols = lax.all_gather(local_cols, 'grp', axis=0, tiled=True)  18.5 us
    unnamed x4, waiting for transfers between devices  16.3 us
    all_gather x1, blocking collectives, local(): all_grads = lax.all_gather(cotangent, 'grp', axis=0, tiled=True)  14.1 us
    slice x1, local copies, waits for them, and re-layouts, local(): grad_weight = summed_whole[:vis_width]  12.5 us
    unnamed x15, local copies, waits for them, and re-layouts  12.1 us
  transfers between devices with their start and end apart: 3, of which 2 were waited for; matrix products, arithmetic and copies ran while one was open for 5% of the time, Pallas kernels for 0%

profile of v1, /device:TPU:0, one launch (start us, length us, event | category | flops | bytes accessed | tf_op | source)
XLA Modules:
  0.0 467.4 jit_solution(4576419194885540608)
XLA Ops:
  8.1 10.9 %all-gather = bf16[8,3,3200]{2,1,0:T(4,128)(2,1)S(1)} all-gather(bf16[1,3,3200]{2,1,0:T(4,128)(2,1)} %bitcast.20), channel_id=1, replica_groups=mesh['grp'=4,'dev'=8] {'dev'}, dimensions={0}, use_global_device_ids=true | all-gather | bytes 172800 | tf_op jit(solution)/shard_map/all_gather | solution.py:49
  19.3 0.8 select_reduce_fusion.1
  20.1 0.7 fusion.19
  20.9 14.1 %all_gather.14 = bf16[96,1024]{1,0:T(8,128)(2,1)S(1)} all-gather(bf16[24,1024]{1,0:T(8,128)(2,1)} %param.14), channel_id=1, replica_groups=mesh['grp'=4,'dev'=8] {'grp'}, dimensions={0}, use_global_device_ids=true | all-gather | bytes 245760 | tf_op jit(solution)/shard_map/all_gather | solution.py:57
  35.5 0.6 gather_fusion.1
  36.1 3.9 convert_reduce_fusion.1
  40.1 6.9 %fusion.13 = f32[3200,1024]{1,0:T(8,128)} fusion(bf16[24,1024]{1,0:T(8,128)(2,1)S(1)} %get-tuple-element.7, f32[24,3200]{1,0:T(8,128)S(1)} %subtract_multiply_fusion, f32[3200]{0:T(1024)S(1)} %copy-done.2, f32[3200]{0:T(1024)S(1)} %copy-done.1), kind=kOutput, calls=%fused_computation.30 | convolution fusion | flops 157516800 | bytes 13489152 | tf_op jit(solution)/shard_map/dot_general | solution.py:61
  46.9 29.9 %concatenate.3 = f32[3204,1024]{1,0:T(8,128)} concatenate(f32[3200,1024]{1,0:T(8,128)} %fusion.13, f32[1,1024]{1,0:T(1,128)S(1)} %bitcast.21, f32[3,1024]{1,0:T(4,128)S(1)} %broadcast_in_dim.25), dimensions={0} | concatenate | bytes 26247168 | tf_op jit(solution)/shard_map/concatenate | solution.py:67
  76.9 221.7 %fusion = f32[808,1024]{1,0:T(8,128)S(1)} fusion(f32[3204,1024]{1,0:T(8,128)} %concatenate.3), kind=kCustom, calls=%all-reduce-scatter | all-reduce-scatter fusion | flops 3309569 | bytes 16433664
  298.7 2.1 collective-permute-start
  300.8 5.4 %fusion.20 = f32[24,3200]{1,0:T(8,128)} fusion(bf16[24,1024]{1,0:T(8,128)(2,1)S(1)} %get-tuple-element.7, bf16[3200,1024]{1,0:T(8,128)(2,1)} %param.12), kind=kOutput, calls=%fused_computation.53 | convolution fusion | flops 157286400 | bytes 6909952 | tf_op jit(solution)/shard_map/dot_general | solution.py:82
  306.3 0.6 dynamic-slice.10
  307.6 7.8 %concatenate.4 = bf16[829,1024]{1,0:T(8,128)(2,1)} concatenate(bf16[21,1024]{1,0:T(8,128)(2,1)S(1)} %collective-permute-done, f32[808,1024]{1,0:T(8,128)S(1)} %fusion), dimensions={0} | concatenate | bytes 5050368
  315.4 3.1 fusion.1
  319.8 0.9 scatter_custom_fusion
  320.7 18.5 %all_gather.13 = bf16[96,1024]{1,0:T(8,128)(2,1)S(1)} all-gather(bf16[24,1024]{1,0:T(8,128)(2,1)S(1)} %get-tuple-element.8), channel_id=1, replica_groups=mesh['grp'=4,'dev'=8] {'grp'}, dimensions={0}, use_global_device_ids=true | all-gather | bytes 245760 | tf_op jit(solution)/shard_map/all_gather | solution.py:55
  339.3 1.2 gather_fusion
  340.5 16.3 %all-reduce.5.cloned.1.call-done = f32[24,3200]{1,0:T(8,128)} async-done(((f32[24,3200]{1,0:T(8,128)}), f32[24,3200]{1,0:T(8,128)}) %all-reduce.5.cloned.1.call-update) | async-done | bytes 307216
  356.8 1.2 fusion.12
  358.0 1.7 multiply_convert_fusion.1
  359.8 77.2 %all-gather.4.cloned.1.call-done = bf16[4,801,1024]{2,1,0:T(8,128)(2,1)} async-done(((bf16[1,801,1024]{2,1,0:T(8,128)(2,1)}), bf16[4,801,1024]{2,1,0:T(8,128)(2,1)}) %all-gather.4.cloned.1.call-update) | async-done | bytes 6561808 | tf_op jit(solution)/shard_map/all_gather | solution.py:76
  437.0 9.0 %reshape.101 = f32[3204,1024]{1,0:T(8,128)} reshape(bf16[4,801,1024]{2,1,0:T(8,128)(2,1)} %all-gather.4.cloned.1.call-done) | data formatting | bytes 19685376 | tf_op jit(solution)/shard_map/convert_element_type | solution.py:78
  446.1 1.4 slice.13
  447.4 12.5 %slice.12 = f32[3200,1024]{1,0:T(8,128)} slice(f32[3204,1024]{1,0:T(8,128)} %reshape.101), slice={[0:3200], [0:1024]} | slice | bytes 26214400 | tf_op jit(solution)/shard_map/slice | solution.py:79
  (35 shorter events, 1.8 us)
Async XLA Ops:
  8.0 32.0 %copy-start.1 = (f32[3200]{0:T(1024)S(1)}, f32[3200]{0:T(1024)}, u32[]{:S(2)}) copy-start(f32[3200]{0:T(1024)} %param.10) | copy-start | bytes 38404
  8.0 32.0 %copy-start.2 = (f32[3200]{0:T(1024)S(1)}, f32[3200]{0:T(1024)}, u32[]{:S(2)}) copy-start(f32[3200]{0:T(1024)} %param.11) | copy-start | bytes 38404
  8.0 348.8 %all-reduce.5.cloned.1.call-start = ((), (), s32[]{:S(2)}) async-start(), calls=%async_computation.1 | async-start | bytes 614400
  35.5 11.5 %copy-start = (f32[24,3200]{1,0:T(8,128)}, f32[24,3200]{1,0:T(8,128)S(1)}, u32[]{:S(2)}) copy-start(f32[24,3200]{1,0:T(8,128)S(1)} %subtract_multiply_fusion) | copy-start | bytes 921604
  298.6 7.7 %copy-start.3 = (u32[32]{0:T(128)S(1)}, u32[32]{0:T(128)}, u32[]{:S(2)}) copy-start(u32[32]{0:T(128)} %constant.53) | copy-start | bytes 388
  298.7 8.9 %collective-permute-start = (bf16[21,1024]{1,0:T(8,128)(2,1)S(1)}, bf16[21,1024]{1,0:T(8,128)(2,1)S(1)}, u32[]{:S(2)}, u32[]{:S(2)}) collective-permute-start(bf16[21,1024]{1,0:T(8,128)(2,1)S(1)} %slice.14), channel_id=1, source_target_pairs={{0,8},{8,16},{16,24},{1,9},{9,17},{17,25},{2,10},{10,18},{18,26},{... | collective-permute-start | bytes 129032
  306.2 12.3 %copy-start.4 = (u32[32]{0:T(128)S(1)}, u32[32]{0:T(128)}, u32[]{:S(2)}) copy-start(u32[32]{0:T(128)} %constant.49) | copy-start | bytes 388
  306.2 130.8 %all-gather.4.cloned.1.call-start = ((), (), s32[]{:S(2)}) async-start(), calls=%async_computation | async-start | bytes 8273920 | tf_op jit(solution)/shard_map/all_gather | solution.py:76
Sparse Core Ops, SparseCore 0:
  306.4 50.4 all-reduce.4
Sparse Core Ops, SparseCore 1:
  318.6 118.4 all-gather.3

commit v2 on v1

--- a/solution.py
+++ b/solution.py
@@ -4,10 +4,8 @@
 from jax.sharding import PartitionSpec as P
 
 epsilon = 1e-05
-
-
-def activate(values):
-    return jax.nn.gelu(values, approximate=True)
+root_two_over_pi = 0.7978845608028654
+cubic = 0.044715
 
 
 def row_targets(img_seq, img_count, img_offset, all_rows, seq_rows):
@@ -33,7 +31,91 @@
     return (unit_rows, inv_scale, unit_rows * ln_gain + ln_shift)
 
 
-def local(feats, ln_gain, ln_shift, w_proj, b_proj, cotangent, img_seq, img_count, img_offset):
+def gelu_and_slope(values):
+    square = values * values
+    bent = jnp.tanh(root_two_over_pi * values * (1.0 + cubic * square))
+    half = 0.5 * (1.0 + bent)
+    slope = half + 0.5 * values * (1.0 - bent * bent) * (
+        root_two_over_pi * (1.0 + 3.0 * cubic * square)
+    )
+    return values * half, slope
+
+
+def gather_groups(block):
+    groups = lax.axis_size("grp")
+    if groups & (groups - 1):
+        return lax.all_gather(block, "grp", axis=0), jnp.arange(groups, dtype=jnp.int32)
+    held = block[None]
+    step = 1
+    while step < groups:
+        pairs = [(group, group ^ step) for group in range(groups)]
+        held = jnp.concatenate([held, lax.ppermute(held, "grp", pairs)], axis=0)
+        step *= 2
+    return held, lax.axis_index("grp") ^ jnp.arange(groups, dtype=jnp.int32)
+
+
+def backward_norm(grad_normed, ln_gain, unit_rows, inv_scale):
+    scaled_grad = grad_normed * ln_gain
+    grad_feats = inv_scale * (
+        scaled_grad
+        - jnp.mean(scaled_grad, axis=1, keepdims=True)
+        - unit_rows * jnp.mean(scaled_grad * unit_rows, axis=1, keepdims=True)
+    )
+    return grad_feats.astype(jnp.bfloat16)
+
+
+def gathered_plan(feats, ln_gain, ln_shift, w_proj, b_proj, cotangent, img_seq, img_count, img_offset):
+    lanes = lax.axis_size("dev")
+    groups = lax.axis_size("grp")
+    my_group = lax.axis_index("grp")
+    own_rows, vis_width = feats.shape
+    group_rows = own_rows * lanes
+    all_rows = group_rows * groups
+    unit_rows, inv_scale, normed = normalize(feats, ln_gain, ln_shift)
+    column, group_of = gather_groups(normed.astype(jnp.bfloat16))
+    grads, _ = gather_groups(cotangent)
+    rows = lax.all_gather(column, "dev", axis=0).reshape(all_rows, vis_width)
+    within = jnp.arange(lanes, dtype=jnp.int32)[:, None] * own_rows + jnp.arange(own_rows, dtype=jnp.int32)
+    slot_rows = (group_of[None, :, None] * group_rows + within[:, None, :]).reshape(all_rows)
+    seq_rows = (
+        group_of[:, None] * group_rows + jnp.arange(group_rows, dtype=jnp.int32)[None, :]
+    ).reshape(all_rows)
+    target = row_targets(img_seq, img_count, img_offset, all_rows, group_rows)
+    slot_target = target[slot_rows]
+    pre_act = jnp.dot(rows, w_proj, preferred_element_type=jnp.float32) + b_proj
+    acted, slope = gelu_and_slope(pre_act)
+    arrivals = slot_target[None, :] == (
+        my_group * group_rows + jnp.arange(group_rows, dtype=jnp.int32)
+    )[:, None]
+    projected = jnp.dot(
+        arrivals.astype(jnp.bfloat16), acted.astype(jnp.bfloat16), preferred_element_type=jnp.float32
+    ).astype(jnp.bfloat16)
+    sources = slot_target[:, None] == seq_rows[None, :]
+    upstream = jnp.dot(
+        sources.astype(jnp.bfloat16),
+        grads.reshape(all_rows, grads.shape[2]),
+        preferred_element_type=jnp.float32,
+    )
+    grad_pre = (upstream * slope).astype(jnp.bfloat16)
+    grad_weight = lax.dot_general(
+        rows, grad_pre, (((0,), (0,)), ((), ())), preferred_element_type=jnp.float32
+    )
+    grad_bias = jnp.sum(grad_pre.astype(jnp.float32), axis=0)
+    is_own = (slot_rows // group_rows)[None, :] == my_group
+    mine = (slot_rows % group_rows)[None, :] == jnp.arange(group_rows, dtype=jnp.int32)[:, None]
+    own_pre = jnp.dot(
+        (is_own & mine).astype(jnp.bfloat16), grad_pre, preferred_element_type=jnp.float32
+    ).astype(jnp.bfloat16)
+    terms = lax.dot_general(
+        own_pre, w_proj, (((1,), (1,)), ((), ())), preferred_element_type=jnp.float32
+    ).reshape(lanes, own_rows, vis_width)
+    swapped = lax.all_to_all(terms.astype(jnp.bfloat16), "dev", 0, 0)
+    grad_normed = jnp.sum(swapped.astype(jnp.float32), axis=0)
+    grad_feats = backward_norm(grad_normed, ln_gain, unit_rows, inv_scale)
+    return (projected, grad_feats, grad_weight, grad_bias)
+
+
+def summed_plan(feats, ln_gain, ln_shift, w_proj, b_proj, cotangent, img_seq, img_count, img_offset):
     lane_count = lax.axis_size("dev")
     groups = lax.axis_size("grp")
     my_group = lax.axis_index("grp")
@@ -50,14 +132,14 @@
     unit_rows, inv_scale, normed = normalize(whole, ln_gain, ln_shift)
     normed = normed.astype(jnp.bfloat16)
     pre_act = jnp.dot(normed, w_proj, preferred_element_type=jnp.float32) + b_proj
-    acted, gelu_pull = jax.vjp(activate, pre_act)
+    acted, slope = gelu_and_slope(pre_act)
     local_cols = acted.astype(jnp.bfloat16)
     all_cols = lax.all_gather(local_cols, "grp", axis=0, tiled=True)
     projected = all_cols[arrivals]
     all_grads = lax.all_gather(cotangent, "grp", axis=0, tiled=True)
     own_targets = lax.dynamic_slice_in_dim(target, row_base, group_rows)
     upstream = all_grads[own_targets]
-    grad_pre = gelu_pull(upstream.astype(jnp.float32))[0].astype(jnp.bfloat16)
+    grad_pre = (upstream.astype(jnp.float32) * slope).astype(jnp.bfloat16)
     weight_term = lax.dot_general(
         normed, grad_pre, (((0,), (0,)), ((), ())), preferred_element_type=jnp.float32
     )
@@ -89,13 +171,16 @@
     lane_start = lax.axis_index("dev") * own_rows
     own_unit = lax.dynamic_slice_in_dim(unit_rows, lane_start, own_rows, 0)
     own_scale = lax.dynamic_slice_in_dim(inv_scale, lane_start, own_rows, 0)
-    scaled_grad = grad_normed * ln_gain
-    grad_feats = own_scale * (
-        scaled_grad
-        - jnp.mean(scaled_grad, axis=1, keepdims=True)
-        - own_unit * jnp.mean(scaled_grad * own_unit, axis=1, keepdims=True)
-    )
-    return (projected, grad_feats.astype(jnp.bfloat16), grad_weight, grad_bias)
+    grad_feats = backward_norm(grad_normed, ln_gain, own_unit, own_scale)
+    return (projected, grad_feats, grad_weight, grad_bias)
+
+
+def local(*arrays):
+    feats, w_proj = arrays[0], arrays[3]
+    all_rows = feats.shape[0] * lax.axis_size("dev") * lax.axis_size("grp")
+    if all_rows * jnp.dtype(jnp.bfloat16).itemsize <= w_proj.shape[1] * jnp.dtype(jnp.float32).itemsize:
+        return gathered_plan(*arrays)
+    return summed_plan(*arrays)
 
 
 def solution(mesh):

time: 469 us -> 51.9 us (0.11)
  the two profiles are of different devices: /device:TPU:0 before, /device:TPU:27 now
where the time goes in v2:
time: 51.9 us; the launch traced here: 51.4 us
  matrix products  17.5 us (34%)
  blocking collectives  12.7 us (24%)
  starting transfers between devices  7.66 us (15%)
  other arithmetic  6.59 us (13%)
  local copies, waits for them, and re-layouts  3.07 us (6%)
  waiting for transfers between devices  3.05 us (6%)
  between operations  0.77 us (1%)
    all_gather x1, blocking collectives, gathered_plan(): rows = lax.all_gather(column, 'dev', axis=0).reshape(all_rows, vis_width)  12.7 us
    dot_general x1, matrix products, gathered_plan(): lax.dot_general(rows, grad_pre, (((0,), (0,)), ((), ())), preferred_eleme...  6.84 us
    dot_general x1, matrix products, gathered_plan(): lax.dot_general(own_pre, w_proj, (((1,), (1,)), ((), ())), preferred_elem...  4.74 us
    dot_general x1, matrix products, gathered_plan(): pre_act = jnp.dot(rows, w_proj, preferred_element_type=jnp.float32) + b_proj  4.06 us
    ppermute x4, starting transfers between devices, gather_groups(): held = jnp.concatenate([held, lax.ppermute(held, 'grp', pairs)], axis=0)  4.03 us
    all_to_all x1, starting transfers between devices, gathered_plan(): swapped = lax.all_to_all(terms.astype(jnp.bfloat16), 'dev', 0, 0)  3.63 us
    ppermute x4, waiting for transfers between devices, gather_groups(): held = jnp.concatenate([held, lax.ppermute(held, 'grp', pairs)], axis=0)  3.05 us
    gather x1, local copies, waits for them, and re-layouts, gathered_plan(): slot_target = target[slot_rows]  1.23 us
  transfers between devices with their start and end apart: 5, of which 1 were waited for; matrix products, arithmetic and copies ran while one was open for 33% of the time, Pallas kernels for 0%

profile of v2, /device:TPU:27, one launch (start us, length us, event | category | flops | bytes accessed | tf_op | source)
XLA Modules:
  0.0 51.4 jit_solution(7149673042646664760)
XLA Ops:
  0.6 0.9 %convert_reduce_fusion.2 = f32[3]{0:T(128)S(1)} fusion(bf16[3,3200]{1,0:T(4,128)(2,1)} %param.9), kind=kLoop, calls=%fused_computation.16 | loop fusion | flops 19197 | bytes 19212 | tf_op jit(solution)/shard_map/reduce_sum | solution.py:27
  1.5 0.9 %fusion.12 = f32[3]{0:T(128)S(1)} fusion(bf16[3,3200]{1,0:T(4,128)(2,1)} %param.9, f32[3]{0:T(128)S(1)} %broadcast_multiply_fusion.2), kind=kLoop, calls=%fused_computation.28 | loop fusion | flops 38397 | bytes 19224 | tf_op jit(solution)/shard_map/reduce_sum | solution.py:29
  2.5 0.9 %fusion.14 = bf16[1,3,3200]{2,1,0:T(4,128)(2,1)S(1)} fusion(bf16[3,3200]{1,0:T(4,128)(2,1)} %param.9, f32[3200]{0:T(1024)} %param.11, f32[3200]{0:T(1024)} %param.10, f32[3]{0:T(128)S(1)} %add_rsqrt_fusion, f32[3]{0:T(128)S(1)} %broadcast_multiply_fusion.2), kind=kLoop, calls=%fused_computation.32 | loop fusion | flops 57600 | bytes 64024 | tf_op jit(solution)/shard_map/broadcast_in_dim | solution.py:48
  3.3 0.2 collective-permute-start
  3.6 1.3 %collective-permute-start.2 = (bf16[1,24,1024]{2,1,0:T(8,128)(2,1)}, bf16[1,24,1024]{2,1,0:T(8,128)(2,1)S(1)}, u32[]{:S(2)}, u32[]{:S(2)}) collective-permute-start(bf16[1,24,1024]{2,1,0:T(8,128)(2,1)} %bitcast.14), channel_id=1, source_target_pairs={{0,8},{8,0},{16,24},{24,16},{1,9},{9,1},{17,25},{25,17},{2,10},{10... | collective-permute-start | bytes 147464 | tf_op jit(solution)/shard_map/ppermute | solution.py:52
  5.2 0.8 %select_reduce_fusion.1 = s32[32]{0:T(128)S(1)} fusion(s32[32]{0:T(128)} %param.16), kind=kLoop, calls=%fused_computation.41 | loop fusion | flops 3040 | bytes 256 | tf_op jit(solution)/shard_map/reduce_sum | solution.py:13
  6.0 0.7 %fusion.35 = (s32[32]{0:T(128)S(1)}, s32[32]{0:T(128)S(1)}) fusion(s32[32]{0:T(128)S(1)} %select_reduce_fusion.1, s32[32]{0:T(128)} %param.16, s32[32]{0:T(128)} %param.17, s32[32]{0:T(128)} %param.15), kind=kLoop, calls=%fused_computation.74 | loop fusion | flops 128 | bytes 768 | tf_op jit(solution)/shard_map/add | solution.py:16
  6.9 0.1 div.28
  7.4 1.2 %gather_fusion = s32[96]{0:T(128)S(1)} fusion(s32[96]{0:T(128)S(1)} %iota_add_fusion.3, s32[1024]{0:T(1024)S(1)} %pad_clamp_fusion), kind=kCustom, calls=%fused_computation | custom fusion | bytes 1152 | tf_op jit(solution)/shard_map/gather | solution.py:84
  8.7 0.1 collective-permute-start.1
  8.8 0.8 %pad_maximum_fusion.2 = bf16[2,24,1024]{2,1,0:T(8,128)(2,1)S(1)} fusion(bf16[1,24,1024]{2,1,0:T(8,128)(2,1)S(1)} %collective-permute-done.2, bf16[1,24,1024]{2,1,0:T(8,128)(2,1)} %bitcast.15), kind=kLoop, calls=%fused_computation.14 | loop fusion | flops 49152 | bytes 196608 | tf_op jit(solution)/shard_map/concatenate | solution.py:52
  9.6 2.4 %collective-permute-start.3 = (bf16[2,24,1024]{2,1,0:T(8,128)(2,1)S(1)}, bf16[2,24,1024]{2,1,0:T(8,128)(2,1)S(1)}, u32[]{:S(2)}, u32[]{:S(2)}) collective-permute-start(bf16[2,24,1024]{2,1,0:T(8,128)(2,1)S(1)} %pad_maximum_fusion.2), channel_id=1, source_target_pairs={{0,16},{8,24},{16,0},{24,8},{1,17},{9,25},{17,1},{25,9},{2,18},{10... | collective-permute-start | bytes 294920 | tf_op jit(solution)/shard_map/ppermute | solution.py:52
  12.0 3.0 %collective-permute-done.1 = bf16[2,3,3200]{2,1,0:T(4,128)(2,1)S(1)} collective-permute-done((bf16[2,3,3200]{2,1,0:T(4,128)(2,1)S(1)}, bf16[2,3,3200]{2,1,0:T(4,128)(2,1)S(1)}, u32[]{:S(2)}, u32[]{:S(2)}) %collective-permute-start.1) | collective-permute-done | bytes 38432 | tf_op jit(solution)/shard_map/ppermute | solution.py:52
  15.1 12.7 %all-gather = bf16[32,3,3200]{2,1,0:T(4,128)(2,1)S(1)} all-gather(bf16[4,3,3200]{2,1,0:T(4,128)(2,1)S(1)} %pad_maximum_fusion.1), channel_id=2, replica_groups=mesh['grp'=4,'dev'=8] {'dev'}, dimensions={0}, use_global_device_ids=true | all-gather | bytes 691200 | tf_op jit(solution)/shard_map/all_gather | solution.py:77
  27.8 0.5 %reshape.164 = bf16[96,3200]{1,0:T(8,128)(2,1)S(1)} reshape(bf16[32,3,3200]{2,1,0:T(4,128)(2,1)S(1)} %all-gather) | data formatting | bytes 1228800 | tf_op jit(solution)/shard_map/reshape | solution.py:77
  28.4 4.1 %convolution_add_fusion = f32[96,1024]{1,0:T(8,128)S(1)} fusion(bf16[96,3200]{1,0:T(8,128)(2,1)S(1)} %reshape.164, bf16[3200,1024]{1,0:T(8,128)(2,1)} %param.12, f32[1024]{0:T(1024)} %param.13), kind=kOutput, calls=%fused_computation.3 | convolution fusion | flops 629243904 | bytes 7565312 | tf_op jit(solution)/shard_map/dot_general | solution.py:85
  32.5 0.9 %convolution_convert_fusion.2 = bf16[24,1024]{1,0:T(8,128)(2,1)} fusion(f32[96,1024]{1,0:T(8,128)S(1)} %convolution_add_fusion, s32[96]{0:T(128)S(1)} %gather_fusion, s32[24]{0:T(128)S(1)} %iota_add_fusion.2), kind=kOutput, calls=%fused_computation.6 | convolution fusion | flops 5630208 | bytes 442848 | tf_op jit(solution)/shard_map/dot_general | solution.py:90
  33.4 1.0 %convert_reduce_fusion.1 = (f32[1024]{0:T(1024)}, bf16[96,1024]{1,0:T(8,128)(2,1)S(1)}) fusion(f32[96,1024]{1,0:T(8,128)S(1)} %convolution_add_fusion, bf16[96,1024]{1,0:T(8,128)(2,1)S(1)} %bitcast.13, s32[96]{0:T(128)S(1)} %add.177, s32[96]{0:T(128)S(1)} %gather_fusion), kind=kOutput, calls=%fused_computation.8 | convolution fusion | flops 20848640 | bytes 791296 | tf_op jit(solution)/shard_map/dot_general | solution.py:94
  34.4 4.7 %convolution_convert_fusion = bf16[24,3200]{1,0:T(8,128)(2,1)S(1)} fusion(bf16[3200,1024]{1,0:T(8,128)(2,1)} %param.12, bf16[96,1024]{1,0:T(8,128)(2,1)S(1)} %get-tuple-element.12, s32[96]{0:T(128)S(1)} %and_select_fusion, pred[96]{0:T(512)(128)(4,1)S(1)} %fusion.30), kind=kOutput, calls=%fused_computation.1 | convolution fusion | flops 162110976 | bytes 6904288 | tf_op jit(solution)/shard_map/dot_general | solution.py:109
  39.1 0.8 %convert_element_type.44 = bf16[8,3,3200]{2,1,0:T(4,128)(2,1)} reshape(bf16[24,3200]{1,0:T(8,128)(2,1)S(1)} %convolution_convert_fusion) | data formatting | bytes 307200 | tf_op jit(solution)/shard_map/convert_element_type | solution.py:112
  39.9 3.6 %all-to-all-start = ((bf16[8,3,3200]{2,1,0:T(4,128)(2,1)}), bf16[8,3,3200]{2,1,0:T(4,128)(2,1)S(1)}, u32[]{:S(2)}, u32[]{:S(2)}) async-start(bf16[8,3,3200]{2,1,0:T(4,128)(2,1)} %convert_element_type.44), calls=%async_computation | async-start | bytes 409600 | tf_op jit(solution)/shard_map/all_to_all | solution.py:112
  43.5 6.8 %fusion.36 = f32[3200,1024]{1,0:T(8,128)} fusion(bf16[96,3200]{1,0:T(8,128)(2,1)S(1)} %reshape.164, bf16[96,1024]{1,0:T(8,128)(2,1)S(1)} %get-tuple-element.12), kind=kOutput, calls=%fused_computation.75 | convolution fusion | flops 629145600 | bytes 13918208 | tf_op jit(solution)/shard_map/dot_general | solution.py:100
  50.5 0.2 multiply_reduce_fusion
  50.7 0.7 %fusion.11 = bf16[3,3200]{1,0:T(4,128)(2,1)} fusion(bf16[3,3200]{1,0:T(4,128)(2,1)S(1)} %copy-done, f32[3,3200]{1,0:T(4,128)S(1)} %convert_reduce_fusion, f32[3]{0:T(128)S(1)} %get-tuple-element.13, f32[3]{0:T(128)S(1)} %get-tuple-element.14, f32[3200]{0:T(1024)S(1)} %copy-done.2, f32[3]{0:T(128)S(1)} %add_rsqrt_fusion, f32[3]{0:T(128)S(1)} %broadcast_multiply_fusion.2), kind=kLoop, calls=%fused_computation.27 | loop fusion | flops 86400 | bytes 89648 | tf_op jit(solution)/shard_map/convert_element_type | solution.py:64
  (34 shorter events, 1.1 us)
Async XLA Ops:
  3.3 5.3 %collective-permute-start = (bf16[1,3,3200]{2,1,0:T(4,128)(2,1)S(1)}, bf16[1,3,3200]{2,1,0:T(4,128)(2,1)S(1)}, u32[]{:S(2)}, u32[]{:S(2)}) collective-permute-start(bf16[1,3,3200]{2,1,0:T(4,128)(2,1)S(1)} %fusion.14), channel_id=1, source_target_pairs={{0,8},{8,0},{16,24},{24,16},{1,9},{9,1},{17,25},{25,17},{2,10},{10... | collective-permute-start | bytes 57608 | tf_op jit(solution)/shard_map/ppermute | solution.py:52
  3.6 5.2 %collective-permute-start.2 = (bf16[1,24,1024]{2,1,0:T(8,128)(2,1)}, bf16[1,24,1024]{2,1,0:T(8,128)(2,1)S(1)}, u32[]{:S(2)}, u32[]{:S(2)}) collective-permute-start(bf16[1,24,1024]{2,1,0:T(8,128)(2,1)} %bitcast.14), channel_id=1, source_target_pairs={{0,8},{8,0},{16,24},{24,16},{1,9},{9,1},{17,25},{25,17},{2,10},{10... | collective-permute-start | bytes 147464 | tf_op jit(solution)/shard_map/ppermute | solution.py:52
  8.7 6.4 %collective-permute-start.1 = (bf16[2,3,3200]{2,1,0:T(4,128)(2,1)S(1)}, bf16[2,3,3200]{2,1,0:T(4,128)(2,1)S(1)}, u32[]{:S(2)}, u32[]{:S(2)}) collective-permute-start(bf16[2,3,3200]{2,1,0:T(4,128)(2,1)S(1)} %pad_maximum_fusion.3), channel_id=1, source_target_pairs={{0,16},{8,24},{16,0},{24,8},{1,17},{9,25},{17,1},{25,9},{2,18},{10... | collective-permute-start | bytes 115208 | tf_op jit(solution)/shard_map/ppermute | solution.py:52
  9.6 23.7 %collective-permute-start.3 = (bf16[2,24,1024]{2,1,0:T(8,128)(2,1)S(1)}, bf16[2,24,1024]{2,1,0:T(8,128)(2,1)S(1)}, u32[]{:S(2)}, u32[]{:S(2)}) collective-permute-start(bf16[2,24,1024]{2,1,0:T(8,128)(2,1)S(1)} %pad_maximum_fusion.2), channel_id=1, source_target_pairs={{0,16},{8,24},{16,0},{24,8},{1,17},{9,25},{17,1},{25,9},{2,18},{10... | collective-permute-start | bytes 294920 | tf_op jit(solution)/shard_map/ppermute | solution.py:52
  28.4 5.0 %copy-start.1 = (bf16[24,1024]{1,0:T(8,128)(2,1)S(1)}, bf16[24,1024]{1,0:T(8,128)(2,1)}, u32[]{:S(2)}) copy-start(bf16[24,1024]{1,0:T(8,128)(2,1)} %param.14) | copy-start | bytes 147460
  39.9 10.5 %all-to-all-start = ((bf16[8,3,3200]{2,1,0:T(4,128)(2,1)}), bf16[8,3,3200]{2,1,0:T(4,128)(2,1)S(1)}, u32[]{:S(2)}, u32[]{:S(2)}) async-start(bf16[8,3,3200]{2,1,0:T(4,128)(2,1)} %convert_element_type.44), calls=%async_computation | async-start | bytes 409600 | tf_op jit(solution)/shard_map/all_to_all | solution.py:112
  43.5 6.9 %copy-start = (bf16[3,3200]{1,0:T(4,128)(2,1)S(1)}, bf16[3,3200]{1,0:T(4,128)(2,1)}, u32[]{:S(2)}) copy-start(bf16[3,3200]{1,0:T(4,128)(2,1)} %param.9) | copy-start | bytes 57604
  43.5 7.0 %copy-start.2 = (f32[3200]{0:T(1024)S(1)}, f32[3200]{0:T(1024)}, u32[]{:S(2)}) copy-start(f32[3200]{0:T(1024)} %param.10) | copy-start | bytes 38404

commit v3 on v1

--- a/solution.py
+++ b/solution.py
@@ -1,13 +1,19 @@
+import functools
+
 import jax
 import jax.numpy as jnp
 from jax import lax
+from jax.experimental import pallas as pl
+from jax.experimental.pallas import tpu as pltpu
 from jax.sharding import PartitionSpec as P
 
 epsilon = 1e-05
-
-
-def activate(values):
-    return jax.nn.gelu(values, approximate=True)
+root_two_over_pi = 0.7978845608028654
+cubic = 0.044715
+MIB = 1 << 20
+WHOLE = pl.BlockSpec(memory_space=pltpu.VMEM)
+SCALARS = pl.BlockSpec(memory_space=pltpu.SMEM)
+LEFT = pl.BlockSpec(memory_space=pl.ANY)
 
 
 def row_targets(img_seq, img_count, img_offset, all_rows, seq_rows):
@@ -33,7 +39,225 @@
     return (unit_rows, inv_scale, unit_rows * ln_gain + ln_shift)
 
 
-def local(feats, ln_gain, ln_shift, w_proj, b_proj, cotangent, img_seq, img_count, img_offset):
+def gelu_and_slope(values):
+    square = values * values
+    bent = jnp.tanh(root_two_over_pi * values * (1.0 + cubic * square))
+    half = 0.5 * (1.0 + bent)
+    slope = half + 0.5 * values * (1.0 - bent * bent) * (
+        root_two_over_pi * (1.0 + 3.0 * cubic * square)
+    )
+    return values * half, slope
+
+
+def backward_norm(grad_normed, ln_gain, unit_rows, inv_scale):
+    scaled_grad = grad_normed * ln_gain
+    grad_feats = inv_scale * (
+        scaled_grad
+        - jnp.mean(scaled_grad, axis=1, keepdims=True)
+        - unit_rows * jnp.mean(scaled_grad * unit_rows, axis=1, keepdims=True)
+    )
+    return grad_feats.astype(jnp.bfloat16)
+
+
+def norm_pack_kernel(block, feats, gain, shift, cotangent, packed):
+    own_rows, vis_width = feats.shape
+    units = cotangent.shape[1]
+    normed = normalize(feats[...], gain[...], shift[...])[2]
+    if block > own_rows:
+        normed = jnp.concatenate([normed, jnp.zeros((block - own_rows, vis_width), jnp.float32)], axis=0)
+    pieces = []
+    for first in range(0, vis_width, units):
+        piece = normed[:, first : first + units]
+        if piece.shape[1] < units:
+            piece = jnp.concatenate([piece, jnp.zeros((block, units - piece.shape[1]), jnp.float32)], axis=1)
+        pieces.append(piece)
+    count = len(pieces) * block
+    packed[:count, :] = jnp.concatenate(pieces, axis=0).astype(jnp.bfloat16)
+    packed[count:, :] = cotangent[...]
+
+
+def unpack_kernel(block, *refs):
+    sources, (column, grads) = refs[:-2], refs[-2:]
+    vis_width, units = column.shape[1], grads.shape[1]
+    parts = [source[place] for source in sources for place in range(source.shape[0])]
+    count = (vis_width + units - 1) // units * block
+    seq_rows = parts[0].shape[0] - count
+    for at, first in enumerate(range(0, vis_width, units)):
+        width = min(units, vis_width - first)
+        piece = jnp.concatenate(
+            [part[at * block : (at + 1) * block, :width].astype(jnp.float32) for part in parts], axis=0
+        )
+        column[:, first : first + width] = piece.astype(jnp.bfloat16)
+    for at, part in enumerate(parts):
+        grads[at * seq_rows : (at + 1) * seq_rows, :] = part[count:, :]
+
+
+def slot_targets(my_group, block, own_rows, lanes, groups, img_seq, img_count, img_offset):
+    group_rows = own_rows * lanes
+    slots = lax.broadcasted_iota(jnp.int32, (1, lanes * groups * block), 1)
+    within = slots & (block - 1)
+    row_ids = (
+        (my_group ^ ((slots // block) & (groups - 1))) * group_rows
+        + slots // (block * groups) * own_rows
+        + within
+    )
+    target = jnp.zeros_like(row_ids)
+    start = jnp.int32(0)
+    for image in range(img_seq.shape[0]):
+        end = start + img_count[image]
+        member = (row_ids >= start) & (row_ids < end)
+        base = img_seq[image] * group_rows + img_offset[image] - start
+        target = jnp.where(member, row_ids + base, target)
+        start = end
+    return jnp.where(within < own_rows, target, -1)
+
+
+def fused_kernel(
+    block, own_rows, lanes, groups, width,
+    place, img_seq, img_count, img_offset, rows, grads, bias, w_far,
+    projected, grad_bias, grad_pre, terms, w_near, total, arrived,
+):
+    units = w_far.shape[1]
+    steps = units // width
+    copies = [
+        pltpu.make_async_copy(w_far.at[:, pl.ds(step * width, width)], w_near.at[step], arrived.at[step])
+        for step in range(steps)
+    ]
+    for copy in copies:
+        copy.start()
+    group_rows = own_rows * lanes
+    all_rows = group_rows * groups
+    slot_count = lanes * groups * block
+    my_group = place[0]
+    target = slot_targets(my_group, block, own_rows, lanes, groups, img_seq, img_count, img_offset)
+    places = lax.broadcasted_iota(jnp.int32, (all_rows, slot_count), 0)
+    distance = places // group_rows
+    seq_rows = places - distance * group_rows + (my_group ^ distance) * group_rows
+    routes = (target == seq_rows).astype(jnp.float32)
+    arrivals = routes[:group_rows].astype(jnp.bfloat16)
+    sources = routes.T.astype(jnp.bfloat16)
+    own_place = lax.broadcasted_iota(jnp.int32, (lanes * block, slot_count), 0)
+    own_slot = lax.broadcasted_iota(jnp.int32, (lanes * block, slot_count), 1)
+    keep = own_slot == own_place // block * (block * groups) + (own_place & (block - 1))
+    keep = keep.astype(jnp.float32).astype(jnp.bfloat16)
+    for step in range(steps):
+        copies[step].wait()
+        span = slice(step * width, (step + 1) * width)
+        weights = w_near[step]
+        pre_act = jnp.dot(rows[...], weights, preferred_element_type=jnp.float32) + bias[:, span]
+        acted, slope = gelu_and_slope(pre_act)
+        projected[:, span] = jnp.dot(
+            arrivals, acted.astype(jnp.bfloat16), preferred_element_type=jnp.float32
+        ).astype(jnp.bfloat16)
+        upstream = jnp.dot(sources, grads[:, span], preferred_element_type=jnp.float32)
+        pulled = (upstream * slope).astype(jnp.bfloat16)
+        grad_pre[:, span] = pulled
+        grad_bias[:, span] = jnp.sum(pulled.astype(jnp.float32), axis=0, keepdims=True)
+        own = jnp.dot(keep, pulled, preferred_element_type=jnp.float32).astype(jnp.bfloat16)
+        term = lax.dot_general(own, weights, (((1,), (1,)), ((), ())), preferred_element_type=jnp.float32)
+        if step:
+            term = total[...] + term
+        if step + 1 < steps:
+            total[...] = term
+        else:
+            terms[...] = term.astype(jnp.bfloat16)
+
+
+def grad_weight_kernel(height, rows, grad_pre, far, near, left):
+    copies = []
+    for step in range(rows.shape[1] // height):
+        span = slice(step * height, (step + 1) * height)
+        near[span, :] = lax.dot_general(
+            rows[:, span], grad_pre[...], (((0,), (0,)), ((), ())), preferred_element_type=jnp.float32
+        )
+        copies.append(pltpu.make_async_copy(near.at[span], far.at[span], left.at[step]))
+        copies[-1].start()
+    for copy in copies:
+        copy.wait()
+
+
+def gathered_plan(feats, ln_gain, ln_shift, w_proj, b_proj, cotangent, img_seq, img_count, img_offset):
+    lanes = lax.axis_size("dev")
+    groups = lax.axis_size("grp")
+    my_group = lax.axis_index("grp")
+    own_rows, vis_width = feats.shape
+    units = w_proj.shape[1]
+    group_rows = own_rows * lanes
+    all_rows = group_rows * groups
+    block = pl.next_power_of_2(own_rows)
+    slot_count = lanes * groups * block
+    bfloat16, float32 = jnp.bfloat16, jnp.float32
+    packed_rows = pl.cdiv(vis_width, units) * block + group_rows
+    held = pl.pallas_call(
+        functools.partial(norm_pack_kernel, block),
+        out_shape=jax.ShapeDtypeStruct((packed_rows, units), bfloat16),
+        in_specs=[WHOLE] * 4,
+        out_specs=WHOLE,
+        compiler_params=pltpu.CompilerParams(vmem_limit_bytes=8 * MIB),
+        name="norm_pack",
+    )(feats, ln_gain[None], ln_shift[None], cotangent)[None]
+    parts = [held]
+    step = 1
+    while step < groups:
+        held = parts[0] if len(parts) == 1 else jnp.concatenate(parts, axis=0)
+        pairs = [(group, group ^ step) for group in range(groups)]
+        parts = [held, lax.ppermute(held, "grp", pairs)]
+        step *= 2
+    column, grads = pl.pallas_call(
+        functools.partial(unpack_kernel, block),
+        out_shape=(
+            jax.ShapeDtypeStruct((groups * block, vis_width), bfloat16),
+            jax.ShapeDtypeStruct((all_rows, units), bfloat16),
+        ),
+        in_specs=[WHOLE] * len(parts),
+        out_specs=(WHOLE, WHOLE),
+        compiler_params=pltpu.CompilerParams(vmem_limit_bytes=8 * MIB),
+        name="unpack",
+    )(*parts)
+    rows = lax.all_gather(column, "dev", axis=0, tiled=True)
+    width = 256 if units % 256 == 0 else units
+    projected, grad_bias, grad_pre, terms = pl.pallas_call(
+        functools.partial(fused_kernel, block, own_rows, lanes, groups, width),
+        out_shape=(
+            jax.ShapeDtypeStruct((group_rows, units), bfloat16),
+            jax.ShapeDtypeStruct((1, units), float32),
+            jax.ShapeDtypeStruct((slot_count, units), bfloat16),
+            jax.ShapeDtypeStruct((lanes * block, vis_width), bfloat16),
+        ),
+        in_specs=[SCALARS] * 4 + [WHOLE] * 3 + [LEFT],
+        out_specs=(WHOLE,) * 4,
+        scratch_shapes=[
+            pltpu.VMEM((units // width, vis_width, width), bfloat16),
+            pltpu.VMEM((lanes * block, vis_width), float32),
+            pltpu.SemaphoreType.DMA((units // width,)),
+        ],
+        compiler_params=pltpu.CompilerParams(vmem_limit_bytes=24 * MIB),
+        name="fused",
+    )(my_group[None], img_seq, img_count, img_offset, rows, grads, b_proj[None], w_proj)
+    swapped = lax.all_to_all(terms.reshape(lanes, block, vis_width), "dev", 0, 0)
+    height = 128 if vis_width % 128 == 0 else vis_width
+    grad_weight = pl.pallas_call(
+        functools.partial(grad_weight_kernel, height),
+        out_shape=jax.ShapeDtypeStruct((vis_width, units), float32),
+        in_specs=[WHOLE] * 2,
+        out_specs=LEFT,
+        scratch_shapes=[
+            pltpu.VMEM((vis_width, units), float32),
+            pltpu.SemaphoreType.DMA((vis_width // height,)),
+        ],
+        compiler_params=pltpu.CompilerParams(vmem_limit_bytes=24 * MIB),
+        cost_estimate=pl.CostEstimate(
+            flops=2 * slot_count * vis_width * units, bytes_accessed=4 * vis_width * units, transcendentals=0
+        ),
+        name="grad_weight",
+    )(rows, grad_pre)
+    grad_normed = jnp.sum(swapped.astype(float32), axis=0)[:own_rows]
+    unit_rows, inv_scale, _ = normalize(feats, ln_gain, ln_shift)
+    grad_feats = backward_norm(grad_normed, ln_gain, unit_rows, inv_scale)
+    return (projected, grad_feats, grad_weight, grad_bias[0])
+
+
+def summed_plan(feats, ln_gain, ln_shift, w_proj, b_proj, cotangent, img_seq, img_count, img_offset):
     lane_count = lax.axis_size("dev")
     groups = lax.axis_size("grp")
     my_group = lax.axis_index("grp")
@@ -50,14 +274,14 @@
     unit_rows, inv_scale, normed = normalize(whole, ln_gain, ln_shift)
     normed = normed.astype(jnp.bfloat16)
     pre_act = jnp.dot(normed, w_proj, preferred_element_type=jnp.float32) + b_proj
-    acted, gelu_pull = jax.vjp(activate, pre_act)
+    acted, slope = gelu_and_slope(pre_act)
     local_cols = acted.astype(jnp.bfloat16)
     all_cols = lax.all_gather(local_cols, "grp", axis=0, tiled=True)
     projected = all_cols[arrivals]
     all_grads = lax.all_gather(cotangent, "grp", axis=0, tiled=True)
     own_targets = lax.dynamic_slice_in_dim(target, row_base, group_rows)
     upstream = all_grads[own_targets]
-    grad_pre = gelu_pull(upstream.astype(jnp.float32))[0].astype(jnp.bfloat16)
+    grad_pre = (upstream.astype(jnp.float32) * slope).astype(jnp.bfloat16)
     weight_term = lax.dot_general(
         normed, grad_pre, (((0,), (0,)), ((), ())), preferred_element_type=jnp.float32
     )
@@ -89,13 +313,18 @@
     lane_start = lax.axis_index("dev") * own_rows
     own_unit = lax.dynamic_slice_in_dim(unit_rows, lane_start, own_rows, 0)
     own_scale = lax.dynamic_slice_in_dim(inv_scale, lane_start, own_rows, 0)
-    scaled_grad = grad_normed * ln_gain
-    grad_feats = own_scale * (
-        scaled_grad
-        - jnp.mean(scaled_grad, axis=1, keepdims=True)
-        - own_unit * jnp.mean(scaled_grad * own_unit, axis=1, keepdims=True)
-    )
-    return (projected, grad_feats.astype(jnp.bfloat16), grad_weight, grad_bias)
+    grad_feats = backward_norm(grad_normed, ln_gain, own_unit, own_scale)
+    return (projected, grad_feats, grad_weight, grad_bias)
+
+
+def local(*arrays):
+    feats, w_proj = arrays[0], arrays[3]
+    all_rows = feats.shape[0] * lax.axis_size("dev") * lax.axis_size("grp")
+    groups = lax.axis_size("grp")
+    lighter = all_rows * jnp.dtype(jnp.bfloat16).itemsize <= w_proj.shape[1] * jnp.dtype(jnp.float32).itemsize
+    if lighter and groups & (groups - 1) == 0:
+        return gathered_plan(*arrays)
+    return summed_plan(*arrays)
 
 
 def solution(mesh):

time: 469 us -> 54.6 us (0.12)
  blocking collectives: 265 us -> 10.4 us
  waiting for transfers between devices: 93.6 us -> 9.2 us
  local copies, waits for them, and re-layouts: 68 us -> 9.24 us
  matrix products: 16.2 us -> 0 us
  between operations: 16.9 us -> 0.73 us
  Pallas kernels: 0 us -> 12.7 us
  starting transfers between devices: 2.21 us -> 9.56 us
    unnamed x1 -> x0, blocking collectives: 222 us -> none
    all_gather x1 -> x0, waiting for transfers between devices: 77.2 us -> none  [local(): lax.all_gather(summed_share.astype(jnp.bfloat16), 'grp', axis=0, tiled=True)]
    all_gather x3 -> x1, blocking collectives: 43.5 us -> 10.4 us  [gathered_plan(): rows = lax.all_gather(column, 'dev', axis=0, tiled=True)]
    concatenate x1 -> x0, local copies, waits for them, and re-layouts: 29.9 us -> none  [local(): jnp.concatenate([weight_term, bias_term[None, :], jnp.zeros((padded_rows...]
    unnamed x4 -> x0, waiting for transfers between devices: 16.3 us -> none
    dot_general x3 -> x0, matrix products: 16.2 us -> none  [the longest x1 6.87 us: local(): lax.dot_general(normed, grad_pre, (((0,), (0,)), ((), ())), preferred_ele...]
    slice x2 -> x0, local copies, waits for them, and re-layouts: 13.9 us -> none  [the longest x1 12.5 us: local(): grad_weight = summed_whole[:vis_width]]
    pallas_call x0 -> x4, Pallas kernels: none -> 12.7 us  [the longest x1 7.31 us: gathered_plan(): pl.pallas_call(functools.partial(fused_kernel, block, own_rows, lanes, gr...]
  transfers between devices with their start and end apart: 3 -> 3, of which waited for: 2 -> 3; matrix products, arithmetic and copies ran while one was open for 5% -> 2% of each run, Pallas kernels for 0% -> 10%
where the time goes in v3:
time: 54.6 us; the launch traced here: 54 us
  Pallas kernels  12.7 us (23%)
  blocking collectives  10.4 us (19%)
  starting transfers between devices  9.56 us (18%)
  local copies, waits for them, and re-layouts  9.24 us (17%)
  waiting for transfers between devices  9.2 us (17%)
  other arithmetic  2.13 us (4%)
  between operations  0.73 us (1%)
    all_gather x1, blocking collectives, gathered_plan(): rows = lax.all_gather(column, 'dev', axis=0, tiled=True)  10.4 us
    ppermute x2, waiting for transfers between devices, gathered_plan(): parts = [held, lax.ppermute(held, 'grp', pairs)]  8.14 us
    pallas_call x1, Pallas kernels, gathered_plan(): pl.pallas_call(functools.partial(fused_kernel, block, own_rows, lanes, gr...  7.31 us
    unnamed x18, local copies, waits for them, and re-layouts  7.06 us
    ppermute x2, starting transfers between devices, gathered_plan(): parts = [held, lax.ppermute(held, 'grp', pairs)]  6.16 us
    pallas_call x1, Pallas kernels, gathered_plan(): pl.pallas_call(functools.partial(grad_weight_kernel, height), out_shape=j...  5.17 us
    all_to_all x1, starting transfers between devices, gathered_plan(): lax.all_to_all(terms.reshape(lanes, block, vis_width), 'dev', 0, 0)  3.39 us
  transfers between devices with their start and end apart: 3, of which 3 were waited for; matrix products, arithmetic and copies ran while one was open for 2% of the time, Pallas kernels for 10%

profile of v3, /device:TPU:0, one launch (start us, length us, event | category | flops | bytes accessed | tf_op | source)
XLA Modules:
  0.0 54.0 jit_solution(5830778955163058424)
XLA Ops:
  0.7 0.7 %broadcast_in_dim.22.shift = f32[1,3200]{1,0:T(1,128)S(1)} reshape(f32[3200]{0:T(1024)} %param.11) | data formatting | bytes 25600 | tf_op jit(solution)/shard_map/broadcast_in_dim | solution.py:198
  1.4 0.7 %broadcast_in_dim.21.gain = f32[1,3200]{1,0:T(1,128)S(1)} reshape(f32[3200]{0:T(1024)} %param.10) | data formatting | bytes 25600 | tf_op jit(solution)/shard_map/broadcast_in_dim | solution.py:198
  2.1 0.7 %copy-done.1 = bf16[3,3200]{1,0:T(4,128)(2,1)S(1)} copy-done((bf16[3,3200]{1,0:T(4,128)(2,1)S(1)}, bf16[3,3200]{1,0:T(4,128)(2,1)}, u32[]{:S(2)}) %copy-start.1) | copy-done | bytes 19224
  2.9 0.8 %copy-done.3 = bf16[24,1024]{1,0:T(8,128)(2,1)S(1)} copy-done((bf16[24,1024]{1,0:T(8,128)(2,1)S(1)}, bf16[24,1024]{1,0:T(8,128)(2,1)}, u32[]{:S(2)}) %copy-start.3) | copy-done | bytes 49176
  3.7 0.2 norm_pack.1
  3.9 3.1 %collective-permute-start = (bf16[1,40,1024]{2,1,0:T(8,128)(2,1)S(1)}, bf16[1,40,1024]{2,1,0:T(8,128)(2,1)S(1)}, u32[]{:S(2)}, u32[]{:S(2)}) collective-permute-start(bf16[1,40,1024]{2,1,0:T(8,128)(2,1)S(1)} %bitcast.4), channel_id=1, source_target_pairs={{0,8},{8,0},{16,24},{24,16},{1,9},{9,1},{17,25},{25,17},{2,10},{10... | collective-permute-start | bytes 245768 | tf_op jit(solution)/shard_map/ppermute | solution.py:204
  7.0 0.1 convert_reduce_fusion.1
  7.1 2.3 %collective-permute-done = bf16[1,40,1024]{2,1,0:T(8,128)(2,1)S(1)} collective-permute-done((bf16[1,40,1024]{2,1,0:T(8,128)(2,1)S(1)}, bf16[1,40,1024]{2,1,0:T(8,128)(2,1)S(1)}, u32[]{:S(2)}, u32[]{:S(2)}) %collective-permute-start) | collective-permute-done | bytes 81952 | tf_op jit(solution)/shard_map/ppermute | solution.py:204
  9.5 3.1 %collective-permute-start.1 = (bf16[2,40,1024]{2,1,0:T(8,128)(2,1)S(1)}, bf16[2,40,1024]{2,1,0:T(8,128)(2,1)S(1)}, u32[]{:S(2)}, u32[]{:S(2)}) collective-permute-start(bf16[2,40,1024]{2,1,0:T(8,128)(2,1)S(1)} %pad_maximum_fusion.refs_0_), channel_id=1, source_target_pairs={{0,16},{8,24},{16,0},{24,8},{1,17},{9,25},{17,1},{25,9},{2,18},{10... | collective-permute-start | bytes 491528 | tf_op jit(solution)/shard_map/ppermute | solution.py:204
  12.5 0.9 %fusion.8 = f32[3]{0:T(128)S(1)} fusion(bf16[3,3200]{1,0:T(4,128)(2,1)} %feats.1, f32[3]{0:T(128)S(1)} %broadcast_multiply_fusion.2), kind=kLoop, calls=%fused_computation.12 | loop fusion | flops 38397 | bytes 19224 | tf_op jit(solution)/shard_map/reduce_sum | solution.py:37
  13.5 5.8 %collective-permute-done.1.refs_1_ = bf16[2,40,1024]{2,1,0:T(8,128)(2,1)S(1)} collective-permute-done((bf16[2,40,1024]{2,1,0:T(8,128)(2,1)S(1)}, bf16[2,40,1024]{2,1,0:T(8,128)(2,1)S(1)}, u32[]{:S(2)}, u32[]{:S(2)}) %collective-permute-start.1) | collective-permute-done | bytes 163872 | tf_op jit(solution)/shard_map/ppermute | solution.py:204
  19.4 10.4 %all_gather.3.rows = bf16[128,3200]{1,0:T(8,128)(2,1)S(1)} all-gather(bf16[16,3200]{1,0:T(8,128)(2,1)S(1)} %get-tuple-element.10), channel_id=1, replica_groups=mesh['grp'=4,'dev'=8] {'dev'}, dimensions={0}, use_global_device_ids=true | all-gather | bytes 921600 | tf_op jit(solution)/shard_map/all_gather | solution.py:217
  29.7 2.9 %copy-done = bf16[3200,1024]{1,0:T(8,128)(2,1)S(1)} copy-done((bf16[3200,1024]{1,0:T(8,128)(2,1)S(1)}, bf16[3200,1024]{1,0:T(8,128)(2,1)}, u32[]{:S(2)}) %copy-start) | copy-done | bytes 6553624
  32.6 0.7 %copy-done.4 = f32[1024]{0:T(1024)S(1)} copy-done((f32[1024]{0:T(1024)S(1)}, f32[1024]{0:T(1024)}, u32[]{:S(2)}) %copy-start.4) | copy-done | bytes 4120
  33.3 0.7 %copy-done.5 = s32[32]{0:T(128)S(1)} copy-done((s32[32]{0:T(128)S(1)}, s32[32]{0:T(128)}, u32[]{:S(2)}) %copy-start.5) | copy-done | bytes 152
  33.9 0.7 %copy-done.6 = s32[32]{0:T(128)S(1)} copy-done((s32[32]{0:T(128)S(1)}, s32[32]{0:T(128)}, u32[]{:S(2)}) %copy-start.6) | copy-done | bytes 152
  34.6 0.7 %copy-done.7 = s32[32]{0:T(128)S(1)} copy-done((s32[32]{0:T(128)S(1)}, s32[32]{0:T(128)}, u32[]{:S(2)}) %copy-start.7) | copy-done | bytes 152
  35.2 7.3 %fused.1 = (bf16[24,1024]{1,0:T(8,128)(2,1)}, f32[1,1024]{1,0:T(1,128)}, bf16[128,1024]{1,0:T(8,128)(2,1)S(1)}, bf16[32,3200]{1,0:T(8,128)(2,1)S(1)}) custom-call(s32[1]{0:T(128)} %bitcast.place, s32[32]{0:T(128)S(1)} %copy-done.5, s32[32]{0:T(128)S(1)} %copy-done.6, s32[32]{0:T(128)S(1)} %copy-done.7, bf16[128,3200]{1,0:T(8,128)(2,1)S(1)} %all_gather.3.rows, ...), custom_call_target="tpu_custom_call" | custom-call | tf_op jit(solution)/shard_map/fused/pallas_call | solution.py:219
  42.6 0.7 %reshape.32 = bf16[8,4,3200]{2,1,0:T(4,128)(2,1)} reshape(bf16[32,3200]{1,0:T(8,128)(2,1)S(1)} %get-tuple-element.13) | data formatting | bytes 409600 | tf_op jit(solution)/shard_map/reshape | solution.py:237
  43.3 3.4 %all-to-all-start = ((bf16[8,4,3200]{2,1,0:T(4,128)(2,1)}), bf16[8,4,3200]{2,1,0:T(4,128)(2,1)S(1)}, u32[]{:S(2)}, u32[]{:S(2)}) async-start(bf16[8,4,3200]{2,1,0:T(4,128)(2,1)} %reshape.32), calls=%async_computation | async-start | bytes 409600 | tf_op jit(solution)/shard_map/all_to_all | solution.py:237
  46.7 5.2 %grad_weight.1 = f32[3200,1024]{1,0:T(8,128)} custom-call(bf16[128,3200]{1,0:T(8,128)(2,1)S(1)} %all_gather.3.rows, bf16[128,1024]{1,0:T(8,128)(2,1)S(1)} %get-tuple-element.14.grad_pre), custom_call_target="tpu_custom_call" | custom-call | flops 838860800 | bytes 13107200 | tf_op jit(solution)/shard_map/grad_weight/pallas_call | solution.py:239
  51.9 1.1 %all-to-all-done = bf16[8,4,3200]{2,1,0:T(4,128)(2,1)S(1)} async-done(((bf16[8,4,3200]{2,1,0:T(4,128)(2,1)}), bf16[8,4,3200]{2,1,0:T(4,128)(2,1)S(1)}, u32[]{:S(2)}, u32[]{:S(2)}) %all-to-all-start) | async-done | bytes 204832 | tf_op jit(solution)/shard_map/all_to_all | solution.py:237
  53.0 0.2 fusion.9
  53.3 0.7 %fusion.7 = bf16[3,3200]{1,0:T(4,128)(2,1)} fusion(bf16[3,3200]{1,0:T(4,128)(2,1)S(1)} %copy-done.2, f32[4,3200]{1,0:T(4,128)S(1)} %convert_reduce_fusion, f32[3]{0:T(128)S(1)} %get-tuple-element.18, f32[3]{0:T(128)S(1)} %get-tuple-element.19, f32[3200]{0:T(1024)S(1)} %copy-done.8, f32[3]{0:T(128)S(1)} %add_rsqrt_fusion, f32[3]{0:T(128)S(1)} %broadcast_multiply_fusion.2), kind=kLoop, calls=%fused_computation.11 | loop fusion | flops 86400 | bytes 89648 | tf_op jit(solution)/shard_map/convert_element_type | solution.py:59
  (17 shorter events, 0.2 us)
Async XLA Ops:
  0.6 52.4 %copy-start.8 = (f32[3200]{0:T(1024)S(1)}, f32[3200]{0:T(1024)}, u32[]{:S(2)}) copy-start(f32[3200]{0:T(1024)} %param.10) | copy-start | bytes 38404
  0.6 52.4 %copy-start.2 = (bf16[3,3200]{1,0:T(4,128)(2,1)S(1)}, bf16[3,3200]{1,0:T(4,128)(2,1)}, u32[]{:S(2)}) copy-start(bf16[3,3200]{1,0:T(4,128)(2,1)} %feats.1) | copy-start | bytes 57604
  2.1 0.7 %copy-start.1 = (bf16[3,3200]{1,0:T(4,128)(2,1)S(1)}, bf16[3,3200]{1,0:T(4,128)(2,1)}, u32[]{:S(2)}) copy-start(bf16[3,3200]{1,0:T(4,128)(2,1)} %feats.1) | copy-start | bytes 57604
  2.9 0.8 %copy-start.3 = (bf16[24,1024]{1,0:T(8,128)(2,1)S(1)}, bf16[24,1024]{1,0:T(8,128)(2,1)}, u32[]{:S(2)}) copy-start(bf16[24,1024]{1,0:T(8,128)(2,1)} %cotangent.1) | copy-start | bytes 147460
  3.9 5.5 %collective-permute-start = (bf16[1,40,1024]{2,1,0:T(8,128)(2,1)S(1)}, bf16[1,40,1024]{2,1,0:T(8,128)(2,1)S(1)}, u32[]{:S(2)}, u32[]{:S(2)}) collective-permute-start(bf16[1,40,1024]{2,1,0:T(8,128)(2,1)S(1)} %bitcast.4), channel_id=1, source_target_pairs={{0,8},{8,0},{16,24},{24,16},{1,9},{9,1},{17,25},{25,17},{2,10},{10... | collective-permute-start | bytes 245768 | tf_op jit(solution)/shard_map/ppermute | solution.py:204
  9.5 9.9 %collective-permute-start.1 = (bf16[2,40,1024]{2,1,0:T(8,128)(2,1)S(1)}, bf16[2,40,1024]{2,1,0:T(8,128)(2,1)S(1)}, u32[]{:S(2)}, u32[]{:S(2)}) collective-permute-start(bf16[2,40,1024]{2,1,0:T(8,128)(2,1)S(1)} %pad_maximum_fusion.refs_0_), channel_id=1, source_target_pairs={{0,16},{8,24},{16,0},{24,8},{1,17},{9,25},{17,1},{25,9},{2,18},{10... | collective-permute-start | bytes 491528 | tf_op jit(solution)/shard_map/ppermute | solution.py:204
  29.7 2.9 %copy-start = (bf16[3200,1024]{1,0:T(8,128)(2,1)S(1)}, bf16[3200,1024]{1,0:T(8,128)(2,1)}, u32[]{:S(2)}) copy-start(bf16[3200,1024]{1,0:T(8,128)(2,1)} %w_far.1) | copy-start | bytes 19660804
  32.6 0.7 %copy-start.4 = (f32[1024]{0:T(1024)S(1)}, f32[1024]{0:T(1024)}, u32[]{:S(2)}) copy-start(f32[1024]{0:T(1024)} %param.13) | copy-start | bytes 12292
  33.3 0.7 %copy-start.5 = (s32[32]{0:T(128)S(1)}, s32[32]{0:T(128)}, u32[]{:S(2)}) copy-start(s32[32]{0:T(128)} %img_seq.1) | copy-start | bytes 388
  33.9 0.7 %copy-start.6 = (s32[32]{0:T(128)S(1)}, s32[32]{0:T(128)}, u32[]{:S(2)}) copy-start(s32[32]{0:T(128)} %img_count.1) | copy-start | bytes 388
  34.6 0.7 %copy-start.7 = (s32[32]{0:T(128)S(1)}, s32[32]{0:T(128)}, u32[]{:S(2)}) copy-start(s32[32]{0:T(128)} %img_offset.1) | copy-start | bytes 388
  43.3 9.7 %all-to-all-start = ((bf16[8,4,3200]{2,1,0:T(4,128)(2,1)}), bf16[8,4,3200]{2,1,0:T(4,128)(2,1)S(1)}, u32[]{:S(2)}, u32[]{:S(2)}) async-start(bf16[8,4,3200]{2,1,0:T(4,128)(2,1)} %reshape.32), calls=%async_computation | async-start | bytes 409600 | tf_op jit(solution)/shard_map/all_to_all | solution.py:237

commit v4 on v3

--- a/solution.py
+++ b/solution.py
@@ -59,37 +59,22 @@
     return grad_feats.astype(jnp.bfloat16)
 
 
-def norm_pack_kernel(block, feats, gain, shift, cotangent, packed):
-    own_rows, vis_width = feats.shape
-    units = cotangent.shape[1]
-    normed = normalize(feats[...], gain[...], shift[...])[2]
-    if block > own_rows:
-        normed = jnp.concatenate([normed, jnp.zeros((block - own_rows, vis_width), jnp.float32)], axis=0)
-    pieces = []
-    for first in range(0, vis_width, units):
-        piece = normed[:, first : first + units]
-        if piece.shape[1] < units:
-            piece = jnp.concatenate([piece, jnp.zeros((block, units - piece.shape[1]), jnp.float32)], axis=1)
-        pieces.append(piece)
-    count = len(pieces) * block
-    packed[:count, :] = jnp.concatenate(pieces, axis=0).astype(jnp.bfloat16)
-    packed[count:, :] = cotangent[...]
-
-
-def unpack_kernel(block, *refs):
-    sources, (column, grads) = refs[:-2], refs[-2:]
-    vis_width, units = column.shape[1], grads.shape[1]
-    parts = [source[place] for source in sources for place in range(source.shape[0])]
-    count = (vis_width + units - 1) // units * block
-    seq_rows = parts[0].shape[0] - count
-    for at, first in enumerate(range(0, vis_width, units)):
-        width = min(units, vis_width - first)
-        piece = jnp.concatenate(
-            [part[at * block : (at + 1) * block, :width].astype(jnp.float32) for part in parts], axis=0
-        )
-        column[:, first : first + width] = piece.astype(jnp.bfloat16)
-    for at, part in enumerate(parts):
-        grads[at * seq_rows : (at + 1) * seq_rows, :] = part[count:, :]
+def norm_kernel(feats, gain, shift, cotangent, normed, grads):
+    rows = normalize(feats[...], gain[...][None], shift[...][None])[2]
+    empty = normed.shape[0] - rows.shape[0]
+    if empty:
+        rows = jnp.concatenate([rows, jnp.zeros((empty, rows.shape[1]), jnp.float32)], axis=0)
+    normed[...] = rows.astype(jnp.bfloat16)
+    grads[...] = cotangent[...]
+
+
+def distance_of(place, groups):
+    distance = jnp.zeros_like(place)
+    step, bit = groups // 2, 1
+    while step:
+        distance = jnp.where((place & bit) != 0, distance + step, distance)
+        step, bit = step // 2, bit * 2
+    return distance
 
 
 def slot_targets(my_group, block, own_rows, lanes, groups, img_seq, img_count, img_offset):
@@ -97,7 +82,7 @@
     slots = lax.broadcasted_iota(jnp.int32, (1, lanes * groups * block), 1)
     within = slots & (block - 1)
     row_ids = (
-        (my_group ^ ((slots // block) & (groups - 1))) * group_rows
+        (my_group ^ distance_of((slots // block) & (groups - 1), groups)) * group_rows
         + slots // (block * groups) * own_rows
         + within
     )
@@ -131,8 +116,8 @@
     my_group = place[0]
     target = slot_targets(my_group, block, own_rows, lanes, groups, img_seq, img_count, img_offset)
     places = lax.broadcasted_iota(jnp.int32, (all_rows, slot_count), 0)
-    distance = places // group_rows
-    seq_rows = places - distance * group_rows + (my_group ^ distance) * group_rows
+    held = places // group_rows
+    seq_rows = places - held * group_rows + (my_group ^ distance_of(held, groups)) * group_rows
     routes = (target == seq_rows).astype(jnp.float32)
     arrivals = routes[:group_rows].astype(jnp.bfloat16)
     sources = routes.T.astype(jnp.bfloat16)
@@ -176,6 +161,10 @@
         copy.wait()
 
 
+def in_hbm(*arrays):
+    return [pltpu.with_memory_space_constraint(array, pltpu.HBM) for array in arrays]
+
+
 def gathered_plan(feats, ln_gain, ln_shift, w_proj, b_proj, cotangent, img_seq, img_count, img_offset):
     lanes = lax.axis_size("dev")
     groups = lax.axis_size("grp")
@@ -187,33 +176,23 @@
     block = pl.next_power_of_2(own_rows)
     slot_count = lanes * groups * block
     bfloat16, float32 = jnp.bfloat16, jnp.float32
-    packed_rows = pl.cdiv(vis_width, units) * block + group_rows
-    held = pl.pallas_call(
-        functools.partial(norm_pack_kernel, block),
-        out_shape=jax.ShapeDtypeStruct((packed_rows, units), bfloat16),
+    column, grads = pl.pallas_call(
+        norm_kernel,
+        out_shape=(
+            jax.ShapeDtypeStruct((block, vis_width), bfloat16),
+            jax.ShapeDtypeStruct(cotangent.shape, bfloat16),
+        ),
         in_specs=[WHOLE] * 4,
-        out_specs=WHOLE,
-        compiler_params=pltpu.CompilerParams(vmem_limit_bytes=8 * MIB),
-        name="norm_pack",
-    )(feats, ln_gain[None], ln_shift[None], cotangent)[None]
-    parts = [held]
-    step = 1
-    while step < groups:
-        held = parts[0] if len(parts) == 1 else jnp.concatenate(parts, axis=0)
-        pairs = [(group, group ^ step) for group in range(groups)]
-        parts = [held, lax.ppermute(held, "grp", pairs)]
-        step *= 2
-    column, grads = pl.pallas_call(
-        functools.partial(unpack_kernel, block),
-        out_shape=(
-            jax.ShapeDtypeStruct((groups * block, vis_width), bfloat16),
-            jax.ShapeDtypeStruct((all_rows, units), bfloat16),
-        ),
-        in_specs=[WHOLE] * len(parts),
         out_specs=(WHOLE, WHOLE),
         compiler_params=pltpu.CompilerParams(vmem_limit_bytes=8 * MIB),
-        name="unpack",
-    )(*parts)
+        name="norm",
+    )(*in_hbm(feats, ln_gain, ln_shift, cotangent))
+    step = groups // 2
+    while step:
+        pairs = [(group, group ^ step) for group in range(groups)]
+        column = jnp.concatenate([column, lax.ppermute(column, "grp", pairs)], axis=0)
+        grads = jnp.concatenate([grads, lax.ppermute(grads, "grp", pairs)], axis=0)
+        step //= 2
     rows = lax.all_gather(column, "dev", axis=0, tiled=True)
     width = 256 if units % 256 == 0 else units
     projected, grad_bias, grad_pre, terms = pl.pallas_call(
@@ -233,7 +212,7 @@
         ],
         compiler_params=pltpu.CompilerParams(vmem_limit_bytes=24 * MIB),
         name="fused",
-    )(my_group[None], img_seq, img_count, img_offset, rows, grads, b_proj[None], w_proj)
+    )(my_group[None], *in_hbm(img_seq, img_count, img_offset), rows, grads, *in_hbm(b_proj[None], w_proj))
     swapped = lax.all_to_all(terms.reshape(lanes, block, vis_width), "dev", 0, 0)
     height = 128 if vis_width % 128 == 0 else vis_width
     grad_weight = pl.pallas_call(

time: 54.6 us -> 43.1 us (0.79)
  local copies, waits for them, and re-layouts: 9.24 us -> 0.74 us
  waiting for transfers between devices: 9.2 us -> 2.44 us
  Pallas kernels: 12.7 us -> 14.2 us
  starting transfers between devices: 9.56 us -> 10.9 us
  other arithmetic: 2.13 us -> 2.96 us
    unnamed x18 -> x4, local copies, waits for them, and re-layouts: 7.06 us -> 0.01 us
    ppermute x2 -> x4, waiting for transfers between devices: 8.14 us -> 1.37 us  [the longest x2 1.36 us: gathered_plan(): grads = jnp.concatenate([grads, lax.ppermute(grads, 'grp', pairs)], axis=0)]
    broadcast_in_dim x2 -> x0, local copies, waits for them, and re-layouts: 1.47 us -> none  [the longest x1 0.74 us: gathered_plan(): ln_shift[None]]
    ppermute x2 -> x4, starting transfers between devices: 6.16 us -> 7.49 us  [the longest x2 6 us: gathered_plan(): lax.ppermute(column, 'grp', pairs)]
    pallas_call x2 -> x1, Pallas kernels: 0.26 us -> 1.09 us  [gathered_plan(): pl.pallas_call(norm_kernel, out_shape=(jax.ShapeDtypeStruct((block, vis_w...]
    reduce_sum x1, other arithmetic: 0.14 us -> 0.88 us  [normalize(): row_mean = jnp.mean(values, axis=1, keepdims=True)]
    pallas_call x1, Pallas kernels: 7.31 us -> 7.94 us  [gathered_plan(): pl.pallas_call(functools.partial(fused_kernel, block, own_rows, lanes, gr...]
  transfers between devices with their start and end apart: 3 -> 5, of which waited for: 3 -> 2; matrix products, arithmetic and copies ran while one was open for 2% -> 5% of each run, Pallas kernels for 10% -> 12%
where the time goes in v4:
time: 43.1 us; the launch traced here: 42.7 us
  Pallas kernels  14.2 us (33%)
  starting transfers between devices  10.9 us (25%)
  blocking collectives  10.7 us (25%)
  other arithmetic  2.96 us (7%)
  waiting for transfers between devices  2.44 us (6%)
  local copies, waits for them, and re-layouts  0.74 us (2%)
  between operations  0.73 us (2%)
    all_gather x1, blocking collectives, gathered_plan(): rows = lax.all_gather(column, 'dev', axis=0, tiled=True)  10.7 us
    pallas_call x1, Pallas kernels, gathered_plan(): pl.pallas_call(functools.partial(fused_kernel, block, own_rows, lanes, gr...  7.94 us
    ppermute x2, starting transfers between devices, gathered_plan(): lax.ppermute(column, 'grp', pairs)  6 us
    pallas_call x1, Pallas kernels, gathered_plan(): pl.pallas_call(functools.partial(grad_weight_kernel, height), out_shape=j...  5.17 us
    all_to_all x1, starting transfers between devices, gathered_plan(): lax.all_to_all(terms.reshape(lanes, block, vis_width), 'dev', 0, 0)  3.39 us
    ppermute x2, starting transfers between devices, gathered_plan(): grads = jnp.concatenate([grads, lax.ppermute(grads, 'grp', pairs)], axis=0)  1.49 us
    ppermute x2, waiting for transfers between devices, gathered_plan(): grads = jnp.concatenate([grads, lax.ppermute(grads, 'grp', pairs)], axis=0)  1.36 us
    pallas_call x1, Pallas kernels, gathered_plan(): pl.pallas_call(norm_kernel, out_shape=(jax.ShapeDtypeStruct((block, vis_w...  1.09 us
  transfers between devices with their start and end apart: 5, of which 2 were waited for; matrix products, arithmetic and copies ran while one was open for 5% of the time, Pallas kernels for 12%

profile of v4, /device:TPU:0, one launch (start us, length us, event | category | flops | bytes accessed | tf_op | source)
XLA Modules:
  0.0 42.7 jit_solution(443030736567563762)
XLA Ops:
  0.6 0.0 copy-start
  0.6 0.0 copy-start.1
  0.7 1.1 %norm.1 = (bf16[4,3200]{1,0:T(4,128)(2,1)S(1)}, bf16[24,1024]{1,0:T(8,128)(2,1)S(1)}) custom-call(bf16[3,3200]{1,0:T(4,128)(2,1)} %feats.1, f32[3200]{0:T(1024)} %gain.1, f32[3200]{0:T(1024)} %shift.1, bf16[24,1024]{1,0:T(8,128)(2,1)} %cotangent.1), custom_call_target="tpu_custom_call" | custom-call | tf_op jit(solution)/shard_map/norm/pallas_call | solution.py:179
  1.8 4.1 %collective-permute-start = (bf16[4,3200]{1,0:T(4,128)(2,1)S(1)}, bf16[4,3200]{1,0:T(4,128)(2,1)S(1)}, u32[]{:S(2)}, u32[]{:S(2)}) collective-permute-start(bf16[4,3200]{1,0:T(4,128)(2,1)S(1)} %get-tuple-element.10), channel_id=1, source_target_pairs={{0,16},{8,24},{16,0},{24,8},{1,17},{9,25},{17,1},{25,9},{2,18},{10... | collective-permute-start | bytes 76808 | tf_op jit(solution)/shard_map/ppermute | solution.py:193
  5.9 0.1 collective-permute-start.2
  5.9 0.9 %convert_reduce_fusion.1 = f32[3]{0:T(128)S(1)} fusion(bf16[3,3200]{1,0:T(4,128)(2,1)} %feats.1), kind=kLoop, calls=%fused_computation.5 | loop fusion | flops 19197 | bytes 19212 | tf_op jit(solution)/shard_map/reduce_sum | solution.py:35
  6.8 0.9 %fusion.8 = f32[3]{0:T(128)S(1)} fusion(bf16[3,3200]{1,0:T(4,128)(2,1)} %feats.1, f32[3]{0:T(128)S(1)} %broadcast_multiply_fusion.2), kind=kLoop, calls=%fused_computation.14 | loop fusion | flops 38397 | bytes 19224 | tf_op jit(solution)/shard_map/reduce_sum | solution.py:37
  7.8 0.0 collective-permute-done
  7.8 1.9 %collective-permute-start.1 = (bf16[8,3200]{1,0:T(8,128)(2,1)S(1)}, bf16[8,3200]{1,0:T(8,128)(2,1)S(1)}, u32[]{:S(2)}, u32[]{:S(2)}) collective-permute-start(bf16[8,3200]{1,0:T(8,128)(2,1)S(1)} %pad_maximum_fusion.3), channel_id=1, source_target_pairs={{0,8},{8,0},{16,24},{24,16},{1,9},{9,1},{17,25},{25,17},{2,10},{10... | collective-permute-start | bytes 153608 | tf_op jit(solution)/shard_map/ppermute | solution.py:193
  9.7 1.4 %collective-permute-done.2 = bf16[24,1024]{1,0:T(8,128)(2,1)S(1)} collective-permute-done((bf16[24,1024]{1,0:T(8,128)(2,1)S(1)}, bf16[24,1024]{1,0:T(8,128)(2,1)S(1)}, u32[]{:S(2)}, u32[]{:S(2)}) %collective-permute-start.2) | collective-permute-done | bytes 49184 | tf_op jit(solution)/shard_map/ppermute | solution.py:194
  11.1 1.4 %collective-permute-start.3 = (bf16[48,1024]{1,0:T(8,128)(2,1)S(1)}, bf16[48,1024]{1,0:T(8,128)(2,1)S(1)}, u32[]{:S(2)}, u32[]{:S(2)}) collective-permute-start(bf16[48,1024]{1,0:T(8,128)(2,1)S(1)} %pad_maximum_fusion.2), channel_id=1, source_target_pairs={{0,8},{8,0},{16,24},{24,16},{1,9},{9,1},{17,25},{25,17},{2,10},{10... | collective-permute-start | bytes 294920 | tf_op jit(solution)/shard_map/ppermute | solution.py:194
  12.5 0.0 collective-permute-done.1
  12.6 10.7 %all_gather.3.rows = bf16[128,3200]{1,0:T(8,128)(2,1)S(1)} all-gather(bf16[16,3200]{1,0:T(8,128)(2,1)S(1)} %pad_maximum_fusion.1), channel_id=1, replica_groups=mesh['grp'=4,'dev'=8] {'dev'}, dimensions={0}, use_global_device_ids=true | all-gather | bytes 921600 | tf_op jit(solution)/shard_map/all_gather | solution.py:196
  23.3 0.0 collective-permute-done.3
  23.3 7.9 %fused.1 = (bf16[24,1024]{1,0:T(8,128)(2,1)}, f32[1,1024]{1,0:T(1,128)}, bf16[128,1024]{1,0:T(8,128)(2,1)S(1)}, bf16[32,3200]{1,0:T(8,128)(2,1)S(1)}) custom-call(s32[1]{0:T(128)} %bitcast.place, s32[32]{0:T(128)} %img_seq.1, s32[32]{0:T(128)} %img_count.1, s32[32]{0:T(128)} %img_offset.1, bf16[128,3200]{1,0:T(8,128)(2,1)S(1)} %all_gather.3.rows, ...), custom_call_target="tpu_custom_call" | custom-call | tf_op jit(solution)/shard_map/fused/pallas_call | solution.py:198
  31.3 0.7 %reshape.32 = bf16[8,4,3200]{2,1,0:T(4,128)(2,1)} reshape(bf16[32,3200]{1,0:T(8,128)(2,1)S(1)} %get-tuple-element.13) | data formatting | bytes 409600 | tf_op jit(solution)/shard_map/reshape | solution.py:216
  32.0 3.4 %all-to-all-start = ((bf16[8,4,3200]{2,1,0:T(4,128)(2,1)}), bf16[8,4,3200]{2,1,0:T(4,128)(2,1)S(1)}, u32[]{:S(2)}, u32[]{:S(2)}) async-start(bf16[8,4,3200]{2,1,0:T(4,128)(2,1)} %reshape.32), calls=%async_computation | async-start | bytes 409600 | tf_op jit(solution)/shard_map/all_to_all | solution.py:216
  35.4 5.2 %grad_weight.1 = f32[3200,1024]{1,0:T(8,128)} custom-call(bf16[128,3200]{1,0:T(8,128)(2,1)S(1)} %all_gather.3.rows, bf16[128,1024]{1,0:T(8,128)(2,1)S(1)} %get-tuple-element.14.grad_pre), custom_call_target="tpu_custom_call" | custom-call | flops 838860800 | bytes 13107200 | tf_op jit(solution)/shard_map/grad_weight/pallas_call | solution.py:218
  40.6 1.1 %all-to-all-done = bf16[8,4,3200]{2,1,0:T(4,128)(2,1)S(1)} async-done(((bf16[8,4,3200]{2,1,0:T(4,128)(2,1)}), bf16[8,4,3200]{2,1,0:T(4,128)(2,1)S(1)}, u32[]{:S(2)}, u32[]{:S(2)}) %all-to-all-start) | async-done | bytes 204832 | tf_op jit(solution)/shard_map/all_to_all | solution.py:216
  41.6 0.1 convert_reduce_fusion
  41.7 0.0 copy-done
  41.7 0.0 copy-done.1
  41.8 0.2 fusion.9
  42.0 0.7 %fusion.7 = bf16[3,3200]{1,0:T(4,128)(2,1)} fusion(bf16[3,3200]{1,0:T(4,128)(2,1)S(1)} %copy-done, f32[4,3200]{1,0:T(4,128)S(1)} %convert_reduce_fusion, f32[3]{0:T(128)S(1)} %get-tuple-element.18, f32[3]{0:T(128)S(1)} %get-tuple-element.19, f32[3200]{0:T(1024)S(1)} %copy-done.1, f32[3]{0:T(128)S(1)} %add_rsqrt_fusion, f32[3]{0:T(128)S(1)} %broadcast_multiply_fusion.2), kind=kLoop, calls=%fused_computation.13 | loop fusion | flops 86400 | bytes 89648 | tf_op jit(solution)/shard_map/convert_element_type | solution.py:59
  (7 shorter events, 0.1 us)
Async XLA Ops:
  0.6 41.1 %copy-start = (bf16[3,3200]{1,0:T(4,128)(2,1)S(1)}, bf16[3,3200]{1,0:T(4,128)(2,1)}, u32[]{:S(2)}) copy-start(bf16[3,3200]{1,0:T(4,128)(2,1)} %feats.1) | copy-start | bytes 57604
  0.6 41.1 %copy-start.1 = (f32[3200]{0:T(1024)S(1)}, f32[3200]{0:T(1024)}, u32[]{:S(2)}) copy-start(f32[3200]{0:T(1024)} %gain.1) | copy-start | bytes 38404
  1.8 6.0 %collective-permute-start = (bf16[4,3200]{1,0:T(4,128)(2,1)S(1)}, bf16[4,3200]{1,0:T(4,128)(2,1)S(1)}, u32[]{:S(2)}, u32[]{:S(2)}) collective-permute-start(bf16[4,3200]{1,0:T(4,128)(2,1)S(1)} %get-tuple-element.10), channel_id=1, source_target_pairs={{0,16},{8,24},{16,0},{24,8},{1,17},{9,25},{17,1},{25,9},{2,18},{10... | collective-permute-start | bytes 76808 | tf_op jit(solution)/shard_map/ppermute | solution.py:193
  5.9 5.2 %collective-permute-start.2 = (bf16[24,1024]{1,0:T(8,128)(2,1)S(1)}, bf16[24,1024]{1,0:T(8,128)(2,1)S(1)}, u32[]{:S(2)}, u32[]{:S(2)}) collective-permute-start(bf16[24,1024]{1,0:T(8,128)(2,1)S(1)} %get-tuple-element.11), channel_id=1, source_target_pairs={{0,16},{8,24},{16,0},{24,8},{1,17},{9,25},{17,1},{25,9},{2,18},{10... | collective-permute-start | bytes 147464 | tf_op jit(solution)/shard_map/ppermute | solution.py:194
  7.8 4.7 %collective-permute-start.1 = (bf16[8,3200]{1,0:T(8,128)(2,1)S(1)}, bf16[8,3200]{1,0:T(8,128)(2,1)S(1)}, u32[]{:S(2)}, u32[]{:S(2)}) collective-permute-start(bf16[8,3200]{1,0:T(8,128)(2,1)S(1)} %pad_maximum_fusion.3), channel_id=1, source_target_pairs={{0,8},{8,0},{16,24},{24,16},{1,9},{9,1},{17,25},{25,17},{2,10},{10... | collective-permute-start | bytes 153608 | tf_op jit(solution)/shard_map/ppermute | solution.py:193
  11.1 12.2 %collective-permute-start.3 = (bf16[48,1024]{1,0:T(8,128)(2,1)S(1)}, bf16[48,1024]{1,0:T(8,128)(2,1)S(1)}, u32[]{:S(2)}, u32[]{:S(2)}) collective-permute-start(bf16[48,1024]{1,0:T(8,128)(2,1)S(1)} %pad_maximum_fusion.2), channel_id=1, source_target_pairs={{0,8},{8,0},{16,24},{24,16},{1,9},{9,1},{17,25},{25,17},{2,10},{10... | collective-permute-start | bytes 294920 | tf_op jit(solution)/shard_map/ppermute | solution.py:194
  32.0 9.7 %all-to-all-start = ((bf16[8,4,3200]{2,1,0:T(4,128)(2,1)}), bf16[8,4,3200]{2,1,0:T(4,128)(2,1)S(1)}, u32[]{:S(2)}, u32[]{:S(2)}) async-start(bf16[8,4,3200]{2,1,0:T(4,128)(2,1)} %reshape.32), calls=%async_computation | async-start | bytes 409600 | tf_op jit(solution)/shard_map/all_to_all | solution.py:216

commit v5 on v4

--- a/solution.py
+++ b/solution.py
@@ -59,13 +59,16 @@
     return grad_feats.astype(jnp.bfloat16)
 
 
-def norm_kernel(feats, gain, shift, cotangent, normed, grads):
-    rows = normalize(feats[...], gain[...][None], shift[...][None])[2]
+def norm_kernel(feats, gain, shift, cotangent, normed, grads, unit, scale, gain_near):
+    unit_rows, inv_scale, rows = normalize(feats[...], gain[...][None], shift[...][None])
     empty = normed.shape[0] - rows.shape[0]
     if empty:
         rows = jnp.concatenate([rows, jnp.zeros((empty, rows.shape[1]), jnp.float32)], axis=0)
     normed[...] = rows.astype(jnp.bfloat16)
     grads[...] = cotangent[...]
+    unit[...] = unit_rows
+    scale[...] = jnp.broadcast_to(inv_scale, scale.shape)
+    gain_near[...] = gain[...][None]
 
 
 def distance_of(place, groups):
@@ -97,58 +100,71 @@
     return jnp.where(within < own_rows, target, -1)
 
 
-def fused_kernel(
-    block, own_rows, lanes, groups, width,
-    place, img_seq, img_count, img_offset, rows, grads, bias, w_far,
-    projected, grad_bias, grad_pre, terms, w_near, total, arrived,
+def fetch_kernel(first, w_far, after, near, arrived):
+    del after
+    copy = pltpu.make_async_copy(w_far.at[pl.ds(first, near.shape[0])], near, arrived)
+    copy.start()
+    copy.wait()
+
+
+def fetch_and_route_kernel(
+    first, block, own_rows, lanes, groups,
+    place, img_seq, img_count, img_offset, bias_far, w_far, after,
+    near, bias, sources, own_sources, arrivals, arrived,
 ):
-    units = w_far.shape[1]
-    steps = units // width
-    copies = [
-        pltpu.make_async_copy(w_far.at[:, pl.ds(step * width, width)], w_near.at[step], arrived.at[step])
-        for step in range(steps)
-    ]
-    for copy in copies:
-        copy.start()
+    del after
+    copy = pltpu.make_async_copy(w_far.at[pl.ds(first, near.shape[0])], near, arrived)
+    copy.start()
+    bias[...] = bias_far[...]
     group_rows = own_rows * lanes
-    all_rows = group_rows * groups
     slot_count = lanes * groups * block
     my_group = place[0]
     target = slot_targets(my_group, block, own_rows, lanes, groups, img_seq, img_count, img_offset)
-    places = lax.broadcasted_iota(jnp.int32, (all_rows, slot_count), 0)
+    places = lax.broadcasted_iota(jnp.int32, (group_rows * groups, slot_count), 0)
     held = places // group_rows
     seq_rows = places - held * group_rows + (my_group ^ distance_of(held, groups)) * group_rows
     routes = (target == seq_rows).astype(jnp.float32)
-    arrivals = routes[:group_rows].astype(jnp.bfloat16)
-    sources = routes.T.astype(jnp.bfloat16)
-    own_place = lax.broadcasted_iota(jnp.int32, (lanes * block, slot_count), 0)
-    own_slot = lax.broadcasted_iota(jnp.int32, (lanes * block, slot_count), 1)
-    keep = own_slot == own_place // block * (block * groups) + (own_place & (block - 1))
-    keep = keep.astype(jnp.float32).astype(jnp.bfloat16)
-    for step in range(steps):
-        copies[step].wait()
-        span = slice(step * width, (step + 1) * width)
-        weights = w_near[step]
-        pre_act = jnp.dot(rows[...], weights, preferred_element_type=jnp.float32) + bias[:, span]
-        acted, slope = gelu_and_slope(pre_act)
-        projected[:, span] = jnp.dot(
-            arrivals, acted.astype(jnp.bfloat16), preferred_element_type=jnp.float32
-        ).astype(jnp.bfloat16)
-        upstream = jnp.dot(sources, grads[:, span], preferred_element_type=jnp.float32)
-        pulled = (upstream * slope).astype(jnp.bfloat16)
-        grad_pre[:, span] = pulled
-        grad_bias[:, span] = jnp.sum(pulled.astype(jnp.float32), axis=0, keepdims=True)
-        own = jnp.dot(keep, pulled, preferred_element_type=jnp.float32).astype(jnp.bfloat16)
-        term = lax.dot_general(own, weights, (((1,), (1,)), ((), ())), preferred_element_type=jnp.float32)
-        if step:
-            term = total[...] + term
-        if step + 1 < steps:
-            total[...] = term
-        else:
-            terms[...] = term.astype(jnp.bfloat16)
-
-
-def grad_weight_kernel(height, rows, grad_pre, far, near, left):
+    arrivals[...] = routes[:group_rows].astype(jnp.bfloat16)
+    turned = routes.T
+    sources[...] = turned.astype(jnp.bfloat16)
+    own_sources[...] = own_slots(turned, block, lanes, groups).astype(jnp.bfloat16)
+    copy.wait()
+
+
+def own_slots(rows, block, lanes, groups):
+    stride = block * groups
+    return jnp.concatenate([rows[lane * stride : lane * stride + block] for lane in range(lanes)], axis=0)
+
+
+def terms_kernel(block, lanes, groups, rows, grads, bias, own_sources, *refs):
+    parts, (pre_act, terms) = refs[:-2], refs[-2:]
+    total, first = bias[...], 0
+    for part in parts:
+        total = total + jnp.dot(
+            rows[:, first : first + part.shape[0]], part[...], preferred_element_type=jnp.float32
+        )
+        first += part.shape[0]
+    pre_act[...] = total
+    slope = gelu_and_slope(own_slots(total, block, lanes, groups))[1]
+    upstream = jnp.dot(own_sources[...], grads[...], preferred_element_type=jnp.float32)
+    own = (upstream * slope).astype(jnp.bfloat16)
+    first = 0
+    for part in parts:
+        term = lax.dot_general(own, part[...], (((1,), (1,)), ((), ())), preferred_element_type=jnp.float32)
+        for lane in range(lanes):
+            terms[lane, :, first : first + part.shape[0]] = term[
+                lane * block : (lane + 1) * block
+            ].astype(jnp.bfloat16)
+        first += part.shape[0]
+
+
+def grad_weight_kernel(
+    height, rows, grads, pre_act, sources, arrivals, projected, grad_bias, far, grad_pre, near, left
+):
+    acted, slope = gelu_and_slope(pre_act[...])
+    upstream = jnp.dot(sources[...], grads[...], preferred_element_type=jnp.float32)
+    pulled = (upstream * slope).astype(jnp.bfloat16)
+    grad_pre[...] = pulled
     copies = []
     for step in range(rows.shape[1] // height):
         span = slice(step * height, (step + 1) * height)
@@ -157,12 +173,36 @@
         )
         copies.append(pltpu.make_async_copy(near.at[span], far.at[span], left.at[step]))
         copies[-1].start()
+    projected[...] = jnp.dot(
+        arrivals[...], acted.astype(jnp.bfloat16), preferred_element_type=jnp.float32
+    ).astype(jnp.bfloat16)
+    grad_bias[...] = jnp.sum(pulled.astype(jnp.float32), axis=0, keepdims=True)
     for copy in copies:
         copy.wait()
 
 
+def finish_kernel(swapped, gain, unit, scale, grad_feats):
+    total = swapped[0].astype(jnp.float32)
+    for lane in range(1, swapped.shape[0]):
+        total = total + swapped[lane].astype(jnp.float32)
+    grad_feats[...] = backward_norm(total[: unit.shape[0]], gain[...], unit[...], scale[:, :1])
+
+
 def in_hbm(*arrays):
     return [pltpu.with_memory_space_constraint(array, pltpu.HBM) for array in arrays]
+
+
+def near_call(kernel, name, outs, in_specs, operands, scratch=(), out_specs=None, moved=0, limit=24):
+    return pl.pallas_call(
+        kernel,
+        out_shape=outs,
+        in_specs=in_specs,
+        out_specs=out_specs or (WHOLE,) * len(outs),
+        scratch_shapes=list(scratch),
+        compiler_params=pltpu.CompilerParams(vmem_limit_bytes=limit * MIB),
+        cost_estimate=pl.CostEstimate(flops=0, bytes_accessed=moved, transcendentals=0),
+        name=name,
+    )(*operands)
 
 
 def gathered_plan(feats, ln_gain, ln_shift, w_proj, b_proj, cotangent, img_seq, img_count, img_offset):
@@ -175,64 +215,95 @@
     all_rows = group_rows * groups
     block = pl.next_power_of_2(own_rows)
     slot_count = lanes * groups * block
-    bfloat16, float32 = jnp.bfloat16, jnp.float32
-    column, grads = pl.pallas_call(
+    half = vis_width // 256 * 128
+    shape, bfloat16, float32 = jax.ShapeDtypeStruct, jnp.bfloat16, jnp.float32
+    w_far, bias_far = in_hbm(w_proj, b_proj[None])
+
+    def exchange(held, step):
+        pairs = [(group, group ^ step) for group in range(groups)]
+        return jnp.concatenate([held, lax.ppermute(held, "grp", pairs)], axis=0)
+
+    column, grads, unit, scale, gain = near_call(
         norm_kernel,
-        out_shape=(
-            jax.ShapeDtypeStruct((block, vis_width), bfloat16),
-            jax.ShapeDtypeStruct(cotangent.shape, bfloat16),
+        "norm",
+        (
+            shape((block, vis_width), bfloat16),
+            shape(cotangent.shape, bfloat16),
+            shape(feats.shape, float32),
+            shape((own_rows, 128), float32),
+            shape((1, vis_width), float32),
         ),
-        in_specs=[WHOLE] * 4,
-        out_specs=(WHOLE, WHOLE),
-        compiler_params=pltpu.CompilerParams(vmem_limit_bytes=8 * MIB),
-        name="norm",
-    )(*in_hbm(feats, ln_gain, ln_shift, cotangent))
+        [WHOLE] * 4,
+        in_hbm(feats, ln_gain, ln_shift, cotangent),
+        limit=8,
+    )
+    (w_low,) = near_call(
+        functools.partial(fetch_kernel, 0),
+        "fetch",
+        (shape((half, units), bfloat16),),
+        [LEFT, LEFT],
+        (w_far, column),
+        [pltpu.SemaphoreType.DMA],
+        moved=2 * half * units,
+    )
     step = groups // 2
     while step:
-        pairs = [(group, group ^ step) for group in range(groups)]
-        column = jnp.concatenate([column, lax.ppermute(column, "grp", pairs)], axis=0)
-        grads = jnp.concatenate([grads, lax.ppermute(grads, "grp", pairs)], axis=0)
+        column, grads = exchange(column, step), exchange(grads, step)
+        if step == groups // 2:
+            later = column
         step //= 2
+    w_high, bias, sources, own_sources, arrivals = near_call(
+        functools.partial(fetch_and_route_kernel, half, block, own_rows, lanes, groups),
+        "fetch_and_route",
+        (
+            shape((vis_width - half, units), bfloat16),
+            shape((1, units), float32),
+            shape((slot_count, all_rows), bfloat16),
+            shape((lanes * block, all_rows), bfloat16),
+            shape((group_rows, slot_count), bfloat16),
+        ),
+        [SCALARS] * 4 + [WHOLE, LEFT, LEFT],
+        (my_group[None], *in_hbm(img_seq, img_count, img_offset), bias_far, w_far, later),
+        [pltpu.SemaphoreType.DMA],
+        moved=2 * (vis_width - half) * units,
+    )
     rows = lax.all_gather(column, "dev", axis=0, tiled=True)
-    width = 256 if units % 256 == 0 else units
-    projected, grad_bias, grad_pre, terms = pl.pallas_call(
-        functools.partial(fused_kernel, block, own_rows, lanes, groups, width),
-        out_shape=(
-            jax.ShapeDtypeStruct((group_rows, units), bfloat16),
-            jax.ShapeDtypeStruct((1, units), float32),
-            jax.ShapeDtypeStruct((slot_count, units), bfloat16),
-            jax.ShapeDtypeStruct((lanes * block, vis_width), bfloat16),
+    pre_act, terms = near_call(
+        functools.partial(terms_kernel, block, lanes, groups),
+        "terms",
+        (shape((slot_count, units), float32), shape((lanes, block, vis_width), bfloat16)),
+        [WHOLE] * 6,
+        (rows, grads, bias, own_sources, w_low, w_high),
+        moved=4 * vis_width * units,
+    )
+    swapped = lax.all_to_all(terms, "dev", 0, 0)
+    height = 128 if vis_width % 128 == 0 else vis_width
+    projected, grad_bias, grad_weight = near_call(
+        functools.partial(grad_weight_kernel, height),
+        "grad_weight",
+        (
+            shape((group_rows, units), bfloat16),
+            shape((1, units), float32),
+            shape((vis_width, units), float32),
         ),
-        in_specs=[SCALARS] * 4 + [WHOLE] * 3 + [LEFT],
-        out_specs=(WHOLE,) * 4,
-        scratch_shapes=[
-            pltpu.VMEM((units // width, vis_width, width), bfloat16),
-            pltpu.VMEM((lanes * block, vis_width), float32),
-            pltpu.SemaphoreType.DMA((units // width,)),
-        ],
-        compiler_params=pltpu.CompilerParams(vmem_limit_bytes=24 * MIB),
-        name="fused",
-    )(my_group[None], *in_hbm(img_seq, img_count, img_offset), rows, grads, *in_hbm(b_proj[None], w_proj))
-    swapped = lax.all_to_all(terms.reshape(lanes, block, vis_width), "dev", 0, 0)
-    height = 128 if vis_width % 128 == 0 else vis_width
-    grad_weight = pl.pallas_call(
-        functools.partial(grad_weight_kernel, height),
-        out_shape=jax.ShapeDtypeStruct((vis_width, units), float32),
-        in_specs=[WHOLE] * 2,
-        out_specs=LEFT,
-        scratch_shapes=[
+        [WHOLE] * 5,
+        (rows, grads, pre_act, sources, arrivals),
+        [
+            pltpu.VMEM((slot_count, units), bfloat16),
             pltpu.VMEM((vis_width, units), float32),
             pltpu.SemaphoreType.DMA((vis_width // height,)),
         ],
-        compiler_params=pltpu.CompilerParams(vmem_limit_bytes=24 * MIB),
-        cost_estimate=pl.CostEstimate(
-            flops=2 * slot_count * vis_width * units, bytes_accessed=4 * vis_width * units, transcendentals=0
-        ),
-        name="grad_weight",
-    )(rows, grad_pre)
-    grad_normed = jnp.sum(swapped.astype(float32), axis=0)[:own_rows]
-    unit_rows, inv_scale, _ = normalize(feats, ln_gain, ln_shift)
-    grad_feats = backward_norm(grad_normed, ln_gain, unit_rows, inv_scale)
+        (WHOLE, WHOLE, LEFT),
+        moved=4 * vis_width * units,
+    )
+    (grad_feats,) = near_call(
+        finish_kernel,
+        "finish",
+        (shape(feats.shape, bfloat16),),
+        [WHOLE] * 4,
+        (swapped, gain, unit, scale),
+        limit=8,
+    )
     return (projected, grad_feats, grad_weight, grad_bias[0])
 
 

time: 43.1 us -> 38.3 us (0.89)
  other arithmetic: 2.96 us -> 0.09 us
  waiting for transfers between devices: 2.44 us -> 0.12 us
  Pallas kernels: 14.2 us -> 16.4 us
  starting transfers between devices: 10.9 us -> 9.73 us
  local copies, waits for them, and re-layouts: 0.74 us -> 0.02 us
    pallas_call x3 -> x6, Pallas kernels: 14.2 us -> 16.4 us  [near_call(): pl.pallas_call(kernel, out_shape=outs, in_specs=in_specs, out_specs=out_s...]
    reduce_sum x4 -> x0, other arithmetic: 2.13 us -> none  [the longest x1 0.95 us: normalize(): jnp.mean(centered * centered, axis=1, keepdims=True) + epsilon]
    ppermute x4, waiting for transfers between devices: 1.37 us -> 0.01 us  [exchange(): return jnp.concatenate([held, lax.ppermute(held, 'grp', pairs)], axis=0)]
    ppermute x4, starting transfers between devices: 7.49 us -> 6.34 us  [exchange(): return jnp.concatenate([held, lax.ppermute(held, 'grp', pairs)], axis=0)]
    all_to_all x1, waiting for transfers between devices: 1.07 us -> 0.1 us  [gathered_plan(): swapped = lax.all_to_all(terms, 'dev', 0, 0)]
    reshape x1 -> x0, local copies, waits for them, and re-layouts: 0.73 us -> none  [gathered_plan(): terms.reshape(lanes, block, vis_width)]
    convert_element_type x1 -> x0, other arithmetic: 0.71 us -> none  [backward_norm(): return grad_feats.astype(jnp.bfloat16)]
  transfers between devices with their start and end apart: 5 -> 5, of which waited for: 2 -> 1; matrix products, arithmetic and copies ran while one was open for 5% -> 0% of each run, Pallas kernels for 12% -> 28%
where the time goes in v5:
time: 38.3 us; the launch traced here: 37.9 us
  Pallas kernels  16.4 us (43%)
  blocking collectives  10.8 us (28%)
  starting transfers between devices  9.73 us (25%)
  between operations  0.72 us (2%)
    pallas_call x6, Pallas kernels, near_call(): pl.pallas_call(kernel, out_shape=outs, in_specs=in_specs, out_specs=out_s...  16.4 us
    all_gather x1, blocking collectives, gathered_plan(): rows = lax.all_gather(column, 'dev', axis=0, tiled=True)  10.8 us
    ppermute x4, starting transfers between devices, exchange(): return jnp.concatenate([held, lax.ppermute(held, 'grp', pairs)], axis=0)  6.34 us
    all_to_all x1, starting transfers between devices, gathered_plan(): swapped = lax.all_to_all(terms, 'dev', 0, 0)  3.39 us
  transfers between devices with their start and end apart: 5, of which 1 were waited for; matrix products, arithmetic and copies ran while one was open for 0% of the time, Pallas kernels for 28%

profile of v5, /device:TPU:0, one launch (start us, length us, event | category | flops | bytes accessed | tf_op | source)
XLA Modules:
  0.0 37.9 jit_solution(3627065211738398548)
XLA Ops:
  0.6 1.1 %norm.1 = (bf16[4,3200]{1,0:T(4,128)(2,1)S(1)}, bf16[24,1024]{1,0:T(8,128)(2,1)S(1)}, f32[3,3200]{1,0:T(4,128)S(1)}, f32[3,128]{1,0:T(4,128)S(1)}, f32[1,3200]{1,0:T(1,128)S(1)}) custom-call(bf16[3,3200]{1,0:T(4,128)(2,1)} %feats.1, f32[3200]{0:T(1024)} %gain.1, f32[3200]{0:T(1024)} %shift.1, bf16[24,1024]{1,0:T(8,128)(2,1)} %cotangent.1), custom_call_target="tpu_custom_call" | custom-call | tf_op jit(solution)/shard_map/norm/pallas_call | solution.py:196
  1.7 4.1 %collective-permute-start = (bf16[4,3200]{1,0:T(4,128)(2,1)S(1)}, bf16[4,3200]{1,0:T(4,128)(2,1)S(1)}, u32[]{:S(2)}, u32[]{:S(2)}) collective-permute-start(bf16[4,3200]{1,0:T(4,128)(2,1)S(1)} %get-tuple-element.19.after), channel_id=1, source_target_pairs={{0,16},{8,24},{16,0},{24,8},{1,17},{9,25},{17,1},{25,9},{2,18},{10... | collective-permute-start | bytes 76808 | tf_op jit(solution)/shard_map/ppermute | solution.py:224
  5.8 0.1 collective-permute-start.2
  5.9 1.9 %fetch.1.refs_0_ = bf16[1536,1024]{1,0:T(8,128)(2,1)S(1)} custom-call(bf16[3200,1024]{1,0:T(8,128)(2,1)} %w_far.3, bf16[4,3200]{1,0:T(4,128)(2,1)S(1)} %get-tuple-element.19.after), custom_call_target="tpu_custom_call" | custom-call | bytes 3145728 | tf_op jit(solution)/shard_map/fetch/pallas_call | solution.py:196
  7.8 0.0 collective-permute-done
  7.9 1.9 %collective-permute-start.1 = (bf16[8,3200]{1,0:T(8,128)(2,1)S(1)}, bf16[8,3200]{1,0:T(8,128)(2,1)S(1)}, u32[]{:S(2)}, u32[]{:S(2)}) collective-permute-start(bf16[8,3200]{1,0:T(8,128)(2,1)S(1)} %pad_maximum_fusion.2.after), channel_id=1, source_target_pairs={{0,8},{8,0},{16,24},{24,16},{1,9},{9,1},{17,25},{25,17},{2,10},{10... | collective-permute-start | bytes 153608 | tf_op jit(solution)/shard_map/ppermute | solution.py:224
  9.8 2.7 %fetch_and_route.1 = (bf16[1664,1024]{1,0:T(8,128)(2,1)S(1)}, f32[1,1024]{1,0:T(1,128)S(1)}, bf16[128,96]{1,0:T(8,128)(2,1)S(1)}, bf16[32,96]{1,0:T(8,128)(2,1)S(1)}, bf16[24,128]{1,0:T(8,128)(2,1)S(1)}) custom-call(s32[1]{0:T(128)} %bitcast.place, s32[32]{0:T(128)} %img_seq.1, s32[32]{0:T(128)} %img_count.1, s32[32]{0:T(128)} %img_offset.1, ...), custom_call_target="tpu_custom_call" | custom-call | bytes 3407872 | tf_op jit(solution)/shard_map/fetch_and_route/pallas_call | solution.py:196
  12.5 0.0 collective-permute-done.2
  12.5 0.3 collective-permute-start.3
  12.8 0.0 collective-permute-done.1
  12.8 10.8 %all_gather.3.rows = bf16[128,3200]{1,0:T(8,128)(2,1)S(1)} all-gather(bf16[16,3200]{1,0:T(8,128)(2,1)S(1)} %pad_maximum_fusion), channel_id=1, replica_groups=mesh['grp'=4,'dev'=8] {'dev'}, dimensions={0}, use_global_device_ids=true | all-gather | bytes 921600 | tf_op jit(solution)/shard_map/all_gather | solution.py:270
  23.7 0.0 collective-permute-done.3
  23.7 3.8 %terms.1 = (f32[128,1024]{1,0:T(8,128)S(1)}, bf16[8,4,3200]{2,1,0:T(4,128)(2,1)}) custom-call(bf16[128,3200]{1,0:T(8,128)(2,1)S(1)} %all_gather.3.rows, bf16[96,1024]{1,0:T(8,128)(2,1)S(1)} %constant_dynamic-update-slice_fusion.grads, f32[1,1024]{1,0:T(1,128)S(1)} %get-tuple-element.21.bias, bf16[32,96]{1,0:T(8,128)(2,1)S(1)} %get-tuple-element.22.own_sources, ...), custom_call_target="tpu_custom_call" | custom-call | bytes 13107200 | tf_op jit(solution)/shard_map/terms/pallas_call | solution.py:196
  27.5 3.4 %all-to-all-start = ((bf16[8,4,3200]{2,1,0:T(4,128)(2,1)}), bf16[8,4,3200]{2,1,0:T(4,128)(2,1)S(1)}, u32[]{:S(2)}, u32[]{:S(2)}) async-start(bf16[8,4,3200]{2,1,0:T(4,128)(2,1)} %get-tuple-element.28), calls=%async_computation | async-start | bytes 409600 | tf_op jit(solution)/shard_map/all_to_all | solution.py:279
  30.9 6.1 %grad_weight.1 = (bf16[24,1024]{1,0:T(8,128)(2,1)}, f32[1,1024]{1,0:T(1,128)}, f32[3200,1024]{1,0:T(8,128)}) custom-call(bf16[128,3200]{1,0:T(8,128)(2,1)S(1)} %all_gather.3.rows, bf16[96,1024]{1,0:T(8,128)(2,1)S(1)} %constant_dynamic-update-slice_fusion.grads, f32[128,1024]{1,0:T(8,128)S(1)} %get-tuple-element.24.pre_act, ...), custom_call_target="tpu_custom_call" | custom-call | bytes 13107200 | tf_op jit(solution)/shard_map/grad_weight/pallas_call | solution.py:196
  37.0 0.1 all-to-all-done.swapped
  37.1 0.8 %finish.1 = bf16[3,3200]{1,0:T(4,128)(2,1)} custom-call(bf16[8,4,3200]{2,1,0:T(4,128)(2,1)S(1)} %all-to-all-done.swapped, f32[1,3200]{1,0:T(1,128)S(1)} %get-tuple-element.29.gain, f32[3,3200]{1,0:T(4,128)S(1)} %get-tuple-element.30.unit, f32[3,128]{1,0:T(4,128)S(1)} %get-tuple-element.31.scale), custom_call_target="tpu_custom_call" | custom-call | tf_op jit(solution)/shard_map/finish/pallas_call | solution.py:196
  (6 shorter events, 0.1 us)
Async XLA Ops:
  1.7 6.1 %collective-permute-start = (bf16[4,3200]{1,0:T(4,128)(2,1)S(1)}, bf16[4,3200]{1,0:T(4,128)(2,1)S(1)}, u32[]{:S(2)}, u32[]{:S(2)}) collective-permute-start(bf16[4,3200]{1,0:T(4,128)(2,1)S(1)} %get-tuple-element.19.after), channel_id=1, source_target_pairs={{0,16},{8,24},{16,0},{24,8},{1,17},{9,25},{17,1},{25,9},{2,18},{10... | collective-permute-start | bytes 76808 | tf_op jit(solution)/shard_map/ppermute | solution.py:224
  5.8 6.7 %collective-permute-start.2 = (bf16[24,1024]{1,0:T(8,128)(2,1)S(1)}, bf16[24,1024]{1,0:T(8,128)(2,1)S(1)}, u32[]{:S(2)}, u32[]{:S(2)}) collective-permute-start(bf16[24,1024]{1,0:T(8,128)(2,1)S(1)} %get-tuple-element.20), channel_id=1, source_target_pairs={{0,16},{8,24},{16,0},{24,8},{1,17},{9,25},{17,1},{25,9},{2,18},{10... | collective-permute-start | bytes 147464 | tf_op jit(solution)/shard_map/ppermute | solution.py:224
  7.9 4.9 %collective-permute-start.1 = (bf16[8,3200]{1,0:T(8,128)(2,1)S(1)}, bf16[8,3200]{1,0:T(8,128)(2,1)S(1)}, u32[]{:S(2)}, u32[]{:S(2)}) collective-permute-start(bf16[8,3200]{1,0:T(8,128)(2,1)S(1)} %pad_maximum_fusion.2.after), channel_id=1, source_target_pairs={{0,8},{8,0},{16,24},{24,16},{1,9},{9,1},{17,25},{25,17},{2,10},{10... | collective-permute-start | bytes 153608 | tf_op jit(solution)/shard_map/ppermute | solution.py:224
  12.5 11.2 %collective-permute-start.3 = (bf16[48,1024]{1,0:T(8,128)(2,1)S(1)}, bf16[48,1024]{1,0:T(8,128)(2,1)S(1)}, u32[]{:S(2)}, u32[]{:S(2)}) collective-permute-start(bf16[48,1024]{1,0:T(8,128)(2,1)S(1)} %pad_maximum_fusion.1), channel_id=1, source_target_pairs={{0,8},{8,0},{16,24},{24,16},{1,9},{9,1},{17,25},{25,17},{2,10},{10... | collective-permute-start | bytes 294920 | tf_op jit(solution)/shard_map/ppermute | solution.py:224
  27.5 9.7 %all-to-all-start = ((bf16[8,4,3200]{2,1,0:T(4,128)(2,1)}), bf16[8,4,3200]{2,1,0:T(4,128)(2,1)S(1)}, u32[]{:S(2)}, u32[]{:S(2)}) async-start(bf16[8,4,3200]{2,1,0:T(4,128)(2,1)} %get-tuple-element.28), calls=%async_computation | async-start | bytes 409600 | tf_op jit(solution)/shard_map/all_to_all | solution.py:279

commit v6 on v5

--- a/solution.py
+++ b/solution.py
@@ -59,16 +59,20 @@
     return grad_feats.astype(jnp.bfloat16)
 
 
-def norm_kernel(feats, gain, shift, cotangent, normed, grads, unit, scale, gain_near):
-    unit_rows, inv_scale, rows = normalize(feats[...], gain[...][None], shift[...][None])
-    empty = normed.shape[0] - rows.shape[0]
-    if empty:
-        rows = jnp.concatenate([rows, jnp.zeros((empty, rows.shape[1]), jnp.float32)], axis=0)
-    normed[...] = rows.astype(jnp.bfloat16)
-    grads[...] = cotangent[...]
-    unit[...] = unit_rows
-    scale[...] = jnp.broadcast_to(inv_scale, scale.shape)
-    gain_near[...] = gain[...][None]
+def norm_kernel(*refs):
+    parts, gain, shift, (normed, unit, scale) = refs[:-5], refs[-5], refs[-4], refs[-3:]
+    blocks = [part[at] for part in parts for at in range(part.shape[0])]
+    block, own_rows = normed.shape[0] // len(blocks), unit.shape[0]
+    rows = []
+    for at, held in enumerate(blocks):
+        unit_rows, inv_scale, made = normalize(held, gain[...], shift[...])
+        rows.append(made)
+        if block > own_rows:
+            rows.append(jnp.zeros((block - own_rows, made.shape[1]), jnp.float32))
+        if at == 0:
+            unit[...] = unit_rows
+            scale[...] = jnp.broadcast_to(inv_scale, scale.shape)
+    normed[...] = jnp.concatenate(rows, axis=0).astype(jnp.bfloat16)
 
 
 def distance_of(place, groups):
@@ -100,22 +104,56 @@
     return jnp.where(within < own_rows, target, -1)
 
 
-def fetch_kernel(first, w_far, after, near, arrived):
-    del after
+def join_kernel(*refs):
+    parts, out, first = refs[:-1], refs[-1], 0
+    for part in parts:
+        out[first : first + part.shape[0]] = part[...]
+        first += part.shape[0]
+
+
+def fetch(first, w_far, near, arrived):
     copy = pltpu.make_async_copy(w_far.at[pl.ds(first, near.shape[0])], near, arrived)
     copy.start()
+    return copy
+
+
+def load_all(pairs, small):
+    loads = [pltpu.make_async_copy(far, close, small.at[at]) for at, (far, close) in enumerate(pairs)]
+    for load in loads:
+        load.start()
+    return loads
+
+
+def fetch_kernel(
+    first, place, w_far, feats_far, grads_far, gain_far, shift_far,
+    near, feats, grads, gain, shift, gain_line, shift_line, arrived, small,
+):
+    del place
+    copy = fetch(first, w_far, near, arrived)
+    pairs = ((feats_far, feats.at[0]), (grads_far, grads), (gain_far, gain_line), (shift_far, shift_line))
+    for load in load_all(pairs, small):
+        load.wait()
+    gain[...] = gain_line[...][None]
+    shift[...] = shift_line[...][None]
     copy.wait()
 
 
 def fetch_and_route_kernel(
     first, block, own_rows, lanes, groups,
-    place, img_seq, img_count, img_offset, bias_far, w_far, after,
-    near, bias, sources, own_sources, arrivals, arrived,
+    place, img_seq_far, img_count_far, img_offset_far, bias_far, w_far, after,
+    near, bias, sources, own_sources, arrivals,
+    img_seq, img_count, img_offset, arrived, small,
 ):
     del after
-    copy = pltpu.make_async_copy(w_far.at[pl.ds(first, near.shape[0])], near, arrived)
-    copy.start()
-    bias[...] = bias_far[...]
+    copy = fetch(first, w_far, near, arrived)
+    pairs = (
+        (img_seq_far, img_seq),
+        (img_count_far, img_count),
+        (img_offset_far, img_offset),
+        (bias_far, bias),
+    )
+    for load in load_all(pairs, small):
+        load.wait()
     group_rows = own_rows * lanes
     slot_count = lanes * groups * block
     my_group = place[0]
@@ -136,8 +174,8 @@
     return jnp.concatenate([rows[lane * stride : lane * stride + block] for lane in range(lanes)], axis=0)
 
 
-def terms_kernel(block, lanes, groups, rows, grads, bias, own_sources, *refs):
-    parts, (pre_act, terms) = refs[:-2], refs[-2:]
+def terms_kernel(block, lanes, groups, width, rows, grads, bias, own_sources, *refs):
+    parts, (pre_act, far, terms, left) = refs[:-4], refs[-4:]
     total, first = bias[...], 0
     for part in parts:
         total = total + jnp.dot(
@@ -148,14 +186,23 @@
     slope = gelu_and_slope(own_slots(total, block, lanes, groups))[1]
     upstream = jnp.dot(own_sources[...], grads[...], preferred_element_type=jnp.float32)
     own = (upstream * slope).astype(jnp.bfloat16)
-    first = 0
+    first, copies = 0, []
     for part in parts:
-        term = lax.dot_general(own, part[...], (((1,), (1,)), ((), ())), preferred_element_type=jnp.float32)
-        for lane in range(lanes):
-            terms[lane, :, first : first + part.shape[0]] = term[
-                lane * block : (lane + 1) * block
-            ].astype(jnp.bfloat16)
-        first += part.shape[0]
+        for start in range(0, part.shape[0], width):
+            size = min(width, part.shape[0] - start)
+            term = lax.dot_general(
+                own, part[start : start + size], (((1,), (1,)), ((), ())), preferred_element_type=jnp.float32
+            )
+            span = slice(first, first + size)
+            for lane in range(lanes):
+                terms[lane, :, span] = term[lane * block : (lane + 1) * block].astype(jnp.bfloat16)
+            copies.append(
+                pltpu.make_async_copy(terms.at[:, :, span], far.at[:, :, span], left.at[len(copies)])
+            )
+            copies[-1].start()
+            first += size
+    for copy in copies:
+        copy.wait()
 
 
 def grad_weight_kernel(
@@ -216,42 +263,51 @@
     block = pl.next_power_of_2(own_rows)
     slot_count = lanes * groups * block
     half = vis_width // 256 * 128
+    width = 896
     shape, bfloat16, float32 = jax.ShapeDtypeStruct, jnp.bfloat16, jnp.float32
-    w_far, bias_far = in_hbm(w_proj, b_proj[None])
-
-    def exchange(held, step):
-        pairs = [(group, group ^ step) for group in range(groups)]
-        return jnp.concatenate([held, lax.ppermute(held, "grp", pairs)], axis=0)
-
-    column, grads, unit, scale, gain = near_call(
-        norm_kernel,
-        "norm",
+    place = my_group[None]
+    feats_far, w_far, bias_far = in_hbm(feats, w_proj, b_proj[None])
+
+    def swap(held, step):
+        return lax.ppermute(held, "grp", [(group, group ^ step) for group in range(groups)])
+
+    def join(*parts):
+        rows = sum(part.shape[0] for part in parts)
+        outs = (shape((rows, *parts[0].shape[1:]), bfloat16),)
+        return near_call(join_kernel, "join", outs, [WHOLE] * len(parts), parts, limit=8)[0]
+
+    step = groups // 2
+    if step:
+        feats_swapped, grads_swapped = swap(feats[None], step), swap(cotangent, step)
+    w_low, column, grads, gain, shift = near_call(
+        functools.partial(fetch_kernel, 0),
+        "fetch",
         (
-            shape((block, vis_width), bfloat16),
+            shape((half, units), bfloat16),
+            shape((1, own_rows, vis_width), bfloat16),
             shape(cotangent.shape, bfloat16),
-            shape(feats.shape, float32),
-            shape((own_rows, 128), float32),
+            shape((1, vis_width), float32),
             shape((1, vis_width), float32),
         ),
-        [WHOLE] * 4,
-        in_hbm(feats, ln_gain, ln_shift, cotangent),
+        [LEFT] * 6,
+        (place, w_far, feats_far, *in_hbm(cotangent, ln_gain, ln_shift)),
+        [
+            pltpu.VMEM((vis_width,), float32),
+            pltpu.VMEM((vis_width,), float32),
+            pltpu.SemaphoreType.DMA,
+            pltpu.SemaphoreType.DMA((4,)),
+        ],
+        moved=vis_width * units,
         limit=8,
     )
-    (w_low,) = near_call(
-        functools.partial(fetch_kernel, 0),
-        "fetch",
-        (shape((half, units), bfloat16),),
-        [LEFT, LEFT],
-        (w_far, column),
-        [pltpu.SemaphoreType.DMA],
-        moved=2 * half * units,
-    )
-    step = groups // 2
+    blocks, later = [column], column
     while step:
-        column, grads = exchange(column, step), exchange(grads, step)
-        if step == groups // 2:
-            later = column
+        blocks = [column, feats_swapped]
+        grads = join(grads, grads_swapped)
         step //= 2
+        if step:
+            column = later = join(*blocks)
+            feats_swapped, grads_swapped = swap(column, step), swap(grads, step)
     w_high, bias, sources, own_sources, arrivals = near_call(
         functools.partial(fetch_and_route_kernel, half, block, own_rows, lanes, groups),
         "fetch_and_route",
@@ -262,18 +318,37 @@
             shape((lanes * block, all_rows), bfloat16),
             shape((group_rows, slot_count), bfloat16),
         ),
-        [SCALARS] * 4 + [WHOLE, LEFT, LEFT],
-        (my_group[None], *in_hbm(img_seq, img_count, img_offset), bias_far, w_far, later),
-        [pltpu.SemaphoreType.DMA],
-        moved=2 * (vis_width - half) * units,
+        [SCALARS] + [LEFT] * 6,
+        (place, *in_hbm(img_seq, img_count, img_offset), bias_far, w_far, later),
+        [pltpu.SMEM(img_seq.shape, jnp.int32)] * 3
+        + [pltpu.SemaphoreType.DMA, pltpu.SemaphoreType.DMA((4,))],
+        moved=vis_width * units,
+        limit=8,
+    )
+    column, unit, scale = near_call(
+        norm_kernel,
+        "norm",
+        (
+            shape((groups * block, vis_width), bfloat16),
+            shape(feats.shape, float32),
+            shape((own_rows, 128), float32),
+        ),
+        [WHOLE] * (len(blocks) + 2),
+        (*blocks, gain, shift),
+        limit=8,
     )
     rows = lax.all_gather(column, "dev", axis=0, tiled=True)
     pre_act, terms = near_call(
-        functools.partial(terms_kernel, block, lanes, groups),
+        functools.partial(terms_kernel, block, lanes, groups, width),
         "terms",
         (shape((slot_count, units), float32), shape((lanes, block, vis_width), bfloat16)),
         [WHOLE] * 6,
         (rows, grads, bias, own_sources, w_low, w_high),
+        [
+            pltpu.VMEM((lanes, block, vis_width), bfloat16),
+            pltpu.SemaphoreType.DMA((pl.cdiv(half, width) + pl.cdiv(vis_width - half, width),)),
+        ],
+        (WHOLE, LEFT),
         moved=4 * vis_width * units,
     )
     swapped = lax.all_to_all(terms, "dev", 0, 0)
@@ -295,6 +370,7 @@
         ],
         (WHOLE, WHOLE, LEFT),
         moved=4 * vis_width * units,
+        limit=20,
     )
     (grad_feats,) = near_call(
         finish_kernel,

time: 38.3 us -> 37.2 us (0.971)
  Pallas kernels: 16.4 us -> 14.9 us
  starting transfers between devices: 9.73 us -> 10.3 us
    pallas_call x6 -> x9, Pallas kernels: 16.4 us -> 14.9 us  [near_call(): pl.pallas_call(kernel, out_shape=outs, in_specs=in_specs, out_specs=out_s...]
    ppermute x4, starting transfers between devices: 6.34 us -> 6.88 us  [swap(): lax.ppermute(held, 'grp', [(group, group ^ step) for group in range(group...]
  transfers between devices with their start and end apart: 5 -> 5, of which waited for: 1 -> 1; matrix products, arithmetic and copies ran while one was open for 0% -> 0% of each run, Pallas kernels for 28% -> 29%
where the time goes in v6:
time: 37.2 us; the launch traced here: 36.6 us
  Pallas kernels  14.9 us (40%)
  blocking collectives  10.6 us (28%)
  starting transfers between devices  10.3 us (28%)
  between operations  0.72 us (2%)
    pallas_call x9, Pallas kernels, near_call(): pl.pallas_call(kernel, out_shape=outs, in_specs=in_specs, out_specs=out_s...  14.9 us
    all_gather x1, blocking collectives, gathered_plan(): rows = lax.all_gather(column, 'dev', axis=0, tiled=True)  10.6 us
    ppermute x4, starting transfers between devices, swap(): lax.ppermute(held, 'grp', [(group, group ^ step) for group in range(group...  6.88 us
    all_to_all x1, starting transfers between devices, gathered_plan(): swapped = lax.all_to_all(terms, 'dev', 0, 0)  3.41 us
  transfers between devices with their start and end apart: 5, of which 1 were waited for; matrix products, arithmetic and copies ran while one was open for 0% of the time, Pallas kernels for 29%

profile of v6, /device:TPU:0, one launch (start us, length us, event | category | flops | bytes accessed | tf_op | source)
XLA Modules:
  0.0 36.6 jit_solution(7790638897673755996)
XLA Ops:
  0.6 4.1 %collective-permute-start = (bf16[1,3,3200]{2,1,0:T(4,128)(2,1)}, bf16[1,3,3200]{2,1,0:T(4,128)(2,1)S(1)}, u32[]{:S(2)}, u32[]{:S(2)}) collective-permute-start(bf16[1,3,3200]{2,1,0:T(4,128)(2,1)} %bitcast.4), channel_id=1, source_target_pairs={{0,16},{8,24},{16,0},{24,8},{1,17},{9,25},{17,1},{25,9},{2,18},{10... | collective-permute-start | bytes 57608 | tf_op jit(solution)/shard_map/ppermute | solution.py:272
  4.7 0.1 collective-permute-start.2
  4.8 2.0 %fetch.1 = (bf16[1536,1024]{1,0:T(8,128)(2,1)S(1)}, bf16[1,3,3200]{2,1,0:T(4,128)(2,1)S(1)}, bf16[24,1024]{1,0:T(8,128)(2,1)S(1)}, f32[1,3200]{1,0:T(1,128)S(1)}, f32[1,3200]{1,0:T(1,128)S(1)}) custom-call(s32[1]{0:T(128)} %bitcast.place, bf16[3200,1024]{1,0:T(8,128)(2,1)} %w_far.3, bf16[3,3200]{1,0:T(4,128)(2,1)} %feats_far.1, bf16[24,1024]{1,0:T(8,128)(2,1)} %grads_far.1, ...), custom_call_target="tpu_custom_call" | custom-call | bytes 3276800 | tf_op jit(solution)/shard_map/fetch/pallas_call | solution.py:243
  6.8 0.0 collective-permute-done.refs_1_
  6.8 1.9 %collective-permute-start.1 = (bf16[2,3,3200]{2,1,0:T(4,128)(2,1)S(1)}, bf16[2,3,3200]{2,1,0:T(4,128)(2,1)S(1)}, u32[]{:S(2)}, u32[]{:S(2)}) collective-permute-start(bf16[2,3,3200]{2,1,0:T(4,128)(2,1)S(1)} %join.3.refs_0_.after), channel_id=1, source_target_pairs={{0,8},{8,0},{16,24},{24,16},{1,9},{9,1},{17,25},{25,17},{2,10},{10... | collective-permute-start | bytes 115208 | tf_op jit(solution)/shard_map/ppermute | solution.py:272
  8.8 2.0 %fetch_and_route.1 = (bf16[1664,1024]{1,0:T(8,128)(2,1)S(1)}, f32[1,1024]{1,0:T(1,128)S(1)}, bf16[128,96]{1,0:T(8,128)(2,1)S(1)}, bf16[32,96]{1,0:T(8,128)(2,1)S(1)}, bf16[24,128]{1,0:T(8,128)(2,1)S(1)}) custom-call(s32[1]{0:T(128)} %bitcast.place, s32[32]{0:T(128)} %img_seq_far.1, s32[32]{0:T(128)} %img_count_far.1, s32[32]{0:T(128)} %img_offset_far.1, ...), custom_call_target="tpu_custom_call" | custom-call | bytes 3276800 | tf_op jit(solution)/shard_map/fetch_and_route/pallas_call | solution.py:243
  10.8 0.0 collective-permute-done.2.refs_1_
  10.8 0.8 %collective-permute-start.3 = (bf16[48,1024]{1,0:T(8,128)(2,1)S(1)}, bf16[48,1024]{1,0:T(8,128)(2,1)S(1)}, u32[]{:S(2)}, u32[]{:S(2)}) collective-permute-start(bf16[48,1024]{1,0:T(8,128)(2,1)S(1)} %join.4.refs_0_), channel_id=1, source_target_pairs={{0,8},{8,0},{16,24},{24,16},{1,9},{9,1},{17,25},{25,17},{2,10},{10... | collective-permute-start | bytes 294920 | tf_op jit(solution)/shard_map/ppermute | solution.py:272
  11.6 0.0 collective-permute-done.1.refs_1_
  11.6 0.3 norm.1
  11.9 10.6 %all_gather.3.rows = bf16[128,3200]{1,0:T(8,128)(2,1)S(1)} all-gather(bf16[16,3200]{1,0:T(8,128)(2,1)S(1)} %get-tuple-element.25), channel_id=1, replica_groups=mesh['grp'=4,'dev'=8] {'dev'}, dimensions={0}, use_global_device_ids=true | all-gather | bytes 921600 | tf_op jit(solution)/shard_map/all_gather | solution.py:340
  22.4 0.0 collective-permute-done.3.refs_1_
  22.4 3.7 %terms.1 = (f32[128,1024]{1,0:T(8,128)S(1)}, bf16[8,4,3200]{2,1,0:T(4,128)(2,1)}) custom-call(bf16[128,3200]{1,0:T(8,128)(2,1)S(1)} %all_gather.3.rows, bf16[96,1024]{1,0:T(8,128)(2,1)S(1)} %join.5.grads, f32[1,1024]{1,0:T(1,128)S(1)} %get-tuple-element.27.bias, bf16[32,96]{1,0:T(8,128)(2,1)S(1)} %get-tuple-element.28.own_sources, ...), custom_call_target="tpu_custom_call" | custom-call | bytes 13107200 | tf_op jit(solution)/shard_map/terms/pallas_call | solution.py:243
  26.2 3.4 %all-to-all-start = ((bf16[8,4,3200]{2,1,0:T(4,128)(2,1)}), bf16[8,4,3200]{2,1,0:T(4,128)(2,1)S(1)}, u32[]{:S(2)}, u32[]{:S(2)}) async-start(bf16[8,4,3200]{2,1,0:T(4,128)(2,1)} %get-tuple-element.35), calls=%async_computation | async-start | bytes 409600 | tf_op jit(solution)/shard_map/all_to_all | solution.py:354
  29.6 6.1 %grad_weight.1 = (bf16[24,1024]{1,0:T(8,128)(2,1)}, f32[1,1024]{1,0:T(1,128)}, f32[3200,1024]{1,0:T(8,128)}) custom-call(bf16[128,3200]{1,0:T(8,128)(2,1)S(1)} %all_gather.3.rows, bf16[96,1024]{1,0:T(8,128)(2,1)S(1)} %join.5.grads, f32[128,1024]{1,0:T(8,128)S(1)} %get-tuple-element.31.pre_act, bf16[128,96]{1,0:T(8,128)(2,1)S(1)} %get-tuple-element.32.sources, ...), custom_call_target="tpu_custom_call" | custom-call | bytes 13107200 | tf_op jit(solution)/shard_map/grad_weight/pallas_call | solution.py:243
  35.7 0.1 all-to-all-done.swapped
  35.8 0.8 %finish.1 = bf16[3,3200]{1,0:T(4,128)(2,1)} custom-call(bf16[8,4,3200]{2,1,0:T(4,128)(2,1)S(1)} %all-to-all-done.swapped, f32[1,3200]{1,0:T(1,128)S(1)} %get-tuple-element.23.refs_2_.gain, f32[3,3200]{1,0:T(4,128)S(1)} %get-tuple-element.36.unit, f32[3,128]{1,0:T(4,128)S(1)} %get-tuple-element.37.scale), custom_call_target="tpu_custom_call" | custom-call | tf_op jit(solution)/shard_map/finish/pallas_call | solution.py:243
  (3 shorter events, 0.0 us)
Async XLA Ops:
  0.6 6.2 %collective-permute-start = (bf16[1,3,3200]{2,1,0:T(4,128)(2,1)}, bf16[1,3,3200]{2,1,0:T(4,128)(2,1)S(1)}, u32[]{:S(2)}, u32[]{:S(2)}) collective-permute-start(bf16[1,3,3200]{2,1,0:T(4,128)(2,1)} %bitcast.4), channel_id=1, source_target_pairs={{0,16},{8,24},{16,0},{24,8},{1,17},{9,25},{17,1},{25,9},{2,18},{10... | collective-permute-start | bytes 57608 | tf_op jit(solution)/shard_map/ppermute | solution.py:272
  4.7 6.1 %collective-permute-start.2 = (bf16[24,1024]{1,0:T(8,128)(2,1)}, bf16[24,1024]{1,0:T(8,128)(2,1)S(1)}, u32[]{:S(2)}, u32[]{:S(2)}) collective-permute-start(bf16[24,1024]{1,0:T(8,128)(2,1)} %grads_far.1), channel_id=1, source_target_pairs={{0,16},{8,24},{16,0},{24,8},{1,17},{9,25},{17,1},{25,9},{2,18},{10... | collective-permute-start | bytes 147464 | tf_op jit(solution)/shard_map/ppermute | solution.py:272
  6.8 4.7 %collective-permute-start.1 = (bf16[2,3,3200]{2,1,0:T(4,128)(2,1)S(1)}, bf16[2,3,3200]{2,1,0:T(4,128)(2,1)S(1)}, u32[]{:S(2)}, u32[]{:S(2)}) collective-permute-start(bf16[2,3,3200]{2,1,0:T(4,128)(2,1)S(1)} %join.3.refs_0_.after), channel_id=1, source_target_pairs={{0,8},{8,0},{16,24},{24,16},{1,9},{9,1},{17,25},{25,17},{2,10},{10... | collective-permute-start | bytes 115208 | tf_op jit(solution)/shard_map/ppermute | solution.py:272
  10.8 11.6 %collective-permute-start.3 = (bf16[48,1024]{1,0:T(8,128)(2,1)S(1)}, bf16[48,1024]{1,0:T(8,128)(2,1)S(1)}, u32[]{:S(2)}, u32[]{:S(2)}) collective-permute-start(bf16[48,1024]{1,0:T(8,128)(2,1)S(1)} %join.4.refs_0_), channel_id=1, source_target_pairs={{0,8},{8,0},{16,24},{24,16},{1,9},{9,1},{17,25},{25,17},{2,10},{10... | collective-permute-start | bytes 294920 | tf_op jit(solution)/shard_map/ppermute | solution.py:272
  26.2 9.7 %all-to-all-start = ((bf16[8,4,3200]{2,1,0:T(4,128)(2,1)}), bf16[8,4,3200]{2,1,0:T(4,128)(2,1)S(1)}, u32[]{:S(2)}, u32[]{:S(2)}) async-start(bf16[8,4,3200]{2,1,0:T(4,128)(2,1)} %get-tuple-element.35), calls=%async_computation | async-start | bytes 409600 | tf_op jit(solution)/shard_map/all_to_all | solution.py:354

commit v7 on v6

--- a/solution.py
+++ b/solution.py
@@ -62,17 +62,70 @@
 def norm_kernel(*refs):
     parts, gain, shift, (normed, unit, scale) = refs[:-5], refs[-5], refs[-4], refs[-3:]
     blocks = [part[at] for part in parts for at in range(part.shape[0])]
-    block, own_rows = normed.shape[0] // len(blocks), unit.shape[0]
     rows = []
     for at, held in enumerate(blocks):
         unit_rows, inv_scale, made = normalize(held, gain[...], shift[...])
         rows.append(made)
-        if block > own_rows:
-            rows.append(jnp.zeros((block - own_rows, made.shape[1]), jnp.float32))
         if at == 0:
             unit[...] = unit_rows
             scale[...] = jnp.broadcast_to(inv_scale, scale.shape)
-    normed[...] = jnp.concatenate(rows, axis=0).astype(jnp.bfloat16)
+    rows = jnp.concatenate(rows, axis=0)
+    width = normed.shape[1]
+    rest = fill(rows[:, width:], width)
+    normed[...] = jnp.concatenate([rows[:, :width], rest], axis=0).astype(jnp.bfloat16)
+
+
+def fill(rows, width):
+    empty = width - rows.shape[1]
+    if not empty:
+        return rows
+    return jnp.concatenate([rows, jnp.zeros((rows.shape[0], empty), rows.dtype)], axis=1)
+
+
+def fold_width(own_rows, vis_width):
+    lines = pl.cdiv(own_rows, 8) * 8
+    width = pl.cdiv(own_rows * vis_width, lines * 128) * 128
+    while True:
+        rest = vis_width % width
+        used = own_rows * (vis_width // width) + (pl.cdiv(own_rows, width // rest) if rest else 0)
+        if used <= lines:
+            return lines, width
+        width += 128
+
+
+def pack(rows, lines, width):
+    own_rows, vis_width = rows.shape
+    whole = vis_width // width * width
+    parts = [rows[:, first : first + width] for first in range(0, whole, width)]
+    if vis_width > whole:
+        beside = width // (vis_width - whole)
+        for first in range(0, own_rows, beside):
+            last = min(first + beside, own_rows)
+            line = jnp.concatenate([rows[row : row + 1, whole:] for row in range(first, last)], axis=1)
+            parts.append(fill(line, width))
+    empty = lines - sum(part.shape[0] for part in parts)
+    if empty:
+        parts.append(jnp.zeros((empty, width), rows.dtype))
+    return jnp.concatenate(parts, axis=0)
+
+
+def unpack(packed, own_rows, vis_width):
+    width = packed.shape[1]
+    count = vis_width // width
+    rest = vis_width - count * width
+    parts = [packed[at * own_rows : (at + 1) * own_rows] for at in range(count)]
+    if rest:
+        beside, base = width // rest, count * own_rows
+        parts.append(
+            jnp.concatenate(
+                [
+                    packed[base + row // beside : base + row // beside + 1, row % beside * rest : (row % beside + 1) * rest]
+                    for row in range(own_rows)
+                ],
+                axis=0,
+            )
+        )
+    return jnp.concatenate(parts, axis=1)
 
 
 def distance_of(place, groups):
@@ -84,15 +137,13 @@
     return distance
 
 
-def slot_targets(my_group, block, own_rows, lanes, groups, img_seq, img_count, img_offset):
+def slot_targets(my_group, own_rows, lanes, groups, img_seq, img_count, img_offset):
     group_rows = own_rows * lanes
-    slots = lax.broadcasted_iota(jnp.int32, (1, lanes * groups * block), 1)
-    within = slots & (block - 1)
-    row_ids = (
-        (my_group ^ distance_of((slots // block) & (groups - 1), groups)) * group_rows
-        + slots // (block * groups) * own_rows
-        + within
-    )
+    slots = lax.broadcasted_iota(jnp.int32, (1, group_rows * groups), 1)
+    lane = slots // (own_rows * groups)
+    left = slots - lane * (own_rows * groups)
+    held = left // own_rows
+    row_ids = (my_group ^ distance_of(held, groups)) * group_rows + (lane - held) * own_rows + left
     target = jnp.zeros_like(row_ids)
     start = jnp.int32(0)
     for image in range(img_seq.shape[0]):
@@ -101,7 +152,7 @@
         base = img_seq[image] * group_rows + img_offset[image] - start
         target = jnp.where(member, row_ids + base, target)
         start = end
-    return jnp.where(within < own_rows, target, -1)
+    return target
 
 
 def join_kernel(*refs):
@@ -139,7 +190,7 @@
 
 
 def fetch_and_route_kernel(
-    first, block, own_rows, lanes, groups,
+    first, own_rows, lanes, groups,
     place, img_seq_far, img_count_far, img_offset_far, bias_far, w_far, after,
     near, bias, sources, own_sources, arrivals,
     img_seq, img_count, img_offset, arrived, small,
@@ -155,58 +206,62 @@
     for load in load_all(pairs, small):
         load.wait()
     group_rows = own_rows * lanes
-    slot_count = lanes * groups * block
+    all_rows = group_rows * groups
     my_group = place[0]
-    target = slot_targets(my_group, block, own_rows, lanes, groups, img_seq, img_count, img_offset)
-    places = lax.broadcasted_iota(jnp.int32, (group_rows * groups, slot_count), 0)
+    target = slot_targets(my_group, own_rows, lanes, groups, img_seq, img_count, img_offset)
+    places = lax.broadcasted_iota(jnp.int32, (all_rows, all_rows), 0)
     held = places // group_rows
     seq_rows = places - held * group_rows + (my_group ^ distance_of(held, groups)) * group_rows
     routes = (target == seq_rows).astype(jnp.float32)
     arrivals[...] = routes[:group_rows].astype(jnp.bfloat16)
     turned = routes.T
     sources[...] = turned.astype(jnp.bfloat16)
-    own_sources[...] = own_slots(turned, block, lanes, groups).astype(jnp.bfloat16)
+    own_sources[...] = own_slots(turned, own_rows, lanes, groups).astype(jnp.bfloat16)
     copy.wait()
 
 
-def own_slots(rows, block, lanes, groups):
-    stride = block * groups
-    return jnp.concatenate([rows[lane * stride : lane * stride + block] for lane in range(lanes)], axis=0)
-
-
-def terms_kernel(block, lanes, groups, width, rows, grads, bias, own_sources, *refs):
-    parts, (pre_act, far, terms, left) = refs[:-4], refs[-4:]
-    total, first = bias[...], 0
-    for part in parts:
-        total = total + jnp.dot(
-            rows[:, first : first + part.shape[0]], part[...], preferred_element_type=jnp.float32
-        )
-        first += part.shape[0]
+def own_slots(rows, own_rows, lanes, groups):
+    stride = own_rows * groups
+    return jnp.concatenate([rows[lane * stride : lane * stride + own_rows] for lane in range(lanes)], axis=0)
+
+
+def terms_kernel(
+    own_rows, lanes, groups, packed, grads, bias, own_sources, low, high, rows, pre_act, far, terms, left
+):
+    stride = own_rows * groups
+    held = packed[...].astype(jnp.float32)
+    upper = [held[2 * lane * stride : (2 * lane + 1) * stride] for lane in range(lanes)]
+    lower = [held[(2 * lane + 1) * stride : 2 * (lane + 1) * stride, : high.shape[0]] for lane in range(lanes)]
+    upper = jnp.concatenate(upper, axis=0).astype(jnp.bfloat16)
+    lower = jnp.concatenate(lower, axis=0).astype(jnp.bfloat16)
+    rows[:, : low.shape[0]] = upper
+    rows[:, low.shape[0] :] = lower
+    total = bias[...] + jnp.dot(upper, low[...], preferred_element_type=jnp.float32)
+    total = total + jnp.dot(lower, high[...], preferred_element_type=jnp.float32)
     pre_act[...] = total
-    slope = gelu_and_slope(own_slots(total, block, lanes, groups))[1]
+    slope = gelu_and_slope(own_slots(total, own_rows, lanes, groups))[1]
     upstream = jnp.dot(own_sources[...], grads[...], preferred_element_type=jnp.float32)
     own = (upstream * slope).astype(jnp.bfloat16)
-    first, copies = 0, []
-    for part in parts:
-        for start in range(0, part.shape[0], width):
-            size = min(width, part.shape[0] - start)
-            term = lax.dot_general(
-                own, part[start : start + size], (((1,), (1,)), ((), ())), preferred_element_type=jnp.float32
-            )
-            span = slice(first, first + size)
-            for lane in range(lanes):
-                terms[lane, :, span] = term[lane * block : (lane + 1) * block].astype(jnp.bfloat16)
-            copies.append(
-                pltpu.make_async_copy(terms.at[:, :, span], far.at[:, :, span], left.at[len(copies)])
-            )
-            copies[-1].start()
-            first += size
+    term = jnp.concatenate(
+        [
+            lax.dot_general(own, part[...], (((1,), (1,)), ((), ())), preferred_element_type=jnp.float32)
+            for part in (low, high)
+        ],
+        axis=1,
+    )
+    copies = []
+    for lane in range(lanes):
+        mine = term[lane * own_rows : (lane + 1) * own_rows]
+        terms[lane] = pack(mine, terms.shape[1], terms.shape[2]).astype(jnp.bfloat16)
+        copies.append(pltpu.make_async_copy(terms.at[lane], far.at[lane], left.at[lane]))
+        copies[-1].start()
     for copy in copies:
         copy.wait()
 
 
 def grad_weight_kernel(
-    height, rows, grads, pre_act, sources, arrivals, projected, grad_bias, far, grad_pre, near, left
+    height, rows, grads, pre_act, sources, arrivals, projected_far, bias_far, far,
+    projected, grad_bias, grad_pre, near, left, small,
 ):
     acted, slope = gelu_and_slope(pre_act[...])
     upstream = jnp.dot(sources[...], grads[...], preferred_element_type=jnp.float32)
@@ -220,10 +275,14 @@
         )
         copies.append(pltpu.make_async_copy(near.at[span], far.at[span], left.at[step]))
         copies[-1].start()
-    projected[...] = jnp.dot(
-        arrivals[...], acted.astype(jnp.bfloat16), preferred_element_type=jnp.float32
-    ).astype(jnp.bfloat16)
-    grad_bias[...] = jnp.sum(pulled.astype(jnp.float32), axis=0, keepdims=True)
+        if step == 0:
+            projected[...] = jnp.dot(
+                arrivals[...], acted.astype(jnp.bfloat16), preferred_element_type=jnp.float32
+            ).astype(jnp.bfloat16)
+            grad_bias[...] = jnp.sum(pulled.astype(jnp.float32), axis=0, keepdims=True)
+            for at, (close, out) in enumerate(((projected, projected_far), (grad_bias, bias_far))):
+                copies.append(pltpu.make_async_copy(close, out, small.at[at]))
+                copies[-1].start()
     for copy in copies:
         copy.wait()
 
@@ -232,7 +291,7 @@
     total = swapped[0].astype(jnp.float32)
     for lane in range(1, swapped.shape[0]):
         total = total + swapped[lane].astype(jnp.float32)
-    grad_feats[...] = backward_norm(total[: unit.shape[0]], gain[...], unit[...], scale[:, :1])
+    grad_feats[...] = backward_norm(unpack(total, *unit.shape), gain[...], unit[...], scale[:, :1])
 
 
 def in_hbm(*arrays):
@@ -260,10 +319,8 @@
     units = w_proj.shape[1]
     group_rows = own_rows * lanes
     all_rows = group_rows * groups
-    block = pl.next_power_of_2(own_rows)
-    slot_count = lanes * groups * block
-    half = vis_width // 256 * 128
-    width = 896
+    half = pl.cdiv(vis_width, 256) * 128
+    lines, width = fold_width(own_rows, vis_width)
     shape, bfloat16, float32 = jax.ShapeDtypeStruct, jnp.bfloat16, jnp.float32
     place = my_group[None]
     feats_far, w_far, bias_far = in_hbm(feats, w_proj, b_proj[None])
@@ -309,14 +366,14 @@
             column = later = join(*blocks)
             feats_swapped, grads_swapped = swap(column, step), swap(grads, step)
     w_high, bias, sources, own_sources, arrivals = near_call(
-        functools.partial(fetch_and_route_kernel, half, block, own_rows, lanes, groups),
+        functools.partial(fetch_and_route_kernel, half, own_rows, lanes, groups),
         "fetch_and_route",
         (
             shape((vis_width - half, units), bfloat16),
             shape((1, units), float32),
-            shape((slot_count, all_rows), bfloat16),
-            shape((lanes * block, all_rows), bfloat16),
-            shape((group_rows, slot_count), bfloat16),
+            shape((all_rows, all_rows), bfloat16),
+            shape((group_rows, all_rows), bfloat16),
+            shape((group_rows, all_rows), bfloat16),
         ),
         [SCALARS] + [LEFT] * 6,
         (place, *in_hbm(img_seq, img_count, img_offset), bias_far, w_far, later),
@@ -329,7 +386,7 @@
         norm_kernel,
         "norm",
         (
-            shape((groups * block, vis_width), bfloat16),
+            shape((2 * groups * own_rows, half), bfloat16),
             shape(feats.shape, float32),
             shape((own_rows, 128), float32),
         ),
@@ -337,18 +394,19 @@
         (*blocks, gain, shift),
         limit=8,
     )
-    rows = lax.all_gather(column, "dev", axis=0, tiled=True)
-    pre_act, terms = near_call(
-        functools.partial(terms_kernel, block, lanes, groups, width),
+    packed = lax.all_gather(column, "dev", axis=0, tiled=True)
+    rows, pre_act, terms = near_call(
+        functools.partial(terms_kernel, own_rows, lanes, groups),
         "terms",
-        (shape((slot_count, units), float32), shape((lanes, block, vis_width), bfloat16)),
+        (
+            shape((all_rows, vis_width), bfloat16),
+            shape((all_rows, units), float32),
+            pltpu.HBM((lanes, lines, width), bfloat16),
+        ),
         [WHOLE] * 6,
-        (rows, grads, bias, own_sources, w_low, w_high),
-        [
-            pltpu.VMEM((lanes, block, vis_width), bfloat16),
-            pltpu.SemaphoreType.DMA((pl.cdiv(half, width) + pl.cdiv(vis_width - half, width),)),
-        ],
-        (WHOLE, LEFT),
+        (packed, grads, bias, own_sources, w_low, w_high),
+        [pltpu.VMEM((lanes, lines, width), bfloat16), pltpu.SemaphoreType.DMA((lanes,))],
+        (WHOLE, WHOLE, LEFT),
         moved=4 * vis_width * units,
     )
     swapped = lax.all_to_all(terms, "dev", 0, 0)
@@ -357,18 +415,21 @@
         functools.partial(grad_weight_kernel, height),
         "grad_weight",
         (
-            shape((group_rows, units), bfloat16),
-            shape((1, units), float32),
-            shape((vis_width, units), float32),
+            pltpu.HBM((group_rows, units), bfloat16),
+            pltpu.HBM((1, units), float32),
+            pltpu.HBM((vis_width, units), float32),
         ),
         [WHOLE] * 5,
         (rows, grads, pre_act, sources, arrivals),
         [
-            pltpu.VMEM((slot_count, units), bfloat16),
+            pltpu.VMEM((group_rows, units), bfloat16),
+            pltpu.VMEM((1, units), float32),
+            pltpu.VMEM((all_rows, units), bfloat16),
             pltpu.VMEM((vis_width, units), float32),
             pltpu.SemaphoreType.DMA((vis_width // height,)),
+            pltpu.SemaphoreType.DMA((2,)),
         ],
-        (WHOLE, WHOLE, LEFT),
+        (LEFT,) * 3,
         moved=4 * vis_width * units,
         limit=20,
     )

time: 37.2 us -> 36.4 us (0.978)
  blocking collectives: 10.6 us -> 10.1 us
  Pallas kernels: 14.9 us -> 14.5 us
    pallas_call x9, Pallas kernels: 14.9 us -> 14.5 us  [near_call(): pl.pallas_call(kernel, out_shape=outs, in_specs=in_specs, out_specs=out_s...]
    all_gather x1, blocking collectives: 10.6 us -> 10.1 us  [gathered_plan(): packed = lax.all_gather(column, 'dev', axis=0, tiled=True)]
  transfers between devices with their start and end apart: 5 -> 5, of which waited for: 1 -> 1; matrix products, arithmetic and copies ran while one was open for 0% -> 0% of each run, Pallas kernels for 29% -> 27%
where the time goes in v7:
time: 36.4 us; the launch traced here: 36 us
  Pallas kernels  14.5 us (40%)
  starting transfers between devices  10.3 us (28%)
  blocking collectives  10.1 us (28%)
  between operations  0.72 us (2%)
    pallas_call x9, Pallas kernels, near_call(): pl.pallas_call(kernel, out_shape=outs, in_specs=in_specs, out_specs=out_s...  14.5 us
    all_gather x1, blocking collectives, gathered_plan(): packed = lax.all_gather(column, 'dev', axis=0, tiled=True)  10.1 us
    ppermute x4, starting transfers between devices, swap(): lax.ppermute(held, 'grp', [(group, group ^ step) for group in range(group...  6.88 us
    all_to_all x1, starting transfers between devices, gathered_plan(): swapped = lax.all_to_all(terms, 'dev', 0, 0)  3.39 us
  transfers between devices with their start and end apart: 5, of which 1 were waited for; matrix products, arithmetic and copies ran while one was open for 0% of the time, Pallas kernels for 27%

profile of v7, /device:TPU:0, one launch (start us, length us, event | category | flops | bytes accessed | tf_op | source)
XLA Modules:
  0.0 36.0 jit_solution(17937170942432286152)
XLA Ops:
  0.6 4.1 %collective-permute-start = (bf16[1,3,3200]{2,1,0:T(4,128)(2,1)}, bf16[1,3,3200]{2,1,0:T(4,128)(2,1)S(1)}, u32[]{:S(2)}, u32[]{:S(2)}) collective-permute-start(bf16[1,3,3200]{2,1,0:T(4,128)(2,1)} %bitcast.4), channel_id=1, source_target_pairs={{0,16},{8,24},{16,0},{24,8},{1,17},{9,25},{17,1},{25,9},{2,18},{10... | collective-permute-start | bytes 57608 | tf_op jit(solution)/shard_map/ppermute | solution.py:329
  4.7 0.1 collective-permute-start.2
  4.8 2.1 %fetch.1 = (bf16[1664,1024]{1,0:T(8,128)(2,1)S(1)}, bf16[1,3,3200]{2,1,0:T(4,128)(2,1)S(1)}, bf16[24,1024]{1,0:T(8,128)(2,1)S(1)}, f32[1,3200]{1,0:T(1,128)S(1)}, f32[1,3200]{1,0:T(1,128)S(1)}) custom-call(s32[1]{0:T(128)} %bitcast.place, bf16[3200,1024]{1,0:T(8,128)(2,1)} %w_far.3, bf16[3,3200]{1,0:T(4,128)(2,1)} %feats_far.1, bf16[24,1024]{1,0:T(8,128)(2,1)} %grads_far.1, ...), custom_call_target="tpu_custom_call" | custom-call | bytes 3276800 | tf_op jit(solution)/shard_map/fetch/pallas_call | solution.py:302
  6.9 0.0 collective-permute-done.refs_1_
  6.9 1.9 %collective-permute-start.1 = (bf16[2,3,3200]{2,1,0:T(4,128)(2,1)S(1)}, bf16[2,3,3200]{2,1,0:T(4,128)(2,1)S(1)}, u32[]{:S(2)}, u32[]{:S(2)}) collective-permute-start(bf16[2,3,3200]{2,1,0:T(4,128)(2,1)S(1)} %join.3.refs_0_.after), channel_id=1, source_target_pairs={{0,8},{8,0},{16,24},{24,16},{1,9},{9,1},{17,25},{25,17},{2,10},{10... | collective-permute-start | bytes 115208 | tf_op jit(solution)/shard_map/ppermute | solution.py:329
  8.8 1.9 %fetch_and_route.1 = (bf16[1536,1024]{1,0:T(8,128)(2,1)S(1)}, f32[1,1024]{1,0:T(1,128)S(1)}, bf16[96,96]{1,0:T(8,128)(2,1)S(1)}, bf16[24,96]{1,0:T(8,128)(2,1)S(1)}, bf16[24,96]{1,0:T(8,128)(2,1)S(1)}) custom-call(s32[1]{0:T(128)} %bitcast.place, s32[32]{0:T(128)} %img_seq_far.1, s32[32]{0:T(128)} %img_count_far.1, s32[32]{0:T(128)} %img_offset_far.1, ...), custom_call_target="tpu_custom_call" | custom-call | bytes 3276800 | tf_op jit(solution)/shard_map/fetch_and_route/pallas_call | solution.py:302
  10.8 0.0 collective-permute-done.2.refs_1_
  10.8 0.8 %collective-permute-start.3 = (bf16[48,1024]{1,0:T(8,128)(2,1)S(1)}, bf16[48,1024]{1,0:T(8,128)(2,1)S(1)}, u32[]{:S(2)}, u32[]{:S(2)}) collective-permute-start(bf16[48,1024]{1,0:T(8,128)(2,1)S(1)} %join.4.refs_0_), channel_id=1, source_target_pairs={{0,8},{8,0},{16,24},{24,16},{1,9},{9,1},{17,25},{25,17},{2,10},{10... | collective-permute-start | bytes 294920 | tf_op jit(solution)/shard_map/ppermute | solution.py:329
  11.6 0.0 collective-permute-done.1.refs_1_
  11.6 0.3 norm.1
  11.9 10.1 %all_gather.3.packed = bf16[192,1664]{1,0:T(8,128)(2,1)S(1)} all-gather(bf16[24,1664]{1,0:T(8,128)(2,1)S(1)} %get-tuple-element.26), channel_id=1, replica_groups=mesh['grp'=4,'dev'=8] {'dev'}, dimensions={0}, use_global_device_ids=true | all-gather | bytes 718848 | tf_op jit(solution)/shard_map/all_gather | solution.py:397
  22.0 0.0 collective-permute-done.3.refs_1_
  22.0 3.9 %terms.1 = (bf16[96,3200]{1,0:T(8,128)(2,1)S(1)}, f32[96,1024]{1,0:T(8,128)S(1)}, bf16[8,8,1280]{2,1,0:T(8,128)(2,1)}) custom-call(bf16[192,1664]{1,0:T(8,128)(2,1)S(1)} %all_gather.3.packed, bf16[96,1024]{1,0:T(8,128)(2,1)S(1)} %join.5.grads, f32[1,1024]{1,0:T(1,128)S(1)} %get-tuple-element.28.bias, bf16[24,96]{1,0:T(8,128)(2,1)S(1)} %get-tuple-element.29.own_sources, ...), custom_call_target="tpu_custom_call" | custom-call | bytes 13107200 | tf_op jit(solution)/shard_map/terms/pallas_call | solution.py:302
  26.0 3.4 %all-to-all-start = ((bf16[8,8,1280]{2,1,0:T(8,128)(2,1)}), bf16[8,8,1280]{2,1,0:T(8,128)(2,1)S(1)}, u32[]{:S(2)}, u32[]{:S(2)}) async-start(bf16[8,8,1280]{2,1,0:T(8,128)(2,1)} %get-tuple-element.37), calls=%async_computation | async-start | bytes 327680 | tf_op jit(solution)/shard_map/all_to_all | solution.py:412
  29.4 5.5 %grad_weight.1 = (bf16[24,1024]{1,0:T(8,128)(2,1)}, f32[1,1024]{1,0:T(1,128)}, f32[3200,1024]{1,0:T(8,128)}) custom-call(bf16[96,3200]{1,0:T(8,128)(2,1)S(1)} %get-tuple-element.32.rows, bf16[96,1024]{1,0:T(8,128)(2,1)S(1)} %join.5.grads, f32[96,1024]{1,0:T(8,128)S(1)} %get-tuple-element.33.pre_act, bf16[96,96]{1,0:T(8,128)(2,1)S(1)} %get-tuple-element.34.sources, ...), custom_call_target="tpu_custom_call" | custom-call | bytes 13107200 | tf_op jit(solution)/shard_map/grad_weight/pallas_call | solution.py:302
  34.9 0.3 all-to-all-done.swapped
  35.2 0.8 %finish.1 = bf16[3,3200]{1,0:T(4,128)(2,1)} custom-call(bf16[8,8,1280]{2,1,0:T(8,128)(2,1)S(1)} %all-to-all-done.swapped, f32[1,3200]{1,0:T(1,128)S(1)} %get-tuple-element.24.refs_2_.gain, f32[3,3200]{1,0:T(4,128)S(1)} %get-tuple-element.38.unit, f32[3,128]{1,0:T(4,128)S(1)} %get-tuple-element.39.scale), custom_call_target="tpu_custom_call" | custom-call | tf_op jit(solution)/shard_map/finish/pallas_call | solution.py:302
  (3 shorter events, 0.0 us)
Async XLA Ops:
  0.6 6.3 %collective-permute-start = (bf16[1,3,3200]{2,1,0:T(4,128)(2,1)}, bf16[1,3,3200]{2,1,0:T(4,128)(2,1)S(1)}, u32[]{:S(2)}, u32[]{:S(2)}) collective-permute-start(bf16[1,3,3200]{2,1,0:T(4,128)(2,1)} %bitcast.4), channel_id=1, source_target_pairs={{0,16},{8,24},{16,0},{24,8},{1,17},{9,25},{17,1},{25,9},{2,18},{10... | collective-permute-start | bytes 57608 | tf_op jit(solution)/shard_map/ppermute | solution.py:329
  4.7 6.0 %collective-permute-start.2 = (bf16[24,1024]{1,0:T(8,128)(2,1)}, bf16[24,1024]{1,0:T(8,128)(2,1)S(1)}, u32[]{:S(2)}, u32[]{:S(2)}) collective-permute-start(bf16[24,1024]{1,0:T(8,128)(2,1)} %grads_far.1), channel_id=1, source_target_pairs={{0,16},{8,24},{16,0},{24,8},{1,17},{9,25},{17,1},{25,9},{2,18},{10... | collective-permute-start | bytes 147464 | tf_op jit(solution)/shard_map/ppermute | solution.py:329
  6.9 4.7 %collective-permute-start.1 = (bf16[2,3,3200]{2,1,0:T(4,128)(2,1)S(1)}, bf16[2,3,3200]{2,1,0:T(4,128)(2,1)S(1)}, u32[]{:S(2)}, u32[]{:S(2)}) collective-permute-start(bf16[2,3,3200]{2,1,0:T(4,128)(2,1)S(1)} %join.3.refs_0_.after), channel_id=1, source_target_pairs={{0,8},{8,0},{16,24},{24,16},{1,9},{9,1},{17,25},{25,17},{2,10},{10... | collective-permute-start | bytes 115208 | tf_op jit(solution)/shard_map/ppermute | solution.py:329
  10.8 11.2 %collective-permute-start.3 = (bf16[48,1024]{1,0:T(8,128)(2,1)S(1)}, bf16[48,1024]{1,0:T(8,128)(2,1)S(1)}, u32[]{:S(2)}, u32[]{:S(2)}) collective-permute-start(bf16[48,1024]{1,0:T(8,128)(2,1)S(1)} %join.4.refs_0_), channel_id=1, source_target_pairs={{0,8},{8,0},{16,24},{24,16},{1,9},{9,1},{17,25},{25,17},{2,10},{10... | collective-permute-start | bytes 294920 | tf_op jit(solution)/shard_map/ppermute | solution.py:329
  26.0 9.2 %all-to-all-start = ((bf16[8,8,1280]{2,1,0:T(8,128)(2,1)}), bf16[8,8,1280]{2,1,0:T(8,128)(2,1)S(1)}, u32[]{:S(2)}, u32[]{:S(2)}) async-start(bf16[8,8,1280]{2,1,0:T(8,128)(2,1)} %get-tuple-element.37), calls=%async_computation | async-start | bytes 327680 | tf_op jit(solution)/shard_map/all_to_all | solution.py:412

commit v8 on v7

--- a/solution.py
+++ b/solution.py
@@ -61,15 +61,11 @@
 
 def norm_kernel(*refs):
     parts, gain, shift, (normed, unit, scale) = refs[:-5], refs[-5], refs[-4], refs[-3:]
-    blocks = [part[at] for part in parts for at in range(part.shape[0])]
-    rows = []
-    for at, held in enumerate(blocks):
-        unit_rows, inv_scale, made = normalize(held, gain[...], shift[...])
-        rows.append(made)
-        if at == 0:
-            unit[...] = unit_rows
-            scale[...] = jnp.broadcast_to(inv_scale, scale.shape)
-    rows = jnp.concatenate(rows, axis=0)
+    blocks = [part[at].astype(jnp.float32) for part in parts for at in range(part.shape[0])]
+    unit_rows, inv_scale, rows = normalize(jnp.concatenate(blocks, axis=0), gain[...], shift[...])
+    own_rows = unit.shape[0]
+    unit[...] = unit_rows[:own_rows]
+    scale[...] = jnp.broadcast_to(inv_scale[:own_rows], scale.shape)
     width = normed.shape[1]
     rest = fill(rows[:, width:], width)
     normed[...] = jnp.concatenate([rows[:, :width], rest], axis=0).astype(jnp.bfloat16)
@@ -226,7 +222,7 @@
 
 
 def terms_kernel(
-    own_rows, lanes, groups, packed, grads, bias, own_sources, low, high, rows, pre_act, far, terms, left
+    own_rows, lanes, groups, piece, packed, grads, bias, own_sources, low, high, rows, pre_act, far, terms, left
 ):
     stride = own_rows * groups
     held = packed[...].astype(jnp.float32)
@@ -242,13 +238,16 @@
     slope = gelu_and_slope(own_slots(total, own_rows, lanes, groups))[1]
     upstream = jnp.dot(own_sources[...], grads[...], preferred_element_type=jnp.float32)
     own = (upstream * slope).astype(jnp.bfloat16)
-    term = jnp.concatenate(
-        [
-            lax.dot_general(own, part[...], (((1,), (1,)), ((), ())), preferred_element_type=jnp.float32)
-            for part in (low, high)
-        ],
-        axis=1,
-    )
+    pieces = []
+    for part in (low, high):
+        for first in range(0, part.shape[0], piece):
+            weights = part[first : min(first + piece, part.shape[0])]
+            left_side, right_side = (weights, own) if len(pieces) % 2 else (own, weights)
+            product = lax.dot_general(
+                left_side, right_side, (((1,), (1,)), ((), ())), preferred_element_type=jnp.float32
+            )
+            pieces.append(product.T if len(pieces) % 2 else product)
+    term = jnp.concatenate(pieces, axis=1)
     copies = []
     for lane in range(lanes):
         mine = term[lane * own_rows : (lane + 1) * own_rows]
@@ -396,7 +395,7 @@
     )
     packed = lax.all_gather(column, "dev", axis=0, tiled=True)
     rows, pre_act, terms = near_call(
-        functools.partial(terms_kernel, own_rows, lanes, groups),
+        functools.partial(terms_kernel, own_rows, lanes, groups, 256),
         "terms",
         (
             shape((all_rows, vis_width), bfloat16),

time: 36.4 us -> 36 us (0.989)
  Pallas kernels: 14.5 us -> 14.1 us
    pallas_call x9, Pallas kernels: 14.5 us -> 14.1 us  [near_call(): pl.pallas_call(kernel, out_shape=outs, in_specs=in_specs, out_specs=out_s...]
where the time goes in v8:
time: 36 us; the launch traced here: 35.6 us
  Pallas kernels  14.1 us (39%)
  starting transfers between devices  10.3 us (29%)
  blocking collectives  10.1 us (28%)
  between operations  0.72 us (2%)
    pallas_call x9, Pallas kernels, near_call(): pl.pallas_call(kernel, out_shape=outs, in_specs=in_specs, out_specs=out_s...  14.1 us
    all_gather x1, blocking collectives, gathered_plan(): packed = lax.all_gather(column, 'dev', axis=0, tiled=True)  10.1 us
    ppermute x4, starting transfers between devices, swap(): lax.ppermute(held, 'grp', [(group, group ^ step) for group in range(group...  6.88 us
    all_to_all x1, starting transfers between devices, gathered_plan(): swapped = lax.all_to_all(terms, 'dev', 0, 0)  3.39 us
  transfers between devices with their start and end apart: 5, of which 1 were waited for; matrix products, arithmetic and copies ran while one was open for 0% of the time, Pallas kernels for 27%

profile of v8, /device:TPU:0, one launch (start us, length us, event | category | flops | bytes accessed | tf_op | source)
XLA Modules:
  0.0 35.6 jit_solution(1338954855362747467)
XLA Ops:
  0.6 4.1 %collective-permute-start = (bf16[1,3,3200]{2,1,0:T(4,128)(2,1)}, bf16[1,3,3200]{2,1,0:T(4,128)(2,1)S(1)}, u32[]{:S(2)}, u32[]{:S(2)}) collective-permute-start(bf16[1,3,3200]{2,1,0:T(4,128)(2,1)} %bitcast.4), channel_id=1, source_target_pairs={{0,16},{8,24},{16,0},{24,8},{1,17},{9,25},{17,1},{25,9},{2,18},{10... | collective-permute-start | bytes 57608 | tf_op jit(solution)/shard_map/ppermute | solution.py:328
  4.7 0.1 collective-permute-start.2
  4.8 2.1 %fetch.1 = (bf16[1664,1024]{1,0:T(8,128)(2,1)S(1)}, bf16[1,3,3200]{2,1,0:T(4,128)(2,1)S(1)}, bf16[24,1024]{1,0:T(8,128)(2,1)S(1)}, f32[1,3200]{1,0:T(1,128)S(1)}, f32[1,3200]{1,0:T(1,128)S(1)}) custom-call(s32[1]{0:T(128)} %bitcast.place, bf16[3200,1024]{1,0:T(8,128)(2,1)} %w_far.3, bf16[3,3200]{1,0:T(4,128)(2,1)} %feats_far.1, bf16[24,1024]{1,0:T(8,128)(2,1)} %grads_far.1, ...), custom_call_target="tpu_custom_call" | custom-call | bytes 3276800 | tf_op jit(solution)/shard_map/fetch/pallas_call | solution.py:301
  6.9 0.0 collective-permute-done.refs_1_
  6.9 1.9 %collective-permute-start.1 = (bf16[2,3,3200]{2,1,0:T(4,128)(2,1)S(1)}, bf16[2,3,3200]{2,1,0:T(4,128)(2,1)S(1)}, u32[]{:S(2)}, u32[]{:S(2)}) collective-permute-start(bf16[2,3,3200]{2,1,0:T(4,128)(2,1)S(1)} %join.3.refs_0_.after), channel_id=1, source_target_pairs={{0,8},{8,0},{16,24},{24,16},{1,9},{9,1},{17,25},{25,17},{2,10},{10... | collective-permute-start | bytes 115208 | tf_op jit(solution)/shard_map/ppermute | solution.py:328
  8.8 1.9 %fetch_and_route.1 = (bf16[1536,1024]{1,0:T(8,128)(2,1)S(1)}, f32[1,1024]{1,0:T(1,128)S(1)}, bf16[96,96]{1,0:T(8,128)(2,1)S(1)}, bf16[24,96]{1,0:T(8,128)(2,1)S(1)}, bf16[24,96]{1,0:T(8,128)(2,1)S(1)}) custom-call(s32[1]{0:T(128)} %bitcast.place, s32[32]{0:T(128)} %img_seq_far.1, s32[32]{0:T(128)} %img_count_far.1, s32[32]{0:T(128)} %img_offset_far.1, ...), custom_call_target="tpu_custom_call" | custom-call | bytes 3276800 | tf_op jit(solution)/shard_map/fetch_and_route/pallas_call | solution.py:301
  10.8 0.0 collective-permute-done.2.refs_1_
  10.8 0.8 %collective-permute-start.3 = (bf16[48,1024]{1,0:T(8,128)(2,1)S(1)}, bf16[48,1024]{1,0:T(8,128)(2,1)S(1)}, u32[]{:S(2)}, u32[]{:S(2)}) collective-permute-start(bf16[48,1024]{1,0:T(8,128)(2,1)S(1)} %join.4.refs_0_), channel_id=1, source_target_pairs={{0,8},{8,0},{16,24},{24,16},{1,9},{9,1},{17,25},{25,17},{2,10},{10... | collective-permute-start | bytes 294920 | tf_op jit(solution)/shard_map/ppermute | solution.py:328
  11.6 0.0 collective-permute-done.1.refs_1_
  11.6 0.3 norm.1
  11.9 10.1 %all_gather.3.packed = bf16[192,1664]{1,0:T(8,128)(2,1)S(1)} all-gather(bf16[24,1664]{1,0:T(8,128)(2,1)S(1)} %get-tuple-element.26), channel_id=1, replica_groups=mesh['grp'=4,'dev'=8] {'dev'}, dimensions={0}, use_global_device_ids=true | all-gather | bytes 718848 | tf_op jit(solution)/shard_map/all_gather | solution.py:396
  22.0 0.0 collective-permute-done.3.refs_1_
  22.0 3.6 %terms.1 = (bf16[96,3200]{1,0:T(8,128)(2,1)S(1)}, f32[96,1024]{1,0:T(8,128)S(1)}, bf16[8,8,1280]{2,1,0:T(8,128)(2,1)}) custom-call(bf16[192,1664]{1,0:T(8,128)(2,1)S(1)} %all_gather.3.packed, bf16[96,1024]{1,0:T(8,128)(2,1)S(1)} %join.5.grads, f32[1,1024]{1,0:T(1,128)S(1)} %get-tuple-element.28.bias, bf16[24,96]{1,0:T(8,128)(2,1)S(1)} %get-tuple-element.29.own_sources, ...), custom_call_target="tpu_custom_call" | custom-call | bytes 13107200 | tf_op jit(solution)/shard_map/terms/pallas_call | solution.py:301
  25.6 3.4 %all-to-all-start = ((bf16[8,8,1280]{2,1,0:T(8,128)(2,1)}), bf16[8,8,1280]{2,1,0:T(8,128)(2,1)S(1)}, u32[]{:S(2)}, u32[]{:S(2)}) async-start(bf16[8,8,1280]{2,1,0:T(8,128)(2,1)} %get-tuple-element.37), calls=%async_computation | async-start | bytes 327680 | tf_op jit(solution)/shard_map/all_to_all | solution.py:411
  29.0 5.5 %grad_weight.1 = (bf16[24,1024]{1,0:T(8,128)(2,1)}, f32[1,1024]{1,0:T(1,128)}, f32[3200,1024]{1,0:T(8,128)}) custom-call(bf16[96,3200]{1,0:T(8,128)(2,1)S(1)} %get-tuple-element.32.rows, bf16[96,1024]{1,0:T(8,128)(2,1)S(1)} %join.5.grads, f32[96,1024]{1,0:T(8,128)S(1)} %get-tuple-element.33.pre_act, bf16[96,96]{1,0:T(8,128)(2,1)S(1)} %get-tuple-element.34.sources, ...), custom_call_target="tpu_custom_call" | custom-call | bytes 13107200 | tf_op jit(solution)/shard_map/grad_weight/pallas_call | solution.py:301
  34.5 0.3 all-to-all-done.swapped
  34.8 0.8 %finish.1 = bf16[3,3200]{1,0:T(4,128)(2,1)} custom-call(bf16[8,8,1280]{2,1,0:T(8,128)(2,1)S(1)} %all-to-all-done.swapped, f32[1,3200]{1,0:T(1,128)S(1)} %get-tuple-element.24.refs_2_.gain, f32[3,3200]{1,0:T(4,128)S(1)} %get-tuple-element.38.unit, f32[3,128]{1,0:T(4,128)S(1)} %get-tuple-element.39.scale), custom_call_target="tpu_custom_call" | custom-call | tf_op jit(solution)/shard_map/finish/pallas_call | solution.py:301
  (3 shorter events, 0.0 us)
Async XLA Ops:
  0.6 6.3 %collective-permute-start = (bf16[1,3,3200]{2,1,0:T(4,128)(2,1)}, bf16[1,3,3200]{2,1,0:T(4,128)(2,1)S(1)}, u32[]{:S(2)}, u32[]{:S(2)}) collective-permute-start(bf16[1,3,3200]{2,1,0:T(4,128)(2,1)} %bitcast.4), channel_id=1, source_target_pairs={{0,16},{8,24},{16,0},{24,8},{1,17},{9,25},{17,1},{25,9},{2,18},{10... | collective-permute-start | bytes 57608 | tf_op jit(solution)/shard_map/ppermute | solution.py:328
  4.7 6.0 %collective-permute-start.2 = (bf16[24,1024]{1,0:T(8,128)(2,1)}, bf16[24,1024]{1,0:T(8,128)(2,1)S(1)}, u32[]{:S(2)}, u32[]{:S(2)}) collective-permute-start(bf16[24,1024]{1,0:T(8,128)(2,1)} %grads_far.1), channel_id=1, source_target_pairs={{0,16},{8,24},{16,0},{24,8},{1,17},{9,25},{17,1},{25,9},{2,18},{10... | collective-permute-start | bytes 147464 | tf_op jit(solution)/shard_map/ppermute | solution.py:328
  6.9 4.7 %collective-permute-start.1 = (bf16[2,3,3200]{2,1,0:T(4,128)(2,1)S(1)}, bf16[2,3,3200]{2,1,0:T(4,128)(2,1)S(1)}, u32[]{:S(2)}, u32[]{:S(2)}) collective-permute-start(bf16[2,3,3200]{2,1,0:T(4,128)(2,1)S(1)} %join.3.refs_0_.after), channel_id=1, source_target_pairs={{0,8},{8,0},{16,24},{24,16},{1,9},{9,1},{17,25},{25,17},{2,10},{10... | collective-permute-start | bytes 115208 | tf_op jit(solution)/shard_map/ppermute | solution.py:328
  10.8 11.2 %collective-permute-start.3 = (bf16[48,1024]{1,0:T(8,128)(2,1)S(1)}, bf16[48,1024]{1,0:T(8,128)(2,1)S(1)}, u32[]{:S(2)}, u32[]{:S(2)}) collective-permute-start(bf16[48,1024]{1,0:T(8,128)(2,1)S(1)} %join.4.refs_0_), channel_id=1, source_target_pairs={{0,8},{8,0},{16,24},{24,16},{1,9},{9,1},{17,25},{25,17},{2,10},{10... | collective-permute-start | bytes 294920 | tf_op jit(solution)/shard_map/ppermute | solution.py:328
  25.6 9.2 %all-to-all-start = ((bf16[8,8,1280]{2,1,0:T(8,128)(2,1)}), bf16[8,8,1280]{2,1,0:T(8,128)(2,1)S(1)}, u32[]{:S(2)}, u32[]{:S(2)}) async-start(bf16[8,8,1280]{2,1,0:T(8,128)(2,1)} %get-tuple-element.37), calls=%async_computation | async-start | bytes 327680 | tf_op jit(solution)/shard_map/all_to_all | solution.py:411

commit v9 on v8

--- a/solution.py
+++ b/solution.py
@@ -242,11 +242,11 @@
     for part in (low, high):
         for first in range(0, part.shape[0], piece):
             weights = part[first : min(first + piece, part.shape[0])]
-            left_side, right_side = (weights, own) if len(pieces) % 2 else (own, weights)
+            left_side, right_side = (own, weights) if len(pieces) % 2 else (weights, own)
             product = lax.dot_general(
                 left_side, right_side, (((1,), (1,)), ((), ())), preferred_element_type=jnp.float32
             )
-            pieces.append(product.T if len(pieces) % 2 else product)
+            pieces.append(product if len(pieces) % 2 else product.T)
     term = jnp.concatenate(pieces, axis=1)
     copies = []
     for lane in range(lanes):

time: 36 us -> 36 us (level)
  no operation moved by 1% of the time
where the time goes in v9:
time: 36 us; the launch traced here: 35.6 us
  Pallas kernels  14.1 us (39%)
  starting transfers between devices  10.3 us (29%)
  blocking collectives  10.1 us (28%)
  between operations  0.72 us (2%)
    pallas_call x9, Pallas kernels, near_call(): pl.pallas_call(kernel, out_shape=outs, in_specs=in_specs, out_specs=out_s...  14.1 us
    all_gather x1, blocking collectives, gathered_plan(): packed = lax.all_gather(column, 'dev', axis=0, tiled=True)  10.1 us
    ppermute x4, starting transfers between devices, swap(): lax.ppermute(held, 'grp', [(group, group ^ step) for group in range(group...  6.88 us
    all_to_all x1, starting transfers between devices, gathered_plan(): swapped = lax.all_to_all(terms, 'dev', 0, 0)  3.39 us
  transfers between devices with their start and end apart: 5, of which 1 were waited for; matrix products, arithmetic and copies ran while one was open for 0% of the time, Pallas kernels for 27%

profile of v9, /device:TPU:0, one launch (start us, length us, event | category | flops | bytes accessed | tf_op | source)
XLA Modules:
  0.0 35.6 jit_solution(17903441416563981338)
XLA Ops:
  0.6 4.1 %collective-permute-start = (bf16[1,3,3200]{2,1,0:T(4,128)(2,1)}, bf16[1,3,3200]{2,1,0:T(4,128)(2,1)S(1)}, u32[]{:S(2)}, u32[]{:S(2)}) collective-permute-start(bf16[1,3,3200]{2,1,0:T(4,128)(2,1)} %bitcast.4), channel_id=1, source_target_pairs={{0,16},{8,24},{16,0},{24,8},{1,17},{9,25},{17,1},{25,9},{2,18},{10... | collective-permute-start | bytes 57608 | tf_op jit(solution)/shard_map/ppermute | solution.py:328
  4.7 0.1 collective-permute-start.2
  4.8 2.1 %fetch.1 = (bf16[1664,1024]{1,0:T(8,128)(2,1)S(1)}, bf16[1,3,3200]{2,1,0:T(4,128)(2,1)S(1)}, bf16[24,1024]{1,0:T(8,128)(2,1)S(1)}, f32[1,3200]{1,0:T(1,128)S(1)}, f32[1,3200]{1,0:T(1,128)S(1)}) custom-call(s32[1]{0:T(128)} %bitcast.place, bf16[3200,1024]{1,0:T(8,128)(2,1)} %w_far.3, bf16[3,3200]{1,0:T(4,128)(2,1)} %feats_far.1, bf16[24,1024]{1,0:T(8,128)(2,1)} %grads_far.1, ...), custom_call_target="tpu_custom_call" | custom-call | bytes 3276800 | tf_op jit(solution)/shard_map/fetch/pallas_call | solution.py:301
  6.9 0.0 collective-permute-done.refs_1_
  6.9 1.9 %collective-permute-start.1 = (bf16[2,3,3200]{2,1,0:T(4,128)(2,1)S(1)}, bf16[2,3,3200]{2,1,0:T(4,128)(2,1)S(1)}, u32[]{:S(2)}, u32[]{:S(2)}) collective-permute-start(bf16[2,3,3200]{2,1,0:T(4,128)(2,1)S(1)} %join.3.refs_0_.after), channel_id=1, source_target_pairs={{0,8},{8,0},{16,24},{24,16},{1,9},{9,1},{17,25},{25,17},{2,10},{10... | collective-permute-start | bytes 115208 | tf_op jit(solution)/shard_map/ppermute | solution.py:328
  8.8 1.9 %fetch_and_route.1 = (bf16[1536,1024]{1,0:T(8,128)(2,1)S(1)}, f32[1,1024]{1,0:T(1,128)S(1)}, bf16[96,96]{1,0:T(8,128)(2,1)S(1)}, bf16[24,96]{1,0:T(8,128)(2,1)S(1)}, bf16[24,96]{1,0:T(8,128)(2,1)S(1)}) custom-call(s32[1]{0:T(128)} %bitcast.place, s32[32]{0:T(128)} %img_seq_far.1, s32[32]{0:T(128)} %img_count_far.1, s32[32]{0:T(128)} %img_offset_far.1, ...), custom_call_target="tpu_custom_call" | custom-call | bytes 3276800 | tf_op jit(solution)/shard_map/fetch_and_route/pallas_call | solution.py:301
  10.8 0.0 collective-permute-done.2.refs_1_
  10.8 0.8 %collective-permute-start.3 = (bf16[48,1024]{1,0:T(8,128)(2,1)S(1)}, bf16[48,1024]{1,0:T(8,128)(2,1)S(1)}, u32[]{:S(2)}, u32[]{:S(2)}) collective-permute-start(bf16[48,1024]{1,0:T(8,128)(2,1)S(1)} %join.4.refs_0_), channel_id=1, source_target_pairs={{0,8},{8,0},{16,24},{24,16},{1,9},{9,1},{17,25},{25,17},{2,10},{10... | collective-permute-start | bytes 294920 | tf_op jit(solution)/shard_map/ppermute | solution.py:328
  11.6 0.0 collective-permute-done.1.refs_1_
  11.6 0.3 norm.1
  11.9 10.1 %all_gather.3.packed = bf16[192,1664]{1,0:T(8,128)(2,1)S(1)} all-gather(bf16[24,1664]{1,0:T(8,128)(2,1)S(1)} %get-tuple-element.26), channel_id=1, replica_groups=mesh['grp'=4,'dev'=8] {'dev'}, dimensions={0}, use_global_device_ids=true | all-gather | bytes 718848 | tf_op jit(solution)/shard_map/all_gather | solution.py:396
  22.0 0.0 collective-permute-done.3.refs_1_
  22.0 3.6 %terms.1 = (bf16[96,3200]{1,0:T(8,128)(2,1)S(1)}, f32[96,1024]{1,0:T(8,128)S(1)}, bf16[8,8,1280]{2,1,0:T(8,128)(2,1)}) custom-call(bf16[192,1664]{1,0:T(8,128)(2,1)S(1)} %all_gather.3.packed, bf16[96,1024]{1,0:T(8,128)(2,1)S(1)} %join.5.grads, f32[1,1024]{1,0:T(1,128)S(1)} %get-tuple-element.28.bias, bf16[24,96]{1,0:T(8,128)(2,1)S(1)} %get-tuple-element.29.own_sources, ...), custom_call_target="tpu_custom_call" | custom-call | bytes 13107200 | tf_op jit(solution)/shard_map/terms/pallas_call | solution.py:301
  25.6 3.4 %all-to-all-start = ((bf16[8,8,1280]{2,1,0:T(8,128)(2,1)}), bf16[8,8,1280]{2,1,0:T(8,128)(2,1)S(1)}, u32[]{:S(2)}, u32[]{:S(2)}) async-start(bf16[8,8,1280]{2,1,0:T(8,128)(2,1)} %get-tuple-element.37), calls=%async_computation | async-start | bytes 327680 | tf_op jit(solution)/shard_map/all_to_all | solution.py:411
  29.0 5.5 %grad_weight.1 = (bf16[24,1024]{1,0:T(8,128)(2,1)}, f32[1,1024]{1,0:T(1,128)}, f32[3200,1024]{1,0:T(8,128)}) custom-call(bf16[96,3200]{1,0:T(8,128)(2,1)S(1)} %get-tuple-element.32.rows, bf16[96,1024]{1,0:T(8,128)(2,1)S(1)} %join.5.grads, f32[96,1024]{1,0:T(8,128)S(1)} %get-tuple-element.33.pre_act, bf16[96,96]{1,0:T(8,128)(2,1)S(1)} %get-tuple-element.34.sources, ...), custom_call_target="tpu_custom_call" | custom-call | bytes 13107200 | tf_op jit(solution)/shard_map/grad_weight/pallas_call | solution.py:301
  34.5 0.3 all-to-all-done.swapped
  34.8 0.8 %finish.1 = bf16[3,3200]{1,0:T(4,128)(2,1)} custom-call(bf16[8,8,1280]{2,1,0:T(8,128)(2,1)S(1)} %all-to-all-done.swapped, f32[1,3200]{1,0:T(1,128)S(1)} %get-tuple-element.24.refs_2_.gain, f32[3,3200]{1,0:T(4,128)S(1)} %get-tuple-element.38.unit, f32[3,128]{1,0:T(4,128)S(1)} %get-tuple-element.39.scale), custom_call_target="tpu_custom_call" | custom-call | tf_op jit(solution)/shard_map/finish/pallas_call | solution.py:301
  (3 shorter events, 0.0 us)
Async XLA Ops:
  0.6 6.3 %collective-permute-start = (bf16[1,3,3200]{2,1,0:T(4,128)(2,1)}, bf16[1,3,3200]{2,1,0:T(4,128)(2,1)S(1)}, u32[]{:S(2)}, u32[]{:S(2)}) collective-permute-start(bf16[1,3,3200]{2,1,0:T(4,128)(2,1)} %bitcast.4), channel_id=1, source_target_pairs={{0,16},{8,24},{16,0},{24,8},{1,17},{9,25},{17,1},{25,9},{2,18},{10... | collective-permute-start | bytes 57608 | tf_op jit(solution)/shard_map/ppermute | solution.py:328
  4.7 6.0 %collective-permute-start.2 = (bf16[24,1024]{1,0:T(8,128)(2,1)}, bf16[24,1024]{1,0:T(8,128)(2,1)S(1)}, u32[]{:S(2)}, u32[]{:S(2)}) collective-permute-start(bf16[24,1024]{1,0:T(8,128)(2,1)} %grads_far.1), channel_id=1, source_target_pairs={{0,16},{8,24},{16,0},{24,8},{1,17},{9,25},{17,1},{25,9},{2,18},{10... | collective-permute-start | bytes 147464 | tf_op jit(solution)/shard_map/ppermute | solution.py:328
  6.9 4.7 %collective-permute-start.1 = (bf16[2,3,3200]{2,1,0:T(4,128)(2,1)S(1)}, bf16[2,3,3200]{2,1,0:T(4,128)(2,1)S(1)}, u32[]{:S(2)}, u32[]{:S(2)}) collective-permute-start(bf16[2,3,3200]{2,1,0:T(4,128)(2,1)S(1)} %join.3.refs_0_.after), channel_id=1, source_target_pairs={{0,8},{8,0},{16,24},{24,16},{1,9},{9,1},{17,25},{25,17},{2,10},{10... | collective-permute-start | bytes 115208 | tf_op jit(solution)/shard_map/ppermute | solution.py:328
  10.8 11.2 %collective-permute-start.3 = (bf16[48,1024]{1,0:T(8,128)(2,1)S(1)}, bf16[48,1024]{1,0:T(8,128)(2,1)S(1)}, u32[]{:S(2)}, u32[]{:S(2)}) collective-permute-start(bf16[48,1024]{1,0:T(8,128)(2,1)S(1)} %join.4.refs_0_), channel_id=1, source_target_pairs={{0,8},{8,0},{16,24},{24,16},{1,9},{9,1},{17,25},{25,17},{2,10},{10... | collective-permute-start | bytes 294920 | tf_op jit(solution)/shard_map/ppermute | solution.py:328
  25.6 9.2 %all-to-all-start = ((bf16[8,8,1280]{2,1,0:T(8,128)(2,1)}), bf16[8,8,1280]{2,1,0:T(8,128)(2,1)S(1)}, u32[]{:S(2)}, u32[]{:S(2)}) async-start(bf16[8,8,1280]{2,1,0:T(8,128)(2,1)} %get-tuple-element.37), calls=%async_computation | async-start | bytes 327680 | tf_op jit(solution)/shard_map/all_to_all | solution.py:411
